TPU v7x, 32 devices: a whole 2x2x4 slice. The times are simulated.
32 devices in a mesh: section: 2 (over core), ctx: 4 (over y, x), fsdp: 4 (over z).
Axes of the slice: x: 2, y: 2, z: 4, core: 2. Of those that a mesh axis runs over, the one named last changes fastest.
Arguments:
- stream_in: bfloat16 [2, 4, 2, 512, 1024], P('section', 'fsdp', None, 'ctx'), may hold values from -6 to 6
- lengths: int32 [4, 2, 3], P('fsdp'), may hold values from 1 to 256, 512 in all within a row
- dealing: int32 [4, 2, 512], P('fsdp'), may hold values from 0 to 511, each once within a row
- attention_gain: float32 [2, 1024], P('section', 'fsdp'), may hold values from 0.25 to 1.75
- query_weight: float32 [2, 1024, 2048], P('section', 'fsdp'), may hold values from -0.1875 to 0.1875
- key_weight: float32 [2, 1024, 1024], P('section', 'fsdp'), may hold values from -0.1875 to 0.1875
- value_weight: float32 [2, 1024, 1024], P('section', 'fsdp'), may hold values from -0.1875 to 0.1875
- query_gain: float32 [2, 128], P('section', 'fsdp'), may hold values from 0.25 to 1.75
- key_gain: float32 [2, 128], P('section', 'fsdp'), may hold values from 0.25 to 1.75
- out_weight: float32 [2, 2048, 1024], P('section', 'fsdp'), may hold values from -1 to 1
- mlp_gain: float32 [2, 1024], P('section', 'fsdp'), may hold values from 0.25 to 1.75
- gate_weight: float32 [2, 1024, 3072], P('section', 'fsdp'), may hold values from -0.1875 to 0.1875
- up_weight: float32 [2, 1024, 3072], P('section', 'fsdp'), may hold values from -0.1875 to 0.1875
- down_weight: float32 [2, 3072, 1024], P('section', 'fsdp'), may hold values from -0.109375 to 0.109375
Outputs:
- boundary: bfloat16 [2, 4, 2, 512, 1024], P('section', 'fsdp', None, 'ctx')
- grad_attention_gain: float32 [2, 1024], P('section', 'fsdp')
- grad_query: float32 [2, 1024, 2048], P('section', 'fsdp')
- grad_key: float32 [2, 1024, 1024], P('section', 'fsdp')
- grad_value: float32 [2, 1024, 1024], P('section', 'fsdp')
- grad_query_gain: float32 [2, 128], P('section', 'fsdp')
- grad_key_gain: float32 [2, 128], P('section', 'fsdp')
- grad_out: float32 [2, 2048, 1024], P('section', 'fsdp')
- grad_mlp_gain: float32 [2, 1024], P('section', 'fsdp')
- grad_gate: float32 [2, 1024, 3072], P('section', 'fsdp')
- grad_up: float32 [2, 1024, 3072], P('section', 'fsdp')
- grad_down: float32 [2, 3072, 1024], P('section', 'fsdp')
Inputs may be any that keep to these rules, and one draw needn't show every extreme that they name: Each row holds the lengths of 3 sequences packed in order that fill the 512 tokens of one micro-batch; the longest is exactly 256. `dealing`: each row is a permutation of the 512 natural indices of a micro-batch.
All inputs are finite; a program needn't handle non-finite values.
Results may differ from a plain program's by a relative error of at most 0.028.
Values may be sent and summed in bfloat16 or wider, within the bound.
No kernel may reach another device: no remote copies, remote signals or barrier semaphores. Data moves between devices by JAX's collectives and lax.ppermute only.
A program may use at most 192 MiB of HBM per device.

v0:
```python
import jax
import jax.numpy as jnp
from jax import lax
from jax.sharding import PartitionSpec as P

HEAD_DIM = 128


epsilon = 1e-06
rope_base = 1000000.0


def from_behind(value, axis, steps):
    count = lax.axis_size(axis)
    first, last = (max(0, -steps), min(count, count - steps))
    return lax.ppermute(value, axis, [(source, source + steps) for source in range(first, last)])


def rms_scale(values, gain):
    scale = lax.rsqrt(jnp.mean(values * values, axis=-1, keepdims=True) + epsilon)
    return values * scale * gain


def rotate(values, cosine, sine):
    half = values.shape[-1] // 2
    turned = jnp.concatenate([-values[..., half:], values[..., :half]], axis=-1)
    return values * cosine + turned * sine


def angles(position, width):
    half = width // 2
    rates = jnp.power(rope_base, jnp.arange(half, dtype=jnp.float32) * (-2.0 / width))
    phase = position.astype(jnp.float32)[..., None] * rates
    phase = jnp.concatenate([phase, phase], axis=-1)
    return (jnp.cos(phase)[..., None, :], jnp.sin(phase)[..., None, :])


def layout(lengths_row, natural):
    bounds = jnp.cumsum(lengths_row, axis=-1)
    passed = (bounds[..., None, :] <= natural[..., :, None]).astype(jnp.int32)
    sequence = jnp.sum(passed, axis=-1)
    position = natural - jnp.sum(passed * lengths_row[..., None, :], axis=-1)
    return (sequence, position)


def swiglu(gate, lifted):
    return gate * jax.nn.sigmoid(gate) * lifted


def head_prepare(raw, gain, cosine, sine):
    shaped = raw.reshape(raw.shape[0], -1, HEAD_DIM)
    return rotate(rms_scale(shaped, gain), cosine, sine)


def plain_dot(left, right):
    return jnp.dot(left, right, preferred_element_type=jnp.float32)


def contract_rows(left, right):
    return lax.dot_general(
        left, right, (((0,), (0,)), ((), ())), preferred_element_type=jnp.float32
    )


def contract_cols(left, right):
    return lax.dot_general(
        left, right, (((1,), (1,)), ((), ())), preferred_element_type=jnp.float32
    )


def visible_of(context):
    sequence_own, natural_own, sequence_all, natural_all, cosine, sine = context
    return (sequence_all[None, :] == sequence_own[:, None]) & (
        natural_all[None, :] <= natural_own[:, None]
    )


def masked_scores(grouped, all_keys, visible):
    scores = jnp.einsum(
        "qvgd,kvd->vgqk", grouped, all_keys, preferred_element_type=jnp.float32
    ) * HEAD_DIM ** (-0.5)
    return jnp.where(visible, scores, -1e30)


def layer_forward(hidden_in, params, context, share_keys):
    (
        attention_gain,
        query_weight,
        key_weight,
        value_weight,
        query_gain,
        key_gain,
        out_weight,
        mlp_gain,
        gate_weight,
        up_weight,
        down_weight,
    ) = params
    cosine, sine = (context[4], context[5])
    rows = hidden_in.shape[0]
    kv_heads = key_weight.shape[1] // HEAD_DIM
    heads = query_weight.shape[1] // HEAD_DIM
    normed = rms_scale(hidden_in, attention_gain.astype(jnp.float32)).astype(jnp.bfloat16)
    query_raw = plain_dot(normed, query_weight)
    key_raw = plain_dot(normed, key_weight)
    value_rows = (
        plain_dot(normed, value_weight).astype(jnp.bfloat16).reshape(rows, kv_heads, HEAD_DIM)
    )
    queries = head_prepare(query_raw, query_gain.astype(jnp.float32), cosine, sine).astype(
        jnp.bfloat16
    )
    key_rows = head_prepare(key_raw, key_gain.astype(jnp.float32), cosine, sine).astype(
        jnp.bfloat16
    )
    all_keys, all_values = share_keys(key_rows, value_rows)
    grouped = queries.reshape(rows, kv_heads, heads // kv_heads, HEAD_DIM)
    scores = masked_scores(grouped, all_keys, visible_of(context))
    top = jnp.max(scores, axis=-1, keepdims=True)
    raised = jnp.exp(scores - top)
    total = jnp.sum(raised, axis=-1, keepdims=True)
    probs_low = (raised / total).astype(jnp.bfloat16)
    log_total = top + jnp.log(total)
    mixed = jnp.einsum("vgqk,kvd->qvgd", probs_low, all_values, preferred_element_type=jnp.float32)
    mixed = mixed.reshape(rows, heads * HEAD_DIM).astype(jnp.bfloat16)
    middle = hidden_in + plain_dot(mixed, out_weight)
    normed_mlp = rms_scale(middle, mlp_gain.astype(jnp.float32)).astype(jnp.bfloat16)
    gate = plain_dot(normed_mlp, gate_weight)
    lifted = plain_dot(normed_mlp, up_weight)
    product = swiglu(gate, lifted).astype(jnp.bfloat16)
    result = middle + plain_dot(product, down_weight)
    kept = (
        hidden_in,
        normed,
        query_raw,
        key_raw,
        queries,
        key_rows,
        value_rows,
        all_keys,
        all_values,
        mixed,
        log_total,
        middle,
        normed_mlp,
        gate,
        lifted,
        product,
    )
    return (result, kept)


def layer_backward(upstream, kept, all_keys, all_values, params, context, scatter_keys):
    (
        attention_gain,
        query_weight,
        key_weight,
        value_weight,
        query_gain,
        key_gain,
        out_weight,
        mlp_gain,
        gate_weight,
        up_weight,
        down_weight,
    ) = params
    hidden_in, normed, query_raw, key_raw, queries = (kept[0], kept[1], kept[2], kept[3], kept[4])
    mixed, log_total, middle, normed_mlp = (kept[9], kept[10], kept[11], kept[12])
    gate, lifted, product = (kept[13], kept[14], kept[15])
    cosine, sine = (context[4], context[5])
    rows = upstream.shape[0]
    kv_heads = key_weight.shape[1] // HEAD_DIM
    heads = query_weight.shape[1] // HEAD_DIM
    scale = HEAD_DIM ** (-0.5)
    branch = upstream.astype(jnp.bfloat16)
    grad_down = contract_rows(product, branch)
    grad_product = contract_cols(branch, down_weight)
    unused, pull = jax.vjp(swiglu, gate, lifted)
    grad_gate_in, grad_lifted = pull(grad_product)
    grad_gate_in = grad_gate_in.astype(jnp.bfloat16)
    grad_lifted = grad_lifted.astype(jnp.bfloat16)
    grad_gate = contract_rows(normed_mlp, grad_gate_in)
    grad_up = contract_rows(normed_mlp, grad_lifted)
    grad_normed_mlp = contract_cols(grad_gate_in, gate_weight) + contract_cols(
        grad_lifted, up_weight
    )
    unused, pull = jax.vjp(rms_scale, middle, mlp_gain.astype(jnp.float32))
    grad_middle_norm, grad_mlp_gain = pull(grad_normed_mlp)
    grad_middle = upstream + grad_middle_norm
    branch_attention = grad_middle.astype(jnp.bfloat16)
    grad_out = contract_rows(mixed, branch_attention)
    grad_mixed = contract_cols(branch_attention, out_weight).astype(jnp.bfloat16)
    grad_mixed = grad_mixed.reshape(rows, kv_heads, heads // kv_heads, HEAD_DIM)
    grouped = queries.reshape(rows, kv_heads, heads // kv_heads, HEAD_DIM)
    scores = masked_scores(grouped, all_keys, visible_of(context))
    probs = jnp.exp(scores - log_total)
    probs_low = probs.astype(jnp.bfloat16)
    grad_probs = jnp.einsum(
        "qvgd,kvd->vgqk", grad_mixed, all_values, preferred_element_type=jnp.float32
    )
    weighted_sum = jnp.sum(probs * grad_probs, axis=-1, keepdims=True)
    grad_scores = (probs * (grad_probs - weighted_sum)).astype(jnp.bfloat16)
    grad_queries = jnp.einsum(
        "vgqk,kvd->qvgd", grad_scores, all_keys, preferred_element_type=jnp.float32
    )
    grad_queries = grad_queries.reshape(rows, heads, HEAD_DIM) * scale

    def key_terms(start, count):
        key_part = (
            jnp.einsum("vgqk,qvgd->kvd", grad_scores, grouped, preferred_element_type=jnp.float32)
            * scale
        )
        value_part = jnp.einsum(
            "vgqk,qvgd->kvd", probs_low, grad_mixed, preferred_element_type=jnp.float32
        )
        return jnp.concatenate([key_part.reshape(count, -1), value_part.reshape(count, -1)], axis=1)

    summed = scatter_keys(key_terms, rows)
    key_width = kv_heads * HEAD_DIM
    grad_key_rows = summed[:, :key_width].reshape(rows, kv_heads, HEAD_DIM)
    grad_values = summed[:, key_width:].astype(jnp.bfloat16)

    def prepare_rows(raw, gain):
        return head_prepare(raw, gain, cosine, sine)

    unused, pull = jax.vjp(prepare_rows, query_raw, query_gain.astype(jnp.float32))
    grad_query_raw, grad_query_gain = pull(grad_queries)
    unused, pull = jax.vjp(prepare_rows, key_raw, key_gain.astype(jnp.float32))
    grad_key_raw, grad_key_gain = pull(grad_key_rows)
    grad_query_raw = grad_query_raw.astype(jnp.bfloat16)
    grad_key_raw = grad_key_raw.astype(jnp.bfloat16)
    grad_query = contract_rows(normed, grad_query_raw)
    grad_key = contract_rows(normed, grad_key_raw)
    grad_value = contract_rows(normed, grad_values)
    grad_normed = contract_cols(grad_query_raw, query_weight) + contract_cols(
        grad_key_raw, key_weight
    )
    grad_normed = grad_normed + contract_cols(grad_values, value_weight)
    unused, pull = jax.vjp(rms_scale, hidden_in, attention_gain.astype(jnp.float32))
    grad_hidden_norm, grad_attention_gain = pull(grad_normed)
    grad_input = grad_middle + grad_hidden_norm
    grads = (
        grad_attention_gain,
        grad_query,
        grad_key,
        grad_value,
        grad_query_gain,
        grad_key_gain,
        grad_out,
        grad_mlp_gain,
        grad_gate,
        grad_up,
        grad_down,
    )
    return (grad_input, grads)


def shards(
    stream_in,
    lengths,
    dealing,
    attention_gain,
    query_weight,
    key_weight,
    value_weight,
    query_gain,
    key_gain,
    out_weight,
    mlp_gain,
    gate_weight,
    up_weight,
    down_weight,
):
    masters = (
        attention_gain,
        query_weight,
        key_weight,
        value_weight,
        query_gain,
        key_gain,
        out_weight,
        mlp_gain,
        gate_weight,
        up_weight,
        down_weight,
    )
    section = lax.axis_index("section")
    last = lax.axis_size("section") - 1
    piece = lax.axis_index("ctx")
    batches = stream_in.shape[2]
    rows = stream_in.shape[3]
    width = stream_in.shape[4]
    slot_source = dealing[0]
    own_start = piece * rows
    natural_slot = lax.dynamic_slice_in_dim(slot_source, own_start, rows, 1)
    sequence_all, position_all = layout(lengths[0], slot_source)
    sequence_own = lax.dynamic_slice_in_dim(sequence_all, own_start, rows, 1)
    position_own = lax.dynamic_slice_in_dim(position_all, own_start, rows, 1)
    part = lax.all_gather(stream_in, "ctx", axis=3, tiled=True)
    count = part.shape[3]
    inside = (natural_slot >= 0) & (natural_slot < count)
    taken = jnp.take_along_axis(
        part[0, 0], jnp.clip(natural_slot, 0, count - 1)[:, :, None], axis=1
    )
    dealt = jnp.where(inside[:, :, None], taken, jnp.zeros((batches, rows, width), jnp.bfloat16))

    def share_forward(key_rows, value_rows):
        return (
            lax.all_gather(key_rows, "ctx", axis=0, tiled=True),
            lax.all_gather(value_rows, "ctx", axis=0, tiled=True),
        )

    def scatter_keys(terms, count):
        return lax.psum_scatter(
            terms(jnp.int32(0), lax.axis_size("ctx") * count).astype(jnp.bfloat16),
            "ctx",
            scatter_dimension=0,
            tiled=True,
        ).astype(jnp.float32)

    cosine_own, sine_own = angles(position_own, HEAD_DIM)

    def context_of(index):

        def select(array):
            return lax.dynamic_index_in_dim(array, index, 0, keepdims=False)

        return (
            select(sequence_own),
            select(natural_slot),
            select(sequence_all),
            select(slot_source),
            select(cosine_own),
            select(sine_own),
        )

    low_masters = tuple((master.astype(jnp.bfloat16) for master in masters))
    full = (
        lax.all_gather(low_masters[0], "fsdp", axis=1, tiled=True),
        lax.all_gather(low_masters[1], "fsdp", axis=1, tiled=True),
        lax.all_gather(low_masters[2], "fsdp", axis=1, tiled=True),
        lax.all_gather(low_masters[3], "fsdp", axis=1, tiled=True),
        lax.all_gather(low_masters[4], "fsdp", axis=1, tiled=True),
        lax.all_gather(low_masters[5], "fsdp", axis=1, tiled=True),
        lax.all_gather(low_masters[6], "fsdp", axis=1, tiled=True),
        lax.all_gather(low_masters[7], "fsdp", axis=1, tiled=True),
        lax.all_gather(low_masters[8], "fsdp", axis=1, tiled=True),
        lax.all_gather(low_masters[9], "fsdp", axis=1, tiled=True),
        lax.all_gather(low_masters[10], "fsdp", axis=1, tiled=True),
    )
    params = tuple((weight[0] for weight in full))
    inbound = jnp.zeros((rows, width), jnp.bfloat16)
    finished = jnp.zeros((batches, rows, width), jnp.bfloat16)
    saved = []
    for step in range(batches + last):
        index = jnp.clip(step - section, 0, batches - 1)
        valid = (step - section >= 0) & (step - section < batches)
        source = jnp.where(
            section == 0, lax.dynamic_index_in_dim(dealt, index, 0, keepdims=False), inbound
        )
        result, kept = layer_forward(
            source.astype(jnp.float32), params, context_of(index), share_forward
        )
        result_low = result.astype(jnp.bfloat16)
        saved.append((kept, index, valid))
        finished = jnp.where(
            valid & (section == last),
            lax.dynamic_update_index_in_dim(finished, result_low, index, 0),
            finished,
        )
        if step < batches:
            inbound = from_behind(result_low, "section", 1)
    back_full = (
        lax.all_gather(low_masters[0], "fsdp", axis=1, tiled=True),
        lax.all_gather(low_masters[1], "fsdp", axis=1, tiled=True),
        lax.all_gather(low_masters[2], "fsdp", axis=1, tiled=True),
        lax.all_gather(low_masters[3], "fsdp", axis=1, tiled=True),
        lax.all_gather(low_masters[4], "fsdp", axis=1, tiled=True),
        lax.all_gather(low_masters[5], "fsdp", axis=1, tiled=True),
        lax.all_gather(low_masters[6], "fsdp", axis=1, tiled=True),
        lax.all_gather(low_masters[7], "fsdp", axis=1, tiled=True),
        lax.all_gather(low_masters[8], "fsdp", axis=1, tiled=True),
        lax.all_gather(low_masters[9], "fsdp", axis=1, tiled=True),
        lax.all_gather(low_masters[10], "fsdp", axis=1, tiled=True),
    )
    back_params = tuple((weight[0] for weight in back_full))
    totals = tuple((jnp.zeros(weight.shape, jnp.float32) for weight in back_params))
    shares = tuple((jnp.zeros(master.shape[1:], jnp.float32) for master in masters))
    returning = jnp.zeros((rows, width), jnp.bfloat16)
    for turn in range(batches + last):
        kept, index, valid = saved[batches + last - 1 - turn]
        all_keys, all_values = (
            lax.all_gather(kept[5], "ctx", axis=0, tiled=True),
            lax.all_gather(kept[6], "ctx", axis=0, tiled=True),
        )
        upstream = jnp.where(
            section == last, lax.dynamic_index_in_dim(dealt, index, 0, keepdims=False), returning
        )
        grad_input, grads = layer_backward(
            upstream.astype(jnp.float32),
            kept,
            all_keys,
            all_values,
            back_params,
            context_of(index),
            scatter_keys,
        )
        grad_low = grad_input.astype(jnp.bfloat16)
        finished = jnp.where(
            valid & (section == 0),
            lax.dynamic_update_index_in_dim(finished, grad_low, index, 0),
            finished,
        )
        weighted = tuple((jnp.where(valid, grad, 0.0) for grad in grads))
        totals = tuple((total + grad for total, grad in zip(totals, weighted)))
        if turn < batches:
            returning = from_behind(grad_low, "section", -1)
    shares = (
        lax.psum_scatter(
            totals[0].astype(jnp.bfloat16), "fsdp", scatter_dimension=0, tiled=True
        ).astype(jnp.float32),
        lax.psum_scatter(
            totals[1].astype(jnp.bfloat16), "fsdp", scatter_dimension=0, tiled=True
        ).astype(jnp.float32),
        lax.psum_scatter(
            totals[2].astype(jnp.bfloat16), "fsdp", scatter_dimension=0, tiled=True
        ).astype(jnp.float32),
        lax.psum_scatter(
            totals[3].astype(jnp.bfloat16), "fsdp", scatter_dimension=0, tiled=True
        ).astype(jnp.float32),
        lax.psum_scatter(
            totals[4].astype(jnp.bfloat16), "fsdp", scatter_dimension=0, tiled=True
        ).astype(jnp.float32),
        lax.psum_scatter(
            totals[5].astype(jnp.bfloat16), "fsdp", scatter_dimension=0, tiled=True
        ).astype(jnp.float32),
        lax.psum_scatter(
            totals[6].astype(jnp.bfloat16), "fsdp", scatter_dimension=0, tiled=True
        ).astype(jnp.float32),
        lax.psum_scatter(
            totals[7].astype(jnp.bfloat16), "fsdp", scatter_dimension=0, tiled=True
        ).astype(jnp.float32),
        lax.psum_scatter(
            totals[8].astype(jnp.bfloat16), "fsdp", scatter_dimension=0, tiled=True
        ).astype(jnp.float32),
        lax.psum_scatter(
            totals[9].astype(jnp.bfloat16), "fsdp", scatter_dimension=0, tiled=True
        ).astype(jnp.float32),
        lax.psum_scatter(
            totals[10].astype(jnp.bfloat16), "fsdp", scatter_dimension=0, tiled=True
        ).astype(jnp.float32),
    )
    summed = (
        lax.psum(shares[0].astype(jnp.bfloat16), "ctx").astype(jnp.float32),
        lax.psum(shares[1].astype(jnp.bfloat16), "ctx").astype(jnp.float32),
        lax.psum(shares[2].astype(jnp.bfloat16), "ctx").astype(jnp.float32),
        lax.psum(shares[3].astype(jnp.bfloat16), "ctx").astype(jnp.float32),
        lax.psum(shares[4].astype(jnp.bfloat16), "ctx").astype(jnp.float32),
        lax.psum(shares[5].astype(jnp.bfloat16), "ctx").astype(jnp.float32),
        lax.psum(shares[6].astype(jnp.bfloat16), "ctx").astype(jnp.float32),
        lax.psum(shares[7].astype(jnp.bfloat16), "ctx").astype(jnp.float32),
        lax.psum(shares[8].astype(jnp.bfloat16), "ctx").astype(jnp.float32),
        lax.psum(shares[9].astype(jnp.bfloat16), "ctx").astype(jnp.float32),
        lax.psum(shares[10].astype(jnp.bfloat16), "ctx").astype(jnp.float32),
    )
    boundary = finished[None, None]
    return (
        boundary,
        summed[0][None],
        summed[1][None],
        summed[2][None],
        summed[3][None],
        summed[4][None],
        summed[5][None],
        summed[6][None],
        summed[7][None],
        summed[8][None],
        summed[9][None],
        summed[10][None],
    )


def solution(mesh):
    placed = (
        P("section", "fsdp", None, "ctx", None),
        P("fsdp", None, None),
        P("fsdp", None, None),
        P("section", "fsdp"),
        P("section", "fsdp", None),
        P("section", "fsdp", None),
        P("section", "fsdp", None),
        P("section", "fsdp"),
        P("section", "fsdp"),
        P("section", "fsdp", None),
        P("section", "fsdp"),
        P("section", "fsdp", None),
        P("section", "fsdp", None),
        P("section", "fsdp", None),
    )
    return jax.shard_map(
        shards,
        mesh=mesh,
        in_specs=placed,
        out_specs=(
            P("section", "fsdp", None, "ctx", None),
            P("section", "fsdp"),
            P("section", "fsdp", None),
            P("section", "fsdp", None),
            P("section", "fsdp", None),
            P("section", "fsdp"),
            P("section", "fsdp"),
            P("section", "fsdp", None),
            P("section", "fsdp"),
            P("section", "fsdp", None),
            P("section", "fsdp", None),
            P("section", "fsdp", None),
        ),
        check_vma=False,
    )
```

profile of v0, /device:TPU:0, one launch (start us, length us, event | category | flops | bytes accessed | tf_op | source)
XLA Modules:
  0.0 1871.3 jit_solution(15764830337283416297)
XLA Ops:
  15.8 14.2 all-reduce.19
  40.5 18.6 all-gather.21.cloned.1.call-done
  61.9 33.1 %all-gather.15.cloned.1.call-done = bf16[1,1,2,512,1024]{4,3,2,1,0:T(8,128)(2,1)} async-done(((bf16[1,1,2,128,1024]{4,3,2,1,0:T(8,128)(2,1)}), bf16[1,1,2,512,1024]{4,3,2,1,0:T(8,128)(2,1)}) %all-gather.15.cloned.1.call-update) | async-done | bytes 2097168 | tf_op jit(solution)/shard_map/all_gather | solution.py:298
  101.6 41.5 %all-gather.17.cloned.1.call-done = bf16[1,1024,1024]{2,1,0:T(8,128)(2,1)} async-done(((bf16[1,256,1024]{2,1,0:T(8,128)(2,1)}), bf16[1,1024,1024]{2,1,0:T(8,128)(2,1)}) %all-gather.17.cloned.1.call-update) | async-done | bytes 2097168 | tf_op jit(solution)/shard_map/all_gather | solution.py:341
  169.2 55.4 %all-gather.25.cloned.1.call-done = bf16[1,1024,2048]{2,1,0:T(8,128)(2,1)} async-done(((bf16[1,256,2048]{2,1,0:T(8,128)(2,1)}), bf16[1,1024,2048]{2,1,0:T(8,128)(2,1)}) %all-gather.25.cloned.1.call-update) | async-done | bytes 4194320 | tf_op jit(solution)/shard_map/all_gather | solution.py:339
  236.0 16.0 all-gather.23.cloned.1.call-done
  256.8 24.0 %all-gather.19.cloned.1.call-done = bf16[512,8,128]{0,2,1:T(8,128)(2,1)} async-done(((bf16[128,8,128]{0,2,1:T(8,128)(2,1)}), bf16[512,8,128]{0,2,1:T(8,128)(2,1)}) %all-gather.19.cloned.1.call-update) | async-done | bytes 1048592 | tf_op jit(solution)/shard_map/all_gather | solution.py:309
  284.3 79.5 %all-gather.27.cloned.1.call-done = bf16[1,2048,1024]{2,1,0:T(8,128)(2,1)} async-done(((bf16[1,512,1024]{2,1,0:T(8,128)(2,1)}), bf16[1,2048,1024]{2,1,0:T(8,128)(2,1)}) %all-gather.27.cloned.1.call-update) | async-done | bytes 4194320 | tf_op jit(solution)/shard_map/all_gather | solution.py:344
  366.9 112.9 %all-gather.29.cloned.1.call-done = bf16[1,1024,3072]{2,1,0:T(8,128)(2,1)} async-done(((bf16[1,256,3072]{2,1,0:T(8,128)(2,1)}), bf16[1,1024,3072]{2,1,0:T(8,128)(2,1)}) %all-gather.29.cloned.1.call-update) | async-done | bytes 6291472 | tf_op jit(solution)/shard_map/all_gather | solution.py:346
  484.7 110.8 %all-gather.31.cloned.1.call-done = bf16[1,1024,3072]{2,1,0:T(8,128)(2,1)} async-done(((bf16[1,256,3072]{2,1,0:T(8,128)(2,1)}), bf16[1,1024,3072]{2,1,0:T(8,128)(2,1)}) %all-gather.31.cloned.1.call-update) | async-done | bytes 6291472 | tf_op jit(solution)/shard_map/all_gather | solution.py:347
  601.1 109.4 %all-gather.33.cloned.1.call-done = bf16[1,3072,1024]{2,1,0:T(8,128)(2,1)} async-done(((bf16[1,768,1024]{2,1,0:T(8,128)(2,1)}), bf16[1,3072,1024]{2,1,0:T(8,128)(2,1)}) %all-gather.33.cloned.1.call-update) | async-done | bytes 6291472 | tf_op jit(solution)/shard_map/all_gather | solution.py:348
  732.6 14.2 all-gather.37.cloned.1.call-done
  752.1 23.6 %all-gather.35.cloned.1.call-done = bf16[512,8,128]{0,2,1:T(8,128)(2,1)} async-done(((bf16[128,8,128]{0,2,1:T(8,128)(2,1)}), bf16[512,8,128]{0,2,1:T(8,128)(2,1)}) %all-gather.35.cloned.1.call-update) | async-done | bytes 1048592 | tf_op jit(solution)/shard_map/all_gather | solution.py:309
  811.4 11.7 all-gather.41.cloned.1.call-done
  827.9 24.0 %all-gather.39.cloned.1.call-done = bf16[512,8,128]{0,2,1:T(8,128)(2,1)} async-done(((bf16[128,8,128]{0,2,1:T(8,128)(2,1)}), bf16[512,8,128]{0,2,1:T(8,128)(2,1)}) %all-gather.39.cloned.1.call-update) | async-done | bytes 1048592 | tf_op jit(solution)/shard_map/all_gather | solution.py:309
  894.4 27.5 %reduce-scatter.31.cloned.1.call-done = bf16[128,2048]{1,0:T(8,128)(2,1)} async-done(((bf16[512,2048]{1,0:T(8,128)(2,1)}), bf16[128,2048]{1,0:T(8,128)(2,1)}) %reduce-scatter.31.cloned.1.call-update) | async-done | bytes 524304
  970.4 31.0 %reduce-scatter.33.cloned.1.call-done = bf16[128,2048]{1,0:T(8,128)(2,1)} async-done(((bf16[512,2048]{1,0:T(8,128)(2,1)}), bf16[128,2048]{1,0:T(8,128)(2,1)}) %reduce-scatter.33.cloned.1.call-update) | async-done | bytes 524304
  1055.0 28.4 %reduce-scatter.35.cloned.1.call-done = bf16[128,2048]{1,0:T(8,128)(2,1)} async-done(((bf16[512,2048]{1,0:T(8,128)(2,1)}), bf16[128,2048]{1,0:T(8,128)(2,1)}) %reduce-scatter.35.cloned.1.call-update) | async-done | bytes 524304
  1189.6 67.6 %reduce-scatter.23.cloned.1.call-done = bf16[512,1024]{1,0:T(8,128)(2,1)} async-done(((bf16[2048,1024]{1,0:T(8,128)(2,1)}), bf16[512,1024]{1,0:T(8,128)(2,1)}) %reduce-scatter.23.cloned.1.call-update) | async-done | bytes 1048592 | tf_op jit(solution)/shard_map/reduce_scatter | solution.py:436
  1257.2 79.6 %reduce-scatter.17.cloned.1.call-done = bf16[256,2048]{1,0:T(8,128)(2,1)} async-done(((bf16[1024,2048]{1,0:T(8,128)(2,1)}), bf16[256,2048]{1,0:T(8,128)(2,1)}) %reduce-scatter.17.cloned.1.call-update) | async-done | bytes 1048592 | tf_op jit(solution)/shard_map/reduce_scatter | solution.py:421
  1336.8 113.7 %reduce-scatter.29.cloned.1.call-done = bf16[768,1024]{1,0:T(8,128)(2,1)} async-done(((bf16[3072,1024]{1,0:T(8,128)(2,1)}), bf16[768,1024]{1,0:T(8,128)(2,1)}) %reduce-scatter.29.cloned.1.call-update) | async-done | bytes 1572880 | tf_op jit(solution)/shard_map/reduce_scatter | solution.py:448
  1450.5 113.7 %reduce-scatter.25.cloned.1.call-done = bf16[256,3072]{1,0:T(8,128)(2,1)} async-done(((bf16[1024,3072]{1,0:T(8,128)(2,1)}), bf16[256,3072]{1,0:T(8,128)(2,1)}) %reduce-scatter.25.cloned.1.call-update) | async-done | bytes 1572880 | tf_op jit(solution)/shard_map/reduce_scatter | solution.py:442
  1564.2 113.6 %reduce-scatter.27.cloned.1.call-done = bf16[256,3072]{1,0:T(8,128)(2,1)} async-done(((bf16[1024,3072]{1,0:T(8,128)(2,1)}), bf16[256,3072]{1,0:T(8,128)(2,1)}) %reduce-scatter.27.cloned.1.call-update) | async-done | bytes 1572880 | tf_op jit(solution)/shard_map/reduce_scatter | solution.py:445
  1712.6 137.9 %all-reduce.24.cloned.1.call-done = (bf16[1,256,2048]{2,1,0:T(8,128)(2,1)}, bf16[1,256,1024]{2,1,0:T(8,128)(2,1)}, bf16[1,256,1024]{2,1,0:T(8,128)(2,1)}, bf16[1...) async-done(((bf16[1,256,2048]{2,1,0:T(8,128)(2,1)}, bf16[1,256,1024]{2,1,0:T(8,128)(2,1)}, ...) | async-done | bytes 7864336 | tf_op jit(solution)/shard_map/psum | solution.py:454
  (767 shorter events, 449.6 us)
Async XLA Ops:
  9.5 85.5 %all-gather.15.cloned.1.call-start = ((), (), s32[]{:S(2)}) async-start(), calls=%async_computation.10 | async-start | bytes 2621440 | tf_op jit(solution)/shard_map/all_gather | solution.py:298
  10.3 132.8 %all-gather.17.cloned.1.call-start = ((), (), s32[]{:S(2)}) async-start(), calls=%async_computation.11 | async-start | bytes 2621440 | tf_op jit(solution)/shard_map/all_gather | solution.py:341
  12.5 212.2 %all-gather.25.cloned.1.call-start = ((), (), s32[]{:S(2)}) async-start(), calls=%async_computation.15 | async-start | bytes 5242880 | tf_op jit(solution)/shard_map/all_gather | solution.py:339
  13.7 238.3 %all-gather.23.cloned.1.call-start = ((), (), s32[]{:S(2)}) async-start(), calls=%async_computation.14 | async-start | bytes 1310720 | tf_op jit(solution)/shard_map/all_gather | solution.py:308
  101.6 179.2 %all-gather.19.cloned.1.call-start = ((), (), s32[]{:S(2)}) async-start(), calls=%async_computation.12 | async-start | bytes 1310720 | tf_op jit(solution)/shard_map/all_gather | solution.py:309
  146.1 217.6 %all-gather.27.cloned.1.call-start = ((), (), s32[]{:S(2)}) async-start(), calls=%async_computation.16 | async-start | bytes 5242880 | tf_op jit(solution)/shard_map/all_gather | solution.py:344
  147.3 332.5 %all-gather.29.cloned.1.call-start = ((), (), s32[]{:S(2)}) async-start(), calls=%async_computation.17 | async-start | bytes 7864320 | tf_op jit(solution)/shard_map/all_gather | solution.py:346
  150.6 444.9 %all-gather.31.cloned.1.call-start = ((), (), s32[]{:S(2)}) async-start(), calls=%async_computation.18 | async-start | bytes 7864320 | tf_op jit(solution)/shard_map/all_gather | solution.py:347
  154.3 556.3 %all-gather.33.cloned.1.call-start = ((), (), s32[]{:S(2)}) async-start(), calls=%async_computation.19 | async-start | bytes 7864320 | tf_op jit(solution)/shard_map/all_gather | solution.py:348
  157.7 589.2 %all-gather.37.cloned.1.call-start = ((), (), s32[]{:S(2)}) async-start(), calls=%async_computation.21 | async-start | bytes 1310720 | tf_op jit(solution)/shard_map/all_gather | solution.py:308
  722.0 53.6 %all-gather.35.cloned.1.call-start = ((), (), s32[]{:S(2)}) async-start(), calls=%async_computation.20 | async-start | bytes 1310720 | tf_op jit(solution)/shard_map/all_gather | solution.py:309
  729.6 93.5 %all-gather.41.cloned.1.call-start = ((), (), s32[]{:S(2)}) async-start(), calls=%async_computation.23 | async-start | bytes 1310720 | tf_op jit(solution)/shard_map/all_gather | solution.py:308
  796.4 55.5 %all-gather.39.cloned.1.call-start = ((), (), s32[]{:S(2)}) async-start(), calls=%async_computation.22 | async-start | bytes 1310720 | tf_op jit(solution)/shard_map/all_gather | solution.py:309
  809.7 112.2 %reduce-scatter.31.cloned.1.call-start = ((), (), s32[]{:S(2)}) async-start(), calls=%async_computation.31 | async-start | bytes 2621440
  886.5 114.9 %reduce-scatter.33.cloned.1.call-start = ((), (), s32[]{:S(2)}) async-start(), calls=%async_computation.32 | async-start | bytes 2621440
  966.1 117.3 %reduce-scatter.35.cloned.1.call-start = ((), (), s32[]{:S(2)}) async-start(), calls=%async_computation.33 | async-start | bytes 2621440
  1048.1 141.5 %reduce-scatter.21.cloned.1.call-start = ((), (), s32[]{:S(2)}) async-start(), calls=%async_computation.26 | async-start | bytes 2621440 | tf_op jit(solution)/shard_map/reduce_scatter | solution.py:427
  1088.0 101.6 %reduce-scatter.19.cloned.1.call-start = ((), (), s32[]{:S(2)}) async-start(), calls=%async_computation.25 | async-start | bytes 2621440 | tf_op jit(solution)/shard_map/reduce_scatter | solution.py:424
  1104.5 152.7 %reduce-scatter.23.cloned.1.call-start = ((), (), s32[]{:S(2)}) async-start(), calls=%async_computation.27 | async-start | bytes 5242880 | tf_op jit(solution)/shard_map/reduce_scatter | solution.py:436
  1111.5 225.3 %reduce-scatter.17.cloned.1.call-start = ((), (), s32[]{:S(2)}) async-start(), calls=%async_computation.24 | async-start | bytes 5242880 | tf_op jit(solution)/shard_map/reduce_scatter | solution.py:421
  1122.8 327.7 %reduce-scatter.29.cloned.1.call-start = ((), (), s32[]{:S(2)}) async-start(), calls=%async_computation.30 | async-start | bytes 7864320 | tf_op jit(solution)/shard_map/reduce_scatter | solution.py:448
  1144.9 419.3 %reduce-scatter.25.cloned.1.call-start = ((), (), s32[]{:S(2)}) async-start(), calls=%async_computation.28 | async-start | bytes 7864320 | tf_op jit(solution)/shard_map/reduce_scatter | solution.py:442
  1167.7 510.1 %reduce-scatter.27.cloned.1.call-start = ((), (), s32[]{:S(2)}) async-start(), calls=%async_computation.29 | async-start | bytes 7864320 | tf_op jit(solution)/shard_map/reduce_scatter | solution.py:445
  1189.5 661.0 %all-reduce.24.cloned.1.call-start = ((), (), s32[]{:S(2)}) async-start(), calls=%async_computation.34 | async-start | bytes 15728640 | tf_op jit(solution)/shard_map/psum | solution.py:454
  (224 other events, 4197.0 us)
Sparse Core Ops, SparseCore 0:
  10.2 48.7 all-gather.20
  60.9 34.0 all-gather.14
  97.2 45.9 all-gather.16
  145.1 79.4 all-gather.24
  226.9 25.0 all-gather.22
  254.2 26.4 all-gather.18
  282.9 80.7 all-gather.26
  365.9 113.8 all-gather.28
  481.9 113.5 all-gather.30
  597.0 113.5 all-gather.32
  749.1 26.4 all-gather.34
  796.5 26.5 all-gather.40
  825.4 26.4 all-gather.38
  886.7 35.1 reduce-scatter.30
  966.2 35.1 reduce-scatter.32
  1048.2 35.1 reduce-scatter.34
  1088.1 44.5 reduce-scatter.20
  1135.6 42.9 reduce-scatter.18
  1180.9 76.2 reduce-scatter.22
  1259.5 77.2 reduce-scatter.16
  1339.2 111.2 reduce-scatter.28
  1452.9 111.2 reduce-scatter.24
  1566.5 111.2 reduce-scatter.26
  1683.1 167.3 all-reduce.23
  (1 shorter events, 24.6 us)
where the time goes:
time: 1880 us; the launch traced here: 1870 us
  waiting for transfers between devices  1390 us (74%)
  matrix products  249 us (13%)
  other arithmetic  81.5 us (4%)
  local copies, waits for them, and re-layouts  64.7 us (3%)
  blocking collectives  52.1 us (3%)
  between operations  19.8 us (1%)
    psum x1, waiting for transfers between devices, shards(): lax.psum(shares[1].astype(jnp.bfloat16), 'ctx').astype(jnp.float32)  138 us
    reduce_scatter x1, waiting for transfers between devices, shards(): lax.psum_scatter(totals[8].astype(jnp.bfloat16), 'fsdp', scatter_dimensio...  114 us
    reduce_scatter x1, waiting for transfers between devices, shards(): lax.psum_scatter(totals[10].astype(jnp.bfloat16), 'fsdp', scatter_dimensi...  114 us
    reduce_scatter x1, waiting for transfers between devices, shards(): lax.psum_scatter(totals[9].astype(jnp.bfloat16), 'fsdp', scatter_dimensio...  114 us
    all_gather x1, waiting for transfers between devices, shards(): lax.all_gather(low_masters[8], 'fsdp', axis=1, tiled=True)  113 us
    all_gather x1, waiting for transfers between devices, shards(): lax.all_gather(low_masters[9], 'fsdp', axis=1, tiled=True)  111 us
    all_gather x1, waiting for transfers between devices, shards(): lax.all_gather(low_masters[10], 'fsdp', axis=1, tiled=True)  109 us
    dot_general x21, matrix products, contract_rows(): lax.dot_general(left, right, (((0,), (0,)), ((), ())), preferred_element_...  101 us
  transfers between devices with their start and end apart: 29, of which 27 were waited for; matrix products, arithmetic and copies ran while one was open for 12% of the time, Pallas kernels for 0%

commit v1 on v0

v1 whole, which is shorter than its diff:
```python
import jax
import jax.numpy as jnp
from jax import lax
from jax.sharding import PartitionSpec as P

HEAD_DIM = 128
GAIN_ROWS = 16
epsilon = 1e-06
rope_base = 1000000.0
low = jnp.bfloat16
f32 = jnp.float32


def swap(value):
    return lax.ppermute(value, "section", [(0, 1), (1, 0)])


def hop(value, step):
    count = lax.axis_size("ctx")
    return lax.ppermute(value, "ctx", [(i, i ^ step) for i in range(count)])


def gather_rows(own):
    return jnp.concatenate([own] + [hop(own, k) for k in range(1, lax.axis_size("ctx"))], axis=0)


def scatter_rows(partial):
    count = lax.axis_size("ctx")
    pieces = partial.astype(low).reshape(count, -1, partial.shape[-1])
    total = pieces[0].astype(f32)
    for k in range(1, count):
        total = total + hop(pieces[k], k).astype(f32)
    return total


def rms_scale(values, gain):
    scale = lax.rsqrt(jnp.mean(values * values, axis=-1, keepdims=True) + epsilon)
    return values * scale * gain


def rotate(values, cosine, sine):
    half = values.shape[-1] // 2
    turned = jnp.concatenate([-values[..., half:], values[..., :half]], axis=-1)
    return values * cosine + turned * sine


def head_prepare(raw, gain, cosine, sine):
    shape = (1,) * (raw.ndim - 2)
    cosine = cosine.reshape(cosine.shape[:1] + shape + cosine.shape[1:])
    sine = sine.reshape(sine.shape[:1] + shape + sine.shape[1:])
    return rotate(rms_scale(raw, gain), cosine, sine)


def swiglu(gate, lifted):
    return gate * jax.nn.sigmoid(gate) * lifted


def dot(left, right):
    return jnp.dot(left, right, preferred_element_type=f32)


def dot_rows(left, right):
    return lax.dot_general(left, right, (((0,), (0,)), ((), ())), preferred_element_type=f32)


def dot_cols(left, right):
    return lax.dot_general(left, right, (((1,), (1,)), ((), ())), preferred_element_type=f32)


def es(text, left, right):
    return jnp.einsum(text, left, right, preferred_element_type=f32)


def layer_forward(hidden, weights, context):
    attention_gain, mlp_gain, query_gain, key_gain, qkv, out, lift, down = weights
    cosine, sine, visible = context
    normed = gather_rows(rms_scale(hidden, attention_gain).astype(low))
    tokens = normed.shape[0]
    raw = dot(normed, qkv).reshape(tokens, 2, -1, HEAD_DIM)
    group = raw.shape[2] - 2
    query_raw, key_raw, value_rows = raw[:, :, :group], raw[:, :, group], raw[:, :, group + 1]
    value_rows = value_rows.astype(low)
    queries = head_prepare(query_raw, query_gain, cosine, sine).astype(low)
    key_rows = head_prepare(key_raw, key_gain, cosine, sine).astype(low)
    scores = es("tvgd,uvd->vgtu", queries, key_rows) * HEAD_DIM ** (-0.5)
    scores = jnp.where(visible, scores, -1e30)
    raised = jnp.exp(scores - jnp.max(scores, axis=-1, keepdims=True))
    probs = raised / jnp.sum(raised, axis=-1, keepdims=True)
    mixed = es("vgtu,uvd->tvgd", probs.astype(low), value_rows).astype(low).reshape(tokens, -1)
    middle = hidden + scatter_rows(dot(mixed, out))
    normed_mlp = gather_rows(rms_scale(middle, mlp_gain).astype(low))
    both = dot(normed_mlp, lift).reshape(tokens, 2, 2, -1)
    gate, lifted = both[:, :, 0], both[:, :, 1]
    product = swiglu(gate, lifted).astype(low).reshape(tokens, -1)
    result = middle + scatter_rows(dot(product, down))
    kept = (hidden, normed, query_raw, key_raw, value_rows, queries, key_rows, probs, mixed)
    return result, kept + (middle, normed_mlp, gate, lifted, product)


def layer_backward(upstream, kept, weights, context):
    attention_gain, mlp_gain, query_gain, key_gain, qkv, out, lift, down = weights
    hidden, normed, query_raw, key_raw, value_rows, queries, key_rows, probs, mixed = kept[:9]
    middle, normed_mlp, gate, lifted, product = kept[9:]
    cosine, sine, visible = context
    scale = HEAD_DIM ** (-0.5)
    tokens = normed.shape[0]
    branch = gather_rows(upstream.astype(low))
    grad_down = dot_rows(product, branch)
    grad_product = dot_cols(branch, down).reshape(gate.shape)
    unused, pull = jax.vjp(swiglu, gate, lifted)
    grad_gate, grad_lifted = pull(grad_product)
    grad_both = jnp.stack([grad_gate.astype(low), grad_lifted.astype(low)], axis=2)
    grad_both = grad_both.reshape(tokens, -1)
    grad_lift = dot_rows(normed_mlp, grad_both)
    grad_normed_mlp = scatter_rows(dot_cols(grad_both, lift))
    unused, pull = jax.vjp(rms_scale, middle, mlp_gain)
    grad_middle, grad_mlp_gain = pull(grad_normed_mlp)
    grad_middle = upstream + grad_middle
    branch = gather_rows(grad_middle.astype(low))
    grad_out = dot_rows(mixed, branch)
    grad_mixed = dot_cols(branch, out).astype(low).reshape(queries.shape)
    probs_low = probs.astype(low)
    grad_probs = es("tvgd,uvd->vgtu", grad_mixed, value_rows)
    weighted = jnp.sum(probs * grad_probs, axis=-1, keepdims=True)
    grad_scores = (probs * (grad_probs - weighted)).astype(low)
    grad_queries = es("vgtu,uvd->tvgd", grad_scores, key_rows) * scale
    grad_keys = es("vgtu,tvgd->uvd", grad_scores, queries) * scale
    grad_values = es("vgtu,tvgd->uvd", probs_low, grad_mixed).astype(low)

    def prepare(raw, gain):
        return head_prepare(raw, gain, cosine, sine)

    unused, pull = jax.vjp(prepare, query_raw, query_gain)
    grad_query_raw, grad_query_gain = pull(grad_queries)
    unused, pull = jax.vjp(prepare, key_raw, key_gain)
    grad_key_raw, grad_key_gain = pull(grad_keys)
    grad_raw = jnp.concatenate(
        [grad_query_raw.astype(low), grad_key_raw.astype(low)[:, :, None], grad_values[:, :, None]],
        axis=2,
    ).reshape(tokens, -1)
    grad_qkv = dot_rows(normed, grad_raw)
    grad_normed = scatter_rows(dot_cols(grad_raw, qkv))
    unused, pull = jax.vjp(rms_scale, hidden, attention_gain)
    grad_hidden, grad_attention_gain = pull(grad_normed)
    gains = (grad_attention_gain, grad_mlp_gain, grad_query_gain, grad_key_gain)
    return grad_middle + grad_hidden, (gains, grad_qkv, grad_out, grad_lift, grad_down)


def shards(
    stream_in,
    lengths,
    dealing,
    attention_gain,
    query_weight,
    key_weight,
    value_weight,
    query_gain,
    key_gain,
    out_weight,
    mlp_gain,
    gate_weight,
    up_weight,
    down_weight,
):
    core = lax.axis_index("section")
    piece = lax.axis_index("ctx")
    count = lax.axis_size("ctx")
    depth = lax.axis_size("fsdp")
    rows, width = stream_in.shape[3], stream_in.shape[4]
    tokens = rows * count
    first = core == 0
    query_half = query_weight.shape[2] // (2 * count)
    key_half = key_weight.shape[2] // (2 * count)
    hidden_half = gate_weight.shape[2] // (2 * count)
    part = query_weight.shape[1]
    aligned = depth == count

    def ordered(own, other, axis=0):
        pair = jnp.where(first, jnp.stack([own, other]), jnp.stack([other, own]))
        return jnp.moveaxis(pair, 0, axis)

    def columns(weight, half, size):
        start = (piece * 2 + half) * size
        return lax.dynamic_slice_in_dim(weight[0], start, size, 1).astype(low)

    def quarter(weight, half, size):
        share = size // count
        return lax.dynamic_slice_in_dim(weight[0], half * size + piece * share, share, 0).astype(low)

    gains = (attention_gain[0], mlp_gain[0], query_gain[0], key_gain[0])
    sizes = [gain.shape[0] for gain in gains]
    block_width = query_half + 2 * key_half
    gain_block = jnp.concatenate(gains).astype(low)
    gain_block = jnp.pad(gain_block, (0, GAIN_ROWS * block_width - gain_block.shape[0]))
    gain_block = gain_block.reshape(GAIN_ROWS, block_width)

    def attention_block(half):
        block = [columns(query_weight, half, query_half), columns(key_weight, half, key_half)]
        block = jnp.concatenate(block + [columns(value_weight, half, key_half)], axis=1)
        return jnp.concatenate([block, gain_block], axis=0)

    def lift_block(half):
        block = [columns(gate_weight, half, hidden_half), columns(up_weight, half, hidden_half)]
        return jnp.concatenate(block, axis=1)

    def row_block(half):
        return jnp.concatenate(
            [quarter(out_weight, half, query_half), quarter(down_weight, half, hidden_half)], axis=0
        )

    def by_layer(make):
        mine = make(core)
        other = swap(make(1 - core))
        return jnp.where(first, mine, other), jnp.where(first, other, mine)

    def both_halves(own):
        return own, swap(own)

    blocks = by_layer(attention_block), by_layer(lift_block)
    row_blocks = by_layer(row_block) if aligned else None
    out_share, down_share = query_half // count, hidden_half // count
    if not aligned:
        whole = []
        for weight, size in ((out_weight, query_half), (down_weight, hidden_half)):
            full = lax.all_gather(weight[0].astype(low), "fsdp", axis=0, tiled=True)
            full = lax.dynamic_slice_in_dim(full, piece * 2 * size, 2 * size, 0)
            other = swap(full)
            layers = jnp.where(first, full, other), jnp.where(first, other, full)
            own = [lax.dynamic_slice_in_dim(v, core * size, size, 0) for v in layers]
            far = [lax.dynamic_slice_in_dim(v, (1 - core) * size, size, 0) for v in layers]
            whole.append([jnp.concatenate(pair, axis=0) for pair in zip(own, far)])

    def layer_weights(layer):
        own = lax.all_gather(blocks[0][layer], "fsdp", axis=0, tiled=False)
        packed = own[:, part:].reshape(depth, -1)
        split = []
        at = 0
        for size in sizes:
            split.append(packed[:, at : at + size].reshape(-1).astype(f32))
            at += size
        qkv = jnp.concatenate(both_halves(own[:, :part].reshape(width, block_width)), axis=1)
        if aligned:
            own = lax.all_gather(row_blocks[layer], "fsdp", axis=0, tiled=False)
            own = lax.all_to_all(own, "ctx", 0, 0, tiled=True)
            far = swap(own)
            out = [half[:, :out_share].reshape(query_half, width) for half in (own, far)]
            down = [half[:, out_share:].reshape(hidden_half, width) for half in (own, far)]
            out, down = jnp.concatenate(out, axis=0), jnp.concatenate(down, axis=0)
        else:
            out, down = whole[0][layer], whole[1][layer]
        own = lax.all_gather(blocks[1][layer], "fsdp", axis=0, tiled=True)
        lift = jnp.concatenate(both_halves(own), axis=1)
        return (*split, qkv, out, lift, down)

    lens = lax.dynamic_index_in_dim(lengths[0], core, 0, keepdims=False)
    slots = lax.dynamic_index_in_dim(dealing[0], core, 0, keepdims=False)
    index = jnp.arange(tokens, dtype=jnp.int32)
    natural = ((index // rows) ^ piece) * rows + index % rows
    bounds = jnp.cumsum(lens)
    passed = (bounds[None, :] <= natural[:, None]).astype(jnp.int32)
    sequence = jnp.sum(passed, axis=1)
    position = natural - jnp.sum(passed * lens[None, :], axis=1)
    half = HEAD_DIM // 2
    rates = jnp.power(rope_base, jnp.arange(half, dtype=f32) * (-2.0 / HEAD_DIM))
    phase = position.astype(f32)[:, None] * rates
    phase = jnp.concatenate([phase, phase], axis=-1)
    visible = (sequence[None, :] == sequence[:, None]) & (natural[None, :] <= natural[:, None])
    context = (jnp.cos(phase), jnp.sin(phase), visible)

    own = lax.dynamic_index_in_dim(stream_in[0, 0], core, 0, keepdims=False)
    other = swap(lax.dynamic_index_in_dim(stream_in[0, 0], 1 - core, 0, keepdims=False))
    hidden = jnp.where(first, own, other)
    cotangent = jnp.where(first, other, own)

    layers = [layer_weights(0), layer_weights(1)]
    result, kept_first = layer_forward(hidden.astype(f32), layers[0], context)
    middle = result.astype(low)
    result, kept_last = layer_forward(middle.astype(f32), layers[1], context)
    last = result.astype(low)
    grad, grads_last = layer_backward(cotangent.astype(f32), kept_last, layers[1], context)
    grad = grad.astype(low)
    grad, grads_first = layer_backward(grad.astype(f32), kept_first, layers[0], context)
    grad = grad.astype(low)

    wanted = lax.dynamic_slice_in_dim(slots, piece * rows, rows, 0)
    wanted = ((wanted // rows) ^ piece) * rows + wanted % rows
    chosen = (wanted[:, None] == index[None, :]).astype(low)

    def dealt(value):
        return dot(chosen, gather_rows(value)).astype(low)

    last, grad = dealt(last), dealt(grad)
    own = jnp.where(first, grad, last)
    other = swap(jnp.where(first, last, grad))
    boundary = ordered(own, other)

    def meet(grad_own, grad_other):
        return grad_own + swap(grad_other.astype(low)).astype(f32)

    def reduced(grads):
        gains, grad_qkv, grad_out, grad_lift, grad_down = grads
        total = meet(grad_qkv[:, :block_width], grad_qkv[:, block_width:])
        split = [gain.reshape(depth, -1) for gain in gains]
        packed = jnp.concatenate(split, axis=1)
        packed = meet(packed, packed)
        packed = jnp.pad(packed, ((0, 0), (0, GAIN_ROWS * block_width - packed.shape[1])))
        packed = packed.reshape(depth, GAIN_ROWS, block_width)
        total = jnp.concatenate([total.reshape(depth, part, block_width), packed], axis=1)
        total = lax.psum_scatter(total.astype(low), "fsdp", scatter_dimension=0, tiled=False)
        attention = lax.all_gather(total, "ctx", axis=0, tiled=False)
        total = meet(grad_lift[:, : 2 * hidden_half], grad_lift[:, 2 * hidden_half :])
        total = lax.psum_scatter(total.astype(low), "fsdp", scatter_dimension=0, tiled=True)
        lift = lax.all_gather(total, "ctx", axis=0, tiled=False)
        out = meet(grad_out[:query_half], grad_out[query_half:])
        down = meet(grad_down[:hidden_half], grad_down[hidden_half:])
        if aligned:
            total = [out.reshape(count, out_share, width), down.reshape(count, down_share, width)]
            total = jnp.concatenate(total, axis=1).astype(low)
            total = lax.all_to_all(total, "ctx", 0, 0, tiled=True)
            total = lax.psum_scatter(total, "fsdp", scatter_dimension=0, tiled=False)
            rest = (lax.all_gather(total, "ctx", axis=0, tiled=False),)
        else:
            rest = []
            for grad, size in ((out, query_half), (down, hidden_half)):
                full = jnp.zeros((2 * count * size, width), low)
                at = (piece * 2 + core) * size
                full = lax.dynamic_update_slice_in_dim(full, grad.astype(low), at, 0)
                full = lax.psum_scatter(full, "fsdp", scatter_dimension=0, tiled=True)
                rest.append(lax.psum(full, "ctx"))
        return (attention, lift, *rest)

    pairs = []
    for from_first, from_last in zip(reduced(grads_first), reduced(grads_last)):
        own = jnp.where(first, from_first, from_last)
        pairs.append((own, swap(jnp.where(first, from_last, from_first))))

    def side(own, other, start, stop):
        both = ordered(own[..., start:stop], other[..., start:stop], axis=1)
        return jnp.moveaxis(both, 2, 0).reshape(1, own.shape[1], -1).astype(f32)

    own, other = pairs[0]
    middle_at = query_half + key_half
    grad_query = side(own[:, :part], other[:, :part], 0, query_half)
    grad_key = side(own[:, :part], other[:, :part], query_half, middle_at)
    grad_value = side(own[:, :part], other[:, :part], middle_at, block_width)
    packed = jnp.sum(own[:, part:].reshape(count, -1).astype(f32), axis=0)
    packed_gains = []
    at = 0
    for size in sizes:
        packed_gains.append(packed[None, at : at + size])
        at += size
    own, other = pairs[1]
    grad_gate = side(own, other, 0, hidden_half)
    grad_up = side(own, other, hidden_half, 2 * hidden_half)
    if aligned:
        own, other = pairs[2]

        def stacked(start, stop):
            both = ordered(own[:, start:stop], other[:, start:stop])
            return both.reshape(1, -1, width).astype(f32)

        grad_out = stacked(0, out_share)
        grad_down = stacked(out_share, out_share + down_share)
    else:
        grad_out, grad_down = [(own.astype(f32) + other.astype(f32))[None] for own, other in pairs[2:]]
    return (
        boundary[None, None],
        packed_gains[0],
        grad_query,
        grad_key,
        grad_value,
        packed_gains[2],
        packed_gains[3],
        grad_out,
        packed_gains[1],
        grad_gate,
        grad_up,
        grad_down,
    )


def solution(mesh):
    weight, gain, row = P("section", "fsdp", None), P("section", "fsdp"), P("fsdp", None, None)
    stream = P("section", "fsdp", None, "ctx", None)
    masters = (gain, weight, weight, weight, gain, gain, weight, gain, weight, weight, weight)
    return jax.shard_map(
        shards,
        mesh=mesh,
        in_specs=(stream, row, row) + masters,
        out_specs=(stream,) + masters,
        check_vma=False,
    )
```

time: 1880 us -> 860 us (0.46)
  waiting for transfers between devices: 1390 us -> 452 us
  matrix products: 249 us -> 73.8 us
  starting transfers between devices: 9.44 us -> 79.5 us
  local copies, waits for them, and re-layouts: 64.7 us -> 114 us
    all_gather x14 -> x12, waiting for transfers between devices: 675 us -> 216 us  [the longest x2 58.9 us: reduced(): lift = lax.all_gather(total, 'ctx', axis=0, tiled=False)]
    reduce_scatter x7 -> x6, waiting for transfers between devices: 488 us -> 85.7 us  [the longest x2 73.3 us: reduced(): lax.psum_scatter(total.astype(low), 'fsdp', scatter_dimension=0, tiled=True)]
    dot_general x81 -> x32, matrix products: 249 us -> 54.2 us  [the longest x8 18.8 us: dot_rows(): lax.dot_general(left, right, (((0,), (0,)), ((), ())), preferred_element_...]
    psum x1 -> x0, waiting for transfers between devices: 138 us -> none  [shards(): lax.psum(shares[1].astype(jnp.bfloat16), 'ctx').astype(jnp.float32)]
    ppermute x4 -> x78, waiting for transfers between devices: 5.83 us -> 143 us  [the longest x54 130 us: hop(): return lax.ppermute(value, 'ctx', [(i, i ^ step) for i in range(count)])]
    unnamed x28 -> x18, waiting for transfers between devices: 88 us -> 1.78 us
    ppermute x4 -> x78, starting transfers between devices: 7.15 us -> 69.1 us  [the longest x54 64.4 us: hop(): return lax.ppermute(value, 'ctx', [(i, i ^ step) for i in range(count)])]
    all_to_all x0 -> x2, blocking collectives: none -> 42.1 us  [reduced(): total = lax.all_to_all(total, 'ctx', 0, 0, tiled=True)]
  transfers between devices with their start and end apart: 29 -> 98, of which waited for: 27 -> 61; matrix products, arithmetic and copies ran while one was open for 12% -> 23% of each run, Pallas kernels for 0% -> 0%
where the time goes in v1:
time: 860 us; the launch traced here: 848 us
  waiting for transfers between devices  452 us (53%)
  local copies, waits for them, and re-layouts  114 us (13%)
  starting transfers between devices  79.5 us (9%)
  matrix products  73.8 us (9%)
  other arithmetic  69.8 us (8%)
  blocking collectives  42.1 us (5%)
  between operations  16.8 us (2%)
    ppermute x54, waiting for transfers between devices, hop(): return lax.ppermute(value, 'ctx', [(i, i ^ step) for i in range(count)])  130 us
    reduce_scatter x2, waiting for transfers between devices, reduced(): lax.psum_scatter(total.astype(low), 'fsdp', scatter_dimension=0, tiled=True)  73.3 us
    ppermute x54, starting transfers between devices, hop(): return lax.ppermute(value, 'ctx', [(i, i ^ step) for i in range(count)])  64.4 us
    all_gather x2, waiting for transfers between devices, reduced(): lift = lax.all_gather(total, 'ctx', axis=0, tiled=False)  58.9 us
    all_gather x2, waiting for transfers between devices, reduced(): rest = (lax.all_gather(total, 'ctx', axis=0, tiled=False),)  43.3 us
    all_to_all x2, blocking collectives, reduced(): total = lax.all_to_all(total, 'ctx', 0, 0, tiled=True)  42.1 us
    unnamed x255, local copies, waits for them, and re-layouts  36.8 us
    all_gather x2, waiting for transfers between devices, layer_weights(): own = lax.all_gather(blocks[1][layer], 'fsdp', axis=0, tiled=True)  34 us
  transfers between devices with their start and end apart: 98, of which 61 were waited for; matrix products, arithmetic and copies ran while one was open for 23% of the time, Pallas kernels for 0%

profile of v1, /device:TPU:0, one launch (start us, length us, event | category | flops | bytes accessed | tf_op | source)
XLA Modules:
  0.0 848.2 jit_solution(5904010626231199406)
XLA Ops:
  25.4 20.1 %all-gather.33.cloned.1.call-done = bf16[1088,512]{1,0:T(8,128)(2,1)} async-done(((bf16[272,512]{1,0:T(8,128)(2,1)}), bf16[1088,512]{1,0:T(8,128)(2,1)}) %all-gather.33.cloned.1.call-update) | async-done | bytes 1114128 | tf_op jit(solution)/shard_map/all_gather | solution.py:234
  53.5 26.3 %all-gather.35.cloned.1.call-done = bf16[640,1024]{1,0:T(8,128)(2,1)} async-done(((bf16[160,1024]{1,0:T(8,128)(2,1)}), bf16[640,1024]{1,0:T(8,128)(2,1)}) %all-gather.35.cloned.1.call-update) | async-done | bytes 1310736 | tf_op jit(solution)/shard_map/all_gather | solution.py:243
  84.1 34.0 %all-gather.19.cloned.1.call-done = bf16[1024,768]{1,0:T(8,128)(2,1)} async-done(((bf16[256,768]{1,0:T(8,128)(2,1)}), bf16[1024,768]{1,0:T(8,128)(2,1)}) %all-gather.19.cloned.1.call-update) | async-done | bytes 1572880 | tf_op jit(solution)/shard_map/all_gather | solution.py:251
  160.4 6.6 collective-permute-done.14
  167.0 8.8 %collective-permute-done.13 = bf16[128,1024]{1,0:T(8,128)(2,1)} collective-permute-done((bf16[128,1024]{1,0:T(8,128)(2,1)S(1)}, bf16[128,1024]{1,0:T(8,128)(2,1)}, u32[]{:S(2)}, u32[]{:S(2)}) %collective-permute-start.13) | collective-permute-done | bytes 262176 | tf_op jit(solution)/shard_map/ppermute | solution.py:20
  183.3 5.2 all-to-all-done
  211.2 5.5 collective-permute-done.22
  277.1 5.2 collective-permute-done.29
  283.4 6.3 collective-permute-done.28
  320.4 5.1 collective-permute-done.36
  364.6 5.8 collective-permute-done.40
  463.2 21.1 %all_to_all.20 = bf16[4,160,1024]{2,1,0:T(8,128)(2,1)} all-to-all(bf16[4,160,1024]{2,1,0:T(8,128)(2,1)S(1)} %pad_maximum_fusion.11), channel_id=1, replica_groups=mesh['section'=2,'ctx'=4,'fsdp'=4] {'ctx'}, dimensions={0} | all-to-all | bytes 2621440 | tf_op jit(solution)/shard_map/all_to_all | solution.py:319
  491.3 21.1 %all_to_all.21 = bf16[4,160,1024]{2,1,0:T(8,128)(2,1)} all-to-all(bf16[4,160,1024]{2,1,0:T(8,128)(2,1)S(1)} %pad_maximum_fusion.10), channel_id=1, replica_groups=mesh['section'=2,'ctx'=4,'fsdp'=4] {'ctx'}, dimensions={0} | all-to-all | bytes 2621440 | tf_op jit(solution)/shard_map/all_to_all | solution.py:319
  537.6 12.3 %reduce-scatter.11.cloned.1.call-done = bf16[1,160,1024]{2,1,0:T(8,128)(2,1)} async-done(((bf16[4,160,1024]{2,1,0:T(8,128)(2,1)}), bf16[1,160,1024]{2,1,0:T(8,128)(2,1)}) %reduce-scatter.11.cloned.1.call-update) | async-done | bytes 327696 | tf_op jit(solution)/shard_map/reduce_scatter | solution.py:320
  550.0 36.9 %reduce-scatter.17.cloned.1.call-done = bf16[256,768]{1,0:T(8,128)(2,1)} async-done(((bf16[1024,768]{1,0:T(8,128)(2,1)}), bf16[256,768]{1,0:T(8,128)(2,1)}) %reduce-scatter.17.cloned.1.call-update) | async-done | bytes 393232 | tf_op jit(solution)/shard_map/reduce_scatter | solution.py:312
  599.9 6.4 collective-permute-done.62
  606.7 5.2 collective-permute-done.57
  617.3 5.9 all-gather.25.cloned.1.call-done
  624.9 36.4 %reduce-scatter.15.cloned.1.call-done = bf16[256,768]{1,0:T(8,128)(2,1)} async-done(((bf16[1024,768]{1,0:T(8,128)(2,1)}), bf16[256,768]{1,0:T(8,128)(2,1)}) %reduce-scatter.15.cloned.1.call-update) | async-done | bytes 393232 | tf_op jit(solution)/shard_map/reduce_scatter | solution.py:312
  661.4 27.9 %all-gather.23.cloned.1.call-done = bf16[4,272,512]{2,1,0:T(8,128)(2,1)} async-done(((bf16[1,272,512]{2,1,0:T(8,128)(2,1)}), bf16[4,272,512]{2,1,0:T(8,128)(2,1)}) %all-gather.23.cloned.1.call-update) | async-done | bytes 1114128 | tf_op jit(solution)/shard_map/all_gather | solution.py:310
  707.0 12.7 %all-gather.29.cloned.1.call-done = bf16[4,160,1024]{2,1,0:T(8,128)(2,1)} async-done(((bf16[1,160,1024]{2,1,0:T(8,128)(2,1)}), bf16[4,160,1024]{2,1,0:T(8,128)(2,1)}) %all-gather.29.cloned.1.call-update) | async-done | bytes 1310736 | tf_op jit(solution)/shard_map/all_gather | solution.py:321
  719.7 30.5 %all-gather.27.cloned.1.call-done = bf16[4,160,1024]{2,1,0:T(8,128)(2,1)} async-done(((bf16[1,160,1024]{2,1,0:T(8,128)(2,1)}), bf16[4,160,1024]{2,1,0:T(8,128)(2,1)}) %all-gather.27.cloned.1.call-update) | async-done | bytes 1310736 | tf_op jit(solution)/shard_map/all_gather | solution.py:321
  756.8 26.2 %all-gather.41.cloned.1.call-done = bf16[1024,768]{1,0:T(8,128)(2,1)} async-done(((bf16[256,768]{1,0:T(8,128)(2,1)}), bf16[1024,768]{1,0:T(8,128)(2,1)}) %all-gather.41.cloned.1.call-update) | async-done | bytes 1572880 | tf_op jit(solution)/shard_map/all_gather | solution.py:313
  783.0 32.7 %all-gather.39.cloned.1.call-done = bf16[1024,768]{1,0:T(8,128)(2,1)} async-done(((bf16[256,768]{1,0:T(8,128)(2,1)}), bf16[1024,768]{1,0:T(8,128)(2,1)}) %all-gather.39.cloned.1.call-update) | async-done | bytes 1572880 | tf_op jit(solution)/shard_map/all_gather | solution.py:313
  (689 shorter events, 427.3 us)
Async XLA Ops:
  13.7 66.1 %all-gather.35.cloned.1.call-start = ((), (), s32[]{:S(2)}) async-start(), calls=%async_computation.24 | async-start | bytes 1638400 | tf_op jit(solution)/shard_map/all_gather | solution.py:243
  18.7 99.3 %all-gather.19.cloned.1.call-start = ((), (), s32[]{:S(2)}) async-start(), calls=%async_computation.10 | async-start | bytes 1966080 | tf_op jit(solution)/shard_map/all_gather | solution.py:251
  23.2 131.3 %all-gather.31.cloned.1.call-start = ((), (), s32[]{:S(2)}) async-start(), calls=%async_computation.22 | async-start | bytes 1638400 | tf_op jit(solution)/shard_map/all_gather | solution.py:243
  24.1 181.2 %all-gather.37.cloned.1.call-start = ((), (), s32[]{:S(2)}) async-start(), calls=%async_computation.25 | async-start | bytes 1392640 | tf_op jit(solution)/shard_map/all_gather | solution.py:234
  46.8 71.4 %collective-permute-start.10 = (bf16[1024,512]{1,0:T(8,128)(2,1)S(1)}, bf16[1024,512]{1,0:T(8,128)(2,1)}, u32[]{:S(2)}, u32[]{:S(2)}) collective-permute-start(bf16[1024,512]{1,0:T(8,128)(2,1)S(1)} %bitcast.429), channel_id=1, source_target_pairs={{0,16},{16,0},{1,17},{17,1},{2,18},{18,2},{3,19},{19,3},{4,20},{20... | collective-permute-start | bytes 3145736 | tf_op jit(solution)/shard_map/ppermute | solution.py:15
  48.0 70.1 %collective-permute-start.9 = (bf16[128,1024]{1,0:T(8,128)(2,1)S(1)}, bf16[128,1024]{1,0:T(8,128)(2,1)S(1)}, u32[]{:S(2)}, u32[]{:S(2)}) collective-permute-start(bf16[128,1024]{1,0:T(8,128)(2,1)S(1)} %fusion.77), channel_id=1, source_target_pairs={{0,12},{4,8},{8,4},{12,0},{1,13},{5,9},{9,5},{13,1},{2,14},{6,10},... | collective-permute-start | bytes 786440 | tf_op jit(solution)/shard_map/ppermute | solution.py:20
  50.5 67.6 %collective-permute-start.8 = (bf16[128,1024]{1,0:T(8,128)(2,1)S(1)}, bf16[128,1024]{1,0:T(8,128)(2,1)S(1)}, u32[]{:S(2)}, u32[]{:S(2)}) collective-permute-start(bf16[128,1024]{1,0:T(8,128)(2,1)S(1)} %fusion.77), channel_id=1, source_target_pairs={{0,8},{4,12},{8,0},{12,4},{1,9},{5,13},{9,1},{13,5},{2,10},{6,14},... | collective-permute-start | bytes 786440 | tf_op jit(solution)/shard_map/ppermute | solution.py:20
  51.0 67.1 %collective-permute-start.7 = (bf16[128,1024]{1,0:T(8,128)(2,1)S(1)}, bf16[128,1024]{1,0:T(8,128)(2,1)S(1)}, u32[]{:S(2)}, u32[]{:S(2)}) collective-permute-start(bf16[128,1024]{1,0:T(8,128)(2,1)S(1)} %fusion.77), channel_id=1, source_target_pairs={{0,4},{4,0},{8,12},{12,8},{1,5},{5,1},{9,13},{13,9},{2,6},{6,2},{1... | collective-permute-start | bytes 786440 | tf_op jit(solution)/shard_map/ppermute | solution.py:20
  118.1 70.4 %collective-permute-start.19 = (bf16[1024,768]{1,0:T(8,128)(2,1)}, bf16[1024,768]{1,0:T(8,128)(2,1)}, u32[]{:S(2)}, u32[]{:S(2)}) collective-permute-start(bf16[1024,768]{1,0:T(8,128)(2,1)} %all-gather.19.cloned.1.call-done), channel_id=1, source_target_pairs={{0,16},{16,0},{1,17},{17,1},{2,18},{18,2},{3,19},{19,3},{4,20},{20... | collective-permute-start | bytes 4718600 | tf_op jit(solution)/shard_map/ppermute | solution.py:15
  158.8 67.1 %all-gather.21.cloned.1.call-start = ((), (), s32[]{:S(2)}) async-start(), calls=%async_computation.11 | async-start | bytes 1966080 | tf_op jit(solution)/shard_map/all_gather | solution.py:251
  159.4 369.5 %reduce-scatter.9.cloned.1.call-start = ((), (), s32[]{:S(2)}) async-start(), calls=%async_computation.14 | async-start | bytes 1392640 | tf_op jit(solution)/shard_map/reduce_scatter | solution.py:309
  225.9 66.2 %collective-permute-start.33 = (bf16[1024,768]{1,0:T(8,128)(2,1)}, bf16[1024,768]{1,0:T(8,128)(2,1)}, u32[]{:S(2)}, u32[]{:S(2)}) collective-permute-start(bf16[1024,768]{1,0:T(8,128)(2,1)} %all-gather.21.cloned.1.call-done), channel_id=1, source_target_pairs={{0,16},{16,0},{1,17},{17,1},{2,18},{18,2},{3,19},{19,3},{4,20},{20... | collective-permute-start | bytes 4718600 | tf_op jit(solution)/shard_map/ppermute | solution.py:15
  419.8 116.6 %reduce-scatter.7.cloned.1.call-start = ((), (), s32[]{:S(2)}) async-start(), calls=%async_computation.12 | async-start | bytes 1392640 | tf_op jit(solution)/shard_map/reduce_scatter | solution.py:309
  458.5 78.6 %reduce-scatter.13.cloned.1.call-start = ((), (), s32[]{:S(2)}) async-start(), calls=%async_computation.18 | async-start | bytes 1638400 | tf_op jit(solution)/shard_map/reduce_scatter | solution.py:320
  512.4 74.5 %reduce-scatter.17.cloned.1.call-start = ((), (), s32[]{:S(2)}) async-start(), calls=%async_computation.21 | async-start | bytes 1966080 | tf_op jit(solution)/shard_map/reduce_scatter | solution.py:312
  521.2 102.0 %all-gather.25.cloned.1.call-start = ((), (), s32[]{:S(2)}) async-start(), calls=%async_computation.15 | async-start | bytes 1392640 | tf_op jit(solution)/shard_map/all_gather | solution.py:310
  528.9 132.4 %reduce-scatter.15.cloned.1.call-start = ((), (), s32[]{:S(2)}) async-start(), calls=%async_computation.20 | async-start | bytes 1966080 | tf_op jit(solution)/shard_map/reduce_scatter | solution.py:312
  536.4 152.8 %all-gather.23.cloned.1.call-start = ((), (), s32[]{:S(2)}) async-start(), calls=%async_computation.13 | async-start | bytes 1392640 | tf_op jit(solution)/shard_map/all_gather | solution.py:310
  537.0 182.8 %all-gather.29.cloned.1.call-start = ((), (), s32[]{:S(2)}) async-start(), calls=%async_computation.19 | async-start | bytes 1638400 | tf_op jit(solution)/shard_map/all_gather | solution.py:321
  537.5 212.7 %all-gather.27.cloned.1.call-start = ((), (), s32[]{:S(2)}) async-start(), calls=%async_computation.17 | async-start | bytes 1638400 | tf_op jit(solution)/shard_map/all_gather | solution.py:321
  549.9 233.0 %all-gather.41.cloned.1.call-start = ((), (), s32[]{:S(2)}) async-start(), calls=%async_computation.27 | async-start | bytes 1966080 | tf_op jit(solution)/shard_map/all_gather | solution.py:313
  586.9 228.7 %all-gather.39.cloned.1.call-start = ((), (), s32[]{:S(2)}) async-start(), calls=%async_computation.26 | async-start | bytes 1966080 | tf_op jit(solution)/shard_map/all_gather | solution.py:313
  617.3 79.0 %collective-permute-start.64 = (bf16[128,1024]{1,0:T(8,128)(2,1)}, bf16[128,1024]{1,0:T(8,128)(2,1)}, u32[]{:S(2)}, u32[]{:S(2)}) collective-permute-start(bf16[128,1024]{1,0:T(8,128)(2,1)} %get-tuple-element.169), channel_id=1, source_target_pairs={{0,16},{16,0},{1,17},{17,1},{2,18},{18,2},{3,19},{19,3},{4,20},{20... | collective-permute-start | bytes 786440 | tf_op jit(solution)/shard_map/ppermute | solution.py:15
  753.2 65.8 %collective-permute-start.74 = (bf16[4,160,1024]{2,1,0:T(8,128)(2,1)}, bf16[4,160,1024]{2,1,0:T(8,128)(2,1)}, u32[]{:S(2)}, u32[]{:S(2)}) collective-permute-start(bf16[4,160,1024]{2,1,0:T(8,128)(2,1)} %get-tuple-element.113), channel_id=1, source_target_pairs={{0,16},{16,0},{1,17},{17,1},{2,18},{18,2},{3,19},{19,3},{4,20},{20... | collective-permute-start | bytes 3932168 | tf_op jit(solution)/shard_map/ppermute | solution.py:15
  (189 other events, 2450.5 us)
Sparse Core Ops, SparseCore 0:
  13.8 31.6 all-gather.32
  47.6 32.1 all-gather.34
  82.0 36.0 all-gather.18
  120.1 31.5 all-gather.30
  153.1 27.9 all-gather.36
  183.1 36.5 all-gather.20
  419.9 25.7 reduce-scatter.8
  458.6 26.8 reduce-scatter.6
  487.8 29.8 reduce-scatter.12
  519.9 29.9 reduce-scatter.10
  552.8 34.0 reduce-scatter.16
  588.6 34.4 all-gather.24
  626.0 35.2 reduce-scatter.14
  663.0 26.1 all-gather.22
  690.9 28.7 all-gather.28
  721.4 28.7 all-gather.26
  752.0 30.9 all-gather.40
  784.7 30.9 all-gather.38

commit v2 on v1

v2 whole, which is shorter than its diff:
```python
import functools

import jax
import jax.numpy as jnp
from jax import lax
from jax.experimental import pallas as pl
from jax.experimental.pallas import tpu as pltpu
from jax.sharding import PartitionSpec as P

HEAD_DIM = 128
GAIN_ROWS = 16
LANES = 256
VMEM_LIMIT = 56 * 1024 * 1024
FLOPS_PER_US = 1.15e9
SCALE = HEAD_DIM ** (-0.5)
epsilon = 1e-06
rope_base = 1000000.0
low = jnp.bfloat16
f32 = jnp.float32


def swap(value):
    return lax.ppermute(value, "section", [(0, 1), (1, 0)])


def hop(value, step):
    count = lax.axis_size("ctx")
    return lax.ppermute(value, "ctx", [(i, i ^ step) for i in range(count)])


def hops(own):
    return [own] + [hop(own, k) for k in range(1, lax.axis_size("ctx"))]


def met(parts):
    return [parts[0]] + [hop(parts[k], k) for k in range(1, len(parts))]


def beside(results, others):
    return lax.optimization_barrier((results, others))


def tie(value, other):
    return lax.optimization_barrier((value, other))[0]


def xored(pieces, index):
    for bit in range(len(pieces).bit_length() - 1):
        turned = ((index >> bit) & 1) == 1
        pieces = [jnp.where(turned, pieces[j ^ (1 << bit)], v) for j, v in enumerate(pieces)]
    return pieces


def dot(left, right):
    return jnp.dot(left, right, preferred_element_type=f32)


def dot_rows(left, right):
    return lax.dot_general(left, right, (((0,), (0,)), ((), ())), preferred_element_type=f32)


def dot_cols(left, right):
    return lax.dot_general(left, right, (((1,), (1,)), ((), ())), preferred_element_type=f32)


def rms_scale(values, gain):
    scale = lax.rsqrt(jnp.mean(values * values, axis=-1, keepdims=True) + epsilon)
    return values * scale * gain


def rms_back(values, gain, grad):
    scale = lax.rsqrt(jnp.mean(values * values, axis=-1, keepdims=True) + epsilon)
    unit = values * scale
    lifted = grad * gain
    grad_values = (lifted - unit * jnp.mean(lifted * unit, axis=-1, keepdims=True)) * scale
    return grad_values, jnp.sum(grad * unit, axis=0, keepdims=True)


def turn(values, cosine, sine):
    return values * cosine + pltpu.roll(values, HEAD_DIM // 2, 1) * sine


def turn_back(grad, cosine, sine):
    return grad * cosine + pltpu.roll(grad * sine, HEAD_DIM // 2, 1)


def chunk(j, size):
    return pl.ds(pl.multiple_of(j * size, size), size)


def span(j, size):
    return slice(j * size, (j + 1) * size)


def join(pieces, target):
    rows = pieces[0].shape[0]
    for i, piece in enumerate(pieces):
        target[span(i, rows), :] = piece[...]


def deal_out(parts, block, value):
    rows = parts[0].shape[0]
    for i, part in enumerate(parts):
        part[:, block] = value[span(i, rows)].astype(part.dtype)


def call(kernel, operands, outputs, took, scratch=(), scalars=(), after=()):
    vmem = pl.BlockSpec(memory_space=pltpu.VMEM)
    smem = pl.BlockSpec(memory_space=pltpu.SMEM)
    anywhere = pl.BlockSpec(memory_space=pl.ANY)
    shapes = [jax.ShapeDtypeStruct(shape, dtype) for shape, dtype in outputs]
    moved = sum(v.size * v.dtype.itemsize for v in [*operands, *shapes])
    skipped, used = len(after), len(scalars)

    def body(*refs):
        kernel(*refs[skipped:])

    return pl.pallas_call(
        body,
        out_shape=shapes,
        in_specs=[anywhere] * skipped + [smem] * used + [vmem] * len(operands),
        out_specs=[vmem] * len(shapes),
        scratch_shapes=[pltpu.VMEM(shape, dtype) for shape, dtype in scratch],
        compiler_params=pltpu.CompilerParams(vmem_limit_bytes=VMEM_LIMIT),
        cost_estimate=pl.CostEstimate(
            flops=int(took * FLOPS_PER_US), bytes_accessed=moved, transcendentals=0
        ),
    )(*after, *scalars, *operands)


def add_kernel(count, rounded, *refs):
    parts, (residual, gain, total, normed) = refs[:count], refs[count:]
    value = residual[...].astype(f32)
    for part in parts:
        value = value + part[...].astype(f32)
    if rounded:
        value = value.astype(low).astype(f32)
    total[...] = value
    normed[...] = rms_scale(value, gain[...]).astype(low)


def add_back_kernel(count, rounded, *refs):
    parts, (upstream, middle, gain, total, sent, grad_gain) = refs[:count], refs[count:]
    grad = parts[0][...].astype(f32)
    for part in parts[1:]:
        grad = grad + part[...].astype(f32)
    grad, gains = rms_back(middle[...].astype(f32), gain[...], grad)
    grad = upstream[...].astype(f32) + grad
    sent[...] = grad.astype(low)
    total[...] = grad.astype(low).astype(f32) if rounded else grad
    grad_gain[...] = gains


def attention_forward_kernel(count, part, raw_rows, *refs):
    pieces, refs = refs[:count], refs[count:]
    if raw_rows:
        gain, *refs = refs
    own_weight, far_weight, cosine, sine, query_gain, key_gain, start, place, place_row, *refs = refs
    normed, raw, queries, keys, mixed, spread, values = refs
    tokens = normed.shape[0]
    rows = pieces[0].shape[0]
    depth = own_weight.shape[0]
    halves = keys.shape[1] // HEAD_DIM
    group = queries.shape[1] // keys.shape[1]
    step = (group + 2) * HEAD_DIM
    if raw_rows:
        for i, piece in enumerate(pieces):
            normed[span(i, rows), :] = rms_scale(piece[...].astype(f32), gain[...]).astype(low)
    else:
        join(pieces, normed)
    for half, weight in enumerate((own_weight, far_weight)):
        for j, at in enumerate((0, part + GAIN_ROWS)):
            total = None
            for z in range(depth):
                term = dot(normed[:, span(z, part)], weight[z, at : at + part, :])
                total = term if total is None else total + term
            raw[:, span(2 * half + j, LANES)] = total

    for half in range(halves):
        base = half * step
        at = base + group * HEAD_DIM
        own = span(half, HEAD_DIM)
        unit = rms_scale(raw[:, at : at + HEAD_DIM], key_gain[...])
        keys[:, own] = turn(unit, cosine[...], sine[...]).astype(low)
        values[:, own] = raw[:, at + HEAD_DIM : at + 2 * HEAD_DIM].astype(low)
        for g in range(group):
            unit = rms_scale(raw[:, base + g * HEAD_DIM : base + (g + 1) * HEAD_DIM], query_gain[...])
            unit = turn(unit, cosine[...], sine[...])
            queries[:, span(half * group + g, HEAD_DIM)] = unit.astype(low)

    @pl.loop(0, tokens // rows)
    def _(i):
        block = chunk(i, rows)
        visible = (place_row[...] >= start[block, :]) & (place_row[...] <= place[block, :])
        for head in range(halves * group):
            own, at = span(head // group, HEAD_DIM), span(head, HEAD_DIM)
            scores = dot_cols(queries[block, at], keys[:, own]) * SCALE
            scores = jnp.where(visible, scores, -1e30)
            top = jnp.max(scores, axis=-1, keepdims=True)
            raised = jnp.exp(scores - top)
            total = jnp.sum(raised, axis=-1, keepdims=True)
            probs = (raised * (1.0 / total)).astype(low)
            mixed[block, at] = dot(probs, values[:, own]).astype(low)
            spread[block, head : head + 1] = top + jnp.log(total)


def rows_kernel(count, ordered, *refs):
    index, left, own, far, *refs = refs
    parts, whole = refs[:count], refs[count]
    if ordered:
        whole[...] = own[...]
    else:
        size = whole.shape[0] // 2
        share = size // count
        for half, value in enumerate((own, far)):
            for k in range(count):
                to = half * size + (index[0] ^ k) * share
                to = pl.ds(pl.multiple_of(to, share), share)
                for j in range(whole.shape[1] // LANES):
                    whole[to, span(j, LANES)] = value[k, span(j, share), :]

    @pl.loop(0, whole.shape[1] // LANES)
    def _(j):
        block = chunk(j, LANES)
        deal_out(parts, block, dot(left[...], whole[:, block]))


def lift_kernel(count, part, *refs):
    pieces, (own_weight, far_weight, normed, gate, lifted, product) = refs[:count], refs[count:]
    half_size = product.shape[1] // 2
    depth = own_weight.shape[0]
    join(pieces, normed)
    for half, weight in enumerate((own_weight, far_weight)):
        both = []
        for j in range(2 * half_size // LANES):
            total = None
            for z in range(depth):
                term = dot(normed[:, span(z, part)], weight[z, span(j, part), :])
                total = term if total is None else total + term
            both.append(total)
        both = jnp.concatenate(both, axis=1)
        one, two = both[:, :half_size], both[:, half_size:]
        at = span(half, half_size)
        gate[:, at] = one
        lifted[:, at] = two
        product[:, at] = (one * jax.nn.sigmoid(one) * two).astype(low)


def mlp_backward_kernel(count, part, *refs):
    pieces, refs = refs[:count], refs[count:]
    own_weight, far_weight, down, gate, lifted, *refs = refs
    parts, (branch, grad_both) = refs[:count], refs[count:]
    size = gate.shape[1] // 2
    depth = own_weight.shape[0]
    join(pieces, branch)
    for half in range(2):
        at = span(half, size)
        grad = dot_cols(branch[...], down[at, :])
        one, two = gate[:, at], lifted[:, at]
        sigmoid = jax.nn.sigmoid(one)
        grad_gate = grad * two * sigmoid * (1.0 + one * (1.0 - sigmoid))
        grad_both[:, span(2 * half, size)] = grad_gate.astype(low)
        grad_both[:, span(2 * half + 1, size)] = (grad * one * sigmoid).astype(low)
    for z in range(depth):
        total = None
        for half, weight in enumerate((own_weight, far_weight)):
            for j in range(2 * size // LANES):
                at = 2 * half * size + j * LANES
                term = dot_cols(grad_both[:, at : at + LANES], weight[z, span(j, part), :])
                total = term if total is None else total + term
        deal_out(parts, span(z, part), total)


def attention_backward_kernel(count, part, *refs):
    pieces, refs = refs[:count], refs[count:]
    own_weight, far_weight, out, *refs = refs
    cosine, sine, query_gain, key_gain, start, place, place_row, *refs = refs
    raw, queries, keys, spread, *refs = refs
    parts, refs = refs[:count], refs[count:]
    branch, grad_raw, grad_query_gain, grad_key_gain, *refs = refs
    grad_mixed, values, grad_queries, grad_keys, grad_values = refs
    tokens, width = branch.shape
    rows = pieces[0].shape[0]
    depth = own_weight.shape[0]
    halves = keys.shape[1] // HEAD_DIM
    group = queries.shape[1] // keys.shape[1]
    step = (group + 2) * HEAD_DIM
    join(pieces, branch)

    @pl.loop(0, grad_mixed.shape[1] // LANES)
    def _(j):
        block = chunk(j, LANES)
        grad_mixed[:, block] = dot_cols(branch[...], out[block, :]).astype(low)

    for half in range(halves):
        at = half * step + (group + 1) * HEAD_DIM
        values[:, span(half, HEAD_DIM)] = raw[:, at : at + HEAD_DIM].astype(low)
    grad_keys[...] = jnp.zeros_like(grad_keys)
    grad_values[...] = jnp.zeros_like(grad_values)

    @pl.loop(0, tokens // rows)
    def _(i):
        block = chunk(i, rows)
        visible = (place_row[...] >= start[block, :]) & (place_row[...] <= place[block, :])
        for head in range(halves * group):
            own, at = span(head // group, HEAD_DIM), span(head, HEAD_DIM)
            query, grad = queries[block, at], grad_mixed[block, at]
            scores = dot_cols(query, keys[:, own]) * SCALE
            scores = jnp.where(visible, scores, -1e30)
            probs = jnp.exp(scores - spread[block, head : head + 1])
            grad_probs = dot_cols(grad, values[:, own])
            weighted = jnp.sum(probs * grad_probs, axis=-1, keepdims=True)
            grad_scores = (probs * (grad_probs - weighted)).astype(low)
            grad_queries[block, at] = dot(grad_scores, keys[:, own]) * SCALE
            grad_keys[:, own] += dot_rows(grad_scores, query) * SCALE
            grad_values[:, own] += dot_rows(probs.astype(low), grad)

    total_query = jnp.zeros((1, HEAD_DIM), f32)
    total_key = jnp.zeros((1, HEAD_DIM), f32)
    for half in range(halves):
        base = half * step
        own = span(half, HEAD_DIM)
        for g in range(group + 1):
            at = slice(base + g * HEAD_DIM, base + (g + 1) * HEAD_DIM)
            if g < group:
                grad, gain = grad_queries[:, span(half * group + g, HEAD_DIM)], query_gain[...]
            else:
                grad, gain = grad_keys[:, own], key_gain[...]
            grad = turn_back(grad, cosine[...], sine[...])
            grad, grad_gain = rms_back(raw[:, at], gain, grad)
            grad_raw[:, at] = grad.astype(low)
            if g < group:
                total_query += grad_gain
            else:
                total_key += grad_gain
        at = base + (group + 1) * HEAD_DIM
        grad_raw[:, at : at + HEAD_DIM] = grad_values[:, own].astype(low)
    grad_query_gain[...] = total_query
    grad_key_gain[...] = total_key
    for z in range(depth):
        total = None
        for half, weight in enumerate((own_weight, far_weight)):
            for j, at in enumerate((0, part + GAIN_ROWS)):
                grad = grad_raw[:, span(2 * half + j, LANES)]
                term = dot_cols(grad, weight[z, at : at + part, :])
                total = term if total is None else total + term
        deal_out(parts, span(z, part), total)


def weight_grads_kernel(part, left, grads, inner, branch, own, far, own_rows, far_rows, turned):
    depth, count = own.shape[0], own_rows.shape[0]
    chunks = grads.shape[1] // (2 * LANES)
    size = inner.shape[1] // 2
    share = size // count
    for z in range(depth):
        turned[span(z, part), :] = left[:, span(z, part)].T
    for half, target in enumerate((own, far)):
        for j in range(chunks):
            total = dot(turned[...], grads[:, span(half * chunks + j, LANES)])
            for z in range(depth):
                target[z, span(j, part), :] = total[span(z, part)].astype(target.dtype)
    for half, target in enumerate((own_rows, far_rows)):
        rows = inner[:, span(half, size)].T
        for j in range(branch.shape[1] // LANES):
            total = dot(rows, branch[:, span(j, LANES)])
            for k in range(count):
                target[k, span(j, share), :] = total[span(k, share)].astype(target.dtype)


def meet_kernel(index, own, recv, own_rows, recv_rows, total, *rows):
    total[...] = (own[...] + recv[...].astype(f32)).astype(low)
    for k, row in enumerate(rows):
        at = index[0] ^ k
        row[...] = (own_rows[at] + recv_rows[at].astype(f32)).astype(low)


def layout_kernel(part, mid, index, *refs):
    total, *refs = refs
    refs = list(refs)
    gains = refs.pop(0) if mid else None
    *rows, out = refs
    depth = out.shape[0]
    size = total.shape[1]
    extra = GAIN_ROWS if mid else 0
    for z in range(depth):
        out[z, :part, :] = total[z, :part, :]
        if mid:
            out[z, part : part + extra, :] = gains[z]
        out[z, part + extra : size + extra, :] = total[z, part:, :]
    for k, row in enumerate(rows):
        out[index[0] ^ k, size + extra :, :] = row[...]


def shards(
    stream_in,
    lengths,
    dealing,
    attention_gain,
    query_weight,
    key_weight,
    value_weight,
    query_gain,
    key_gain,
    out_weight,
    mlp_gain,
    gate_weight,
    up_weight,
    down_weight,
):
    core = lax.axis_index("section")
    piece = lax.axis_index("ctx")
    count = lax.axis_size("ctx")
    depth = lax.axis_size("fsdp")
    rows, width = stream_in.shape[3], stream_in.shape[4]
    tokens = rows * count
    first = core == 0
    query_half = query_weight.shape[2] // (2 * count)
    key_half = key_weight.shape[2] // (2 * count)
    hidden_half = gate_weight.shape[2] // (2 * count)
    part = query_weight.shape[1]
    aligned = depth == count
    out_share, down_share = query_half // count, hidden_half // count
    index = piece.astype(jnp.int32).reshape(1)
    chunks = width // LANES
    qkv_rows = 2 * part + GAIN_ROWS
    lift_rows = 2 * hidden_half // LANES * part

    where = jnp.stack([piece, core]).astype(jnp.int32)

    def cut(kernel, weights, constants, size):
        def half(i, where):
            return jnp.where(i == 0, 1 - where[1], where[1])

        def columns(i, where):
            return 0, 0, where[0] * 2 + half(i, where)

        def shares(i, where):
            return 0, half(i, where) * count + where[0], 0

        in_specs = [
            pl.BlockSpec((1, height, breadth), shares if by_rows else columns)
            for _, height, breadth, by_rows in weights
        ]
        in_specs += [pl.BlockSpec(v.shape, lambda i, where: (0, 0)) for v in constants]
        return pl.pallas_call(
            kernel,
            grid_spec=pltpu.PrefetchScalarGridSpec(
                num_scalar_prefetch=1,
                grid=(2,),
                in_specs=in_specs,
                out_specs=pl.BlockSpec((1, size, LANES), lambda i, where: (i, 0, 0)),
            ),
            out_shape=jax.ShapeDtypeStruct((2, size, LANES), low),
            compiler_params=pltpu.CompilerParams(vmem_limit_bytes=VMEM_LIMIT),
            cost_estimate=pl.CostEstimate(
                flops=int(3 * FLOPS_PER_US), bytes_accessed=12 * size * LANES, transcendentals=0
            ),
        )(where, *[weight for weight, *_ in weights], *constants)

    def place_shares(weight, out, at):
        share = weight.shape[1]
        for j in range(chunks):
            out[0, at + j * share : at + (j + 1) * share, :] = weight[0, :, span(j, LANES)].astype(low)

    def qkv_cut_kernel(where, query, key, value, *refs):
        *rest, gains, out = refs
        out[0, :part, :] = query[0].astype(low)
        out[0, part : part + GAIN_ROWS, :] = gains[...]
        at = slice(part + GAIN_ROWS, qkv_rows)
        out[0, at, :key_half] = key[0].astype(low)
        out[0, at, key_half:] = value[0].astype(low)
        if aligned:
            place_shares(rest[0], out, qkv_rows)

    def mlp_cut_kernel(where, gate, up, *refs):
        *rest, out = refs
        both = jnp.concatenate([gate[0].astype(low), up[0].astype(low)], axis=1)
        for j in range(2 * hidden_half // LANES):
            out[0, span(j, part), :] = both[:, span(j, LANES)]
        if aligned:
            place_shares(rest[0], out, lift_rows)

    gains = (attention_gain[0], mlp_gain[0], query_gain[0], key_gain[0])
    sizes = [gain.shape[0] for gain in gains]
    gain_block = jnp.concatenate(gains).astype(low)
    gain_block = jnp.pad(gain_block, (0, GAIN_ROWS * LANES - gain_block.shape[0]))
    gain_block = gain_block.reshape(GAIN_ROWS, LANES)

    def by_layer(cuts):
        mine, other = cuts[1], swap(cuts[0])
        return jnp.where(first, mine, other), jnp.where(first, other, mine)

    weights = [(query_weight, part, query_half, False), (key_weight, part, key_half, False)]
    weights += [(value_weight, part, key_half, False)]
    weights += [(out_weight, out_share, width, True)] if aligned else []
    size = qkv_rows + (chunks * out_share if aligned else 0)
    attention_blocks = by_layer(cut(qkv_cut_kernel, weights, [gain_block], size))
    weights = [(gate_weight, part, hidden_half, False), (up_weight, part, hidden_half, False)]
    weights += [(down_weight, down_share, width, True)] if aligned else []
    size = lift_rows + (chunks * down_share if aligned else 0)
    mlp_blocks = by_layer(cut(mlp_cut_kernel, weights, [], size))

    def gathered(block):
        return lax.all_gather(block, "fsdp", axis=0, tiled=False)

    def gathered_direct(block):
        pieces = [block]
        for k in range(1, depth):
            pieces.append(lax.ppermute(block, "fsdp", [(i, i ^ k) for i in range(depth)]))
        return jnp.stack(xored(pieces, lax.axis_index("fsdp")))

    def whole_rows(weight, size):
        full = lax.all_gather(weight[0].astype(low), "fsdp", axis=0, tiled=True)
        full = lax.dynamic_slice_in_dim(full, piece * 2 * size, 2 * size, 0)
        other = swap(full)
        layers = jnp.where(first, full, other), jnp.where(first, other, full)
        own = [lax.dynamic_slice_in_dim(v, core * size, size, 0) for v in layers]
        far = [lax.dynamic_slice_in_dim(v, (1 - core) * size, size, 0) for v in layers]
        return [jnp.concatenate(pair, axis=0) for pair in zip(own, far)]

    def shared_rows(value):
        sent = [lax.dynamic_index_in_dim(value, piece ^ k, 0, keepdims=False) for k in range(count)]
        own = jnp.stack(met(sent))
        return own, swap(own)

    def split_gains(own):
        found, at = [], 0
        flat = own[:, part : part + GAIN_ROWS].reshape(depth, -1)
        for size in sizes:
            found.append(flat[:, at : at + size].reshape(1, -1).astype(f32))
            at += size
        return found

    lens = lax.dynamic_index_in_dim(lengths[0], core, 0, keepdims=False)
    slots = lax.dynamic_index_in_dim(dealing[0], core, 0, keepdims=False)
    order = jnp.arange(tokens, dtype=jnp.int32)
    natural = ((order // rows) ^ piece) * rows + order % rows
    bounds = jnp.cumsum(lens)
    passed = (bounds[None, :] <= natural[:, None]).astype(jnp.int32)
    start = jnp.sum(passed * lens[None, :], axis=1)
    position = natural - start
    rates = jnp.power(rope_base, jnp.arange(HEAD_DIM // 2, dtype=f32) * (-2.0 / HEAD_DIM))
    phase = position.astype(f32)[:, None] * rates
    cosine, sine = jnp.cos(phase), jnp.sin(phase)
    cosine = jnp.concatenate([cosine, cosine], axis=-1)
    sine = jnp.concatenate([-sine, sine], axis=-1)
    places = [start[:, None], natural[:, None], natural[None, :]]

    own = lax.dynamic_index_in_dim(stream_in[0, 0], core, 0, keepdims=False)
    other = swap(lax.dynamic_index_in_dim(stream_in[0, 0], 1 - core, 0, keepdims=False))
    entering = jnp.where(first, own, other)
    cotangent = jnp.where(first, other, own)

    wide, half_wide = (rows, width), (tokens, width)
    heads_wide, hidden_wide = 2 * query_half, 2 * hidden_half

    def add(parts, residual, gain, rounded, after=()):
        kernel = functools.partial(add_kernel, count, rounded)
        outputs = [(wide, f32), (wide, low)]
        return call(kernel, [*parts, residual, gain], outputs, 2, after=after)

    def add_back(parts, upstream, middle, gain, rounded, after=()):
        kernel = functools.partial(add_back_kernel, count, rounded)
        outputs = [(wide, f32), (wide, low), ((1, width), f32)]
        return call(kernel, [*parts, upstream, middle, gain], outputs, 2, after=after)

    def attention_forward(pieces, weights, found, raw_rows, after=()):
        kernel = functools.partial(attention_forward_kernel, count, part, raw_rows)
        outputs = [(half_wide, low), ((tokens, 2 * (query_half + 2 * key_half)), f32)]
        outputs += [((tokens, heads_wide), low), ((tokens, 2 * key_half), low)]
        outputs += [((tokens, heads_wide), low), ((tokens, heads_wide // HEAD_DIM), f32)]
        operands = [*pieces] + ([found[0]] if raw_rows else [])
        operands += [*weights, cosine, sine, found[2], found[3], *places]
        return call(kernel, operands, outputs, 12, [((tokens, 2 * key_half), low)], after=after)

    def rows_product(left, shares, after=()):
        kernel = functools.partial(rows_kernel, count, not aligned)
        outputs = [(wide, low)] * count + [((left.shape[1], width), low)]
        *parts, whole = call(kernel, [left, *shares], outputs, 4, scalars=[index], after=after)
        return parts, whole

    def lift_forward(pieces, weights, after=()):
        kernel = functools.partial(lift_kernel, count, part)
        outputs = [(half_wide, low)] + [((tokens, hidden_wide), f32)] * 2
        outputs += [((tokens, hidden_wide), low)]
        return call(kernel, [*pieces, *weights], outputs, 6, after=after)

    def mlp_backward(pieces, weights, down, kept, after=()):
        kernel = functools.partial(mlp_backward_kernel, count, part)
        outputs = [(wide, low)] * count + [(half_wide, low), ((tokens, 2 * hidden_wide), low)]
        operands = [*pieces, *weights, down, kept[1], kept[2]]
        *parts, branch, both = call(kernel, operands, outputs, 9, after=after)
        return parts, branch, both

    def attention_backward(pieces, weights, out, found, kept, after=()):
        kernel = functools.partial(attention_backward_kernel, count, part)
        normed, raw, queries, keys, mixed, spread = kept
        outputs = [(wide, low)] * count + [(half_wide, low), (raw.shape, low)]
        outputs += [((1, HEAD_DIM), f32)] * 2
        scratch = [(queries.shape, low), (keys.shape, low), (queries.shape, f32)]
        scratch += [(keys.shape, f32)] * 2
        operands = [*pieces, *weights, out, cosine, sine, found[2], found[3], *places]
        operands += [raw, queries, keys, spread]
        *parts, branch, grad_raw, query, key = call(
            kernel, operands, outputs, 18, scratch, after=after
        )
        return parts, branch, grad_raw, (query, key)

    def weight_grads(left, grads, inner, branch, after=()):
        kernel = functools.partial(weight_grads_kernel, part)
        shape = (depth, grads.shape[1] // (2 * LANES) * part, LANES)
        row_shape = (count, inner.shape[1] // (2 * count) * chunks, LANES)
        outputs = [(shape, f32), (shape, low), (row_shape, f32), (row_shape, low)]
        operands = [left, grads, inner, branch]
        return call(kernel, operands, outputs, 6, [((width, tokens), low)], after=after)

    own = gathered_direct(attention_blocks[0])
    pieces = hops(tie(entering, attention_blocks[0]))
    own = tie(own, pieces)
    qkv_first = [own, swap(own)]
    found_first = split_gains(own)
    if aligned:
        out_first = shared_rows(own[:, qkv_rows:])
    else:
        outs, downs = whole_rows(out_weight, query_half), whole_rows(down_weight, hidden_half)
        out_first = [outs[0], outs[0]]
    kept_attention_first = attention_forward(pieces, qkv_first, found_first, True)
    kept_attention_first, out_first = beside(kept_attention_first, out_first)
    parts, out_first = rows_product(kept_attention_first[4], out_first)
    middle_first, normed = add(met(parts), entering, found_first[1], False)
    own = tie(gathered(tie(mlp_blocks[0], own)), normed)
    lift_first = [own, swap(own)]
    down_first = shared_rows(own[:, lift_rows:]) if aligned else [downs[0], downs[0]]
    kept_mlp_first = lift_forward(hops(normed), lift_first)
    kept_mlp_first, down_first = beside(kept_mlp_first, down_first)
    parts, down_first = rows_product(kept_mlp_first[3], down_first)

    own = tie(gathered(attention_blocks[1]), kept_mlp_first[3])
    qkv_last = [own, swap(own)]
    found_last = split_gains(own)
    out_last = shared_rows(own[:, qkv_rows:]) if aligned else [outs[1], outs[1]]
    hidden_last, normed = add(met(parts), middle_first, found_last[0], True)
    kept_attention_last = attention_forward(
        hops(normed), qkv_last, found_last, False, after=[out_last[1]]
    )
    parts, out_last = rows_product(kept_attention_last[4], out_last)
    middle_last, normed = add(met(parts), hidden_last, found_last[1], False)
    own = tie(gathered(mlp_blocks[1]), normed)
    lift_last = [own, swap(own)]
    down_last = shared_rows(own[:, lift_rows:]) if aligned else [downs[1], downs[1]]
    kept_mlp_last = lift_forward(hops(normed), lift_last)
    kept_mlp_last, down_last = beside(kept_mlp_last, down_last)
    last_parts, down_last = rows_product(kept_mlp_last[3], down_last)

    def meet(grads, swapped):
        own, far, own_rows, far_rows = grads
        if not aligned:
            total = (own + swapped[0].astype(f32)).astype(low)
            return total, [own_rows + swapped[1].astype(f32)]
        outputs = [(own.shape, low)] + [(own_rows.shape[1:], low)] * count
        operands = [own, swapped[0], own_rows, swapped[1]]
        total, *rows_by = call(meet_kernel, operands, outputs, 4, scalars=[index])
        return total, rows_by

    def met_gains(gains):
        split = jnp.concatenate([gain.reshape(depth, -1) for gain in gains], axis=1)
        split = split + swap(split.astype(low)).astype(f32)
        split = jnp.pad(split, ((0, 0), (0, GAIN_ROWS * LANES - split.shape[1])))
        return split.reshape(depth, GAIN_ROWS, LANES).astype(low)

    def laid_out(total, rows_by, gains=None):
        operands = [total] + ([] if gains is None else [gains])
        size = total.shape[1] + (0 if gains is None else GAIN_ROWS)
        if aligned:
            operands += rows_by
            size += rows_by[0].shape[0]
        kernel = functools.partial(layout_kernel, part, gains is not None)
        outputs = [((depth, size, LANES), low)]
        return call(kernel, operands, outputs, 3, scalars=[index])[0]

    def scattered(operand):
        return lax.psum_scatter(operand, "fsdp", scatter_dimension=0, tiled=False)

    def rows_fallback(rest):
        (rest,) = rest
        share = rest.shape[1] // chunks
        rest = rest.reshape(count, chunks, share, LANES).swapaxes(1, 2).reshape(-1, width)
        full = jnp.zeros((2 * count * rest.shape[0], width), low)
        at = (piece * 2 + core) * rest.shape[0]
        full = lax.dynamic_update_slice_in_dim(full, rest.astype(low), at, 0)
        return lax.psum(lax.psum_scatter(full, "fsdp", scatter_dimension=0, tiled=True), "ctx")

    wanted = lax.dynamic_slice_in_dim(slots, piece * rows, rows, 0)
    wanted = ((wanted // rows) ^ piece) * rows + wanted % rows
    chosen = (wanted[:, None] == order[None, :]).astype(low)

    def dealt(pieces):
        return dot(chosen, jnp.concatenate(pieces, axis=0)).astype(low)

    def returned(pieces, layer):
        own = jnp.stack(pieces)
        return own, lax.ppermute(own, "section", [(1 - layer, layer)])

    pieces = hops(cotangent)
    parts, branch, both = mlp_backward(pieces, lift_last, down_last, kept_mlp_last)
    parts = met(parts)
    mlp_grads = weight_grads(kept_mlp_last[0], both, kept_mlp_last[3], branch)
    grad, sent, mlp_gain = add_back(
        parts, cotangent, middle_last, found_last[1], False, after=[mlp_grads[1]]
    )
    swapped = swap(mlp_grads[1]), swap(mlp_grads[3])
    pieces = hops(sent)
    mlp_total, mlp_rows = meet(mlp_grads, swapped)
    results = attention_backward(
        pieces, qkv_last, out_last, found_last, kept_attention_last, after=[mlp_total]
    )
    results, last_parts = beside(results, met(tie(last_parts, pieces[1])))
    parts, branch, grad_raw, head_gains = results
    last = middle_last
    for value in last_parts:
        last = last + value.astype(f32)
    last = last.astype(low)
    mlp_rows = met(mlp_rows)
    parts = met(parts)
    attention_grads = weight_grads(
        kept_attention_last[0], grad_raw, kept_attention_last[4], branch
    )
    mlp_operand = laid_out(mlp_total, mlp_rows)
    mlp_last = scattered(mlp_operand)
    grad, sent, gain = add_back(
        parts, grad, hidden_last, found_last[0], True, after=[attention_grads[1], mlp_operand]
    )
    gains = (gain, mlp_gain, *head_gains)
    down_grad_last = None if aligned else rows_fallback(mlp_rows)

    swapped = swap(attention_grads[1]), swap(attention_grads[3])
    pieces = hops(sent)
    attention_total, attention_rows = meet(attention_grads, swapped)
    results = mlp_backward(
        pieces, lift_first, down_first, kept_mlp_first, after=[attention_total]
    )
    results, last = beside(results, hops(tie(last, pieces[1])))
    parts, branch, both = results
    last = dealt(last)
    attention_rows = met(attention_rows)
    gains = met_gains(gains)
    parts = met(parts)
    attention_operand = laid_out(attention_total, attention_rows, gains)
    mlp_grads = weight_grads(kept_mlp_first[0], both, kept_mlp_first[3], branch)
    attention_last = scattered(attention_operand)
    out_grad_last = None if aligned else rows_fallback(attention_rows)
    grad, sent, mlp_gain = add_back(
        parts,
        grad,
        middle_first,
        found_first[1],
        False,
        after=[mlp_grads[1], attention_operand, mlp_last],
    )
    swapped = swap(mlp_grads[1]), swap(mlp_grads[3])
    pieces = hops(sent)
    mlp_total, mlp_rows = meet(mlp_grads, swapped)
    results = attention_backward(
        pieces, qkv_first, out_first, found_first, kept_attention_first, after=[mlp_total]
    )
    results, mlp_last = beside(results, hops(tie(mlp_last, pieces[1])))
    parts, branch, grad_raw, head_gains = results
    mlp_rows = met(mlp_rows)
    parts = met(parts)
    mlp_operand = laid_out(mlp_total, mlp_rows)
    attention_grads = weight_grads(
        kept_attention_first[0], grad_raw, kept_attention_first[4], branch
    )
    mlp_first = scattered(mlp_operand)
    swapped = swap(attention_grads[1]), swap(attention_grads[3])
    attention_total, attention_rows = meet(attention_grads, swapped)
    attention_rows = met(attention_rows)
    down_grad_first = None if aligned else rows_fallback(mlp_rows)
    grad, sent, gain = add_back(
        parts, grad, entering, found_first[0], True, after=[attention_grads[1], mlp_operand]
    )
    gains = met_gains((gain, mlp_gain, *head_gains))
    attention_operand = laid_out(attention_total, attention_rows, gains)
    attention_first = scattered(attention_operand)
    out_grad_first = None if aligned else rows_fallback(attention_rows)
    attention_last = hops(tie(attention_last, sent))
    mlp_first = hops(tie(mlp_first, attention_last[1]))
    grad = dealt(hops(tie(sent, mlp_first[1])))
    mlp_last, attention_last = returned(mlp_last, 1), returned(attention_last, 1)
    mlp_first = returned(mlp_first, 0)

    def settle(kernel, from_first, from_last, outputs):
        size = from_first[0].shape[1]

        def block_of(layer):
            def at(i, where):
                return jnp.where(where[1] == layer, i ^ where[0], 0), 0, 0

            return pl.BlockSpec((1, size, LANES), at)

        return pl.pallas_call(
            kernel,
            grid_spec=pltpu.PrefetchScalarGridSpec(
                num_scalar_prefetch=1,
                grid=(count,),
                in_specs=[block_of(0), block_of(0), block_of(1), block_of(1)],
                out_specs=[
                    pl.BlockSpec(block, functools.partial(lambda at, i, where: at(i), at))
                    for _, block, at in outputs
                ],
            ),
            out_shape=[jax.ShapeDtypeStruct(shape, f32) for shape, _, _ in outputs],
            compiler_params=pltpu.CompilerParams(vmem_limit_bytes=VMEM_LIMIT),
            cost_estimate=pl.CostEstimate(
                flops=0, bytes_accessed=12 * count * size * LANES, transcendentals=0
            ),
        )(where, *from_first, *from_last)

    def halves_of(where, blocks, body):
        @pl.when(where[1] == 0)
        def _():
            body(0, blocks[0])
            body(1, blocks[1])

        @pl.when(where[1] == 1)
        def _():
            body(1, blocks[2])
            body(0, blocks[3])

    def place_rows(block, at, half, out):
        share = out.shape[1]
        for j in range(chunks):
            out[half, :, span(j, LANES)] = block[0, at + j * share : at + (j + 1) * share, :].astype(f32)

    def mlp_settle_kernel(where, *refs):
        blocks, (gate, up, *down) = refs[:4], refs[4:]

        def body(half, block):
            both = [block[0, span(j, part), :].astype(f32) for j in range(2 * hidden_half // LANES)]
            both = jnp.concatenate(both, axis=1)
            gate[:, span(half, hidden_half)] = both[:, :hidden_half]
            up[:, span(half, hidden_half)] = both[:, hidden_half:]
            if aligned:
                place_rows(block, lift_rows, half, down[0])

        halves_of(where, blocks, body)

    def attention_settle_kernel(where, *refs):
        blocks, (query, key, value, sums, *out) = refs[:4], refs[4:]

        @pl.when(pl.program_id(0) == 0)
        def _():
            sums[...] = jnp.zeros_like(sums)

        def body(half, block):
            query[:, span(half, query_half)] = block[0, :part, :].astype(f32)
            both = block[0, part + GAIN_ROWS : qkv_rows, :].astype(f32)
            key[:, span(half, key_half)] = both[:, :key_half]
            value[:, span(half, key_half)] = both[:, key_half:]
            if half == 0:
                sums[...] += block[0, part : part + GAIN_ROWS, :].astype(f32)
            if aligned:
                place_rows(block, qkv_rows, half, out[0])

        halves_of(where, blocks, body)

    def column_output(size):
        return ((part, 2 * count * size), (part, 2 * size), lambda i: (0, i))

    def row_output(size):
        return ((2, size, width), (2, size // count, width), lambda i: (0, i, 0))

    outputs = [column_output(hidden_half)] * 2 + ([row_output(hidden_half)] if aligned else [])
    grad_gate, grad_up, *grad_down = settle(
        mlp_settle_kernel, mlp_first, mlp_last, outputs
    )
    attention_first = returned(hops(tie(attention_first, grad_gate)), 0)
    outputs = [column_output(query_half)] + [column_output(key_half)] * 2
    outputs += [((GAIN_ROWS, LANES), (GAIN_ROWS, LANES), lambda i: (0, 0))]
    outputs += [row_output(query_half)] if aligned else []
    grad_query, grad_key, grad_value, sums, *grad_out = settle(
        attention_settle_kernel, attention_first, attention_last, outputs
    )
    if aligned:
        grad_out, grad_down = grad_out[0].reshape(-1, width), grad_down[0].reshape(-1, width)
    else:
        pair = []
        for one, two in ((out_grad_first, out_grad_last), (down_grad_first, down_grad_last)):
            own = jnp.where(first, one, two).astype(f32)
            pair.append(own + swap(jnp.where(first, two, one)).astype(f32))
        grad_out, grad_down = pair
    sums = sums.reshape(1, -1)
    split, at = [], 0
    for size in sizes:
        split.append(sums[:, at : at + size])
        at += size

    own = jnp.where(first, grad, last)
    other = swap(jnp.where(first, last, grad))
    boundary = jnp.where(first, jnp.stack([own, other]), jnp.stack([other, own]))
    return (
        boundary[None, None],
        split[0],
        grad_query[None],
        grad_key[None],
        grad_value[None],
        split[2],
        split[3],
        grad_out[None],
        split[1],
        grad_gate[None],
        grad_up[None],
        grad_down[None],
    )


def solution(mesh):
    weight, gain, row = P("section", "fsdp", None), P("section", "fsdp"), P("fsdp", None, None)
    stream = P("section", "fsdp", None, "ctx", None)
    masters = (gain, weight, weight, weight, gain, gain, weight, gain, weight, weight, weight)
    return jax.shard_map(
        shards,
        mesh=mesh,
        in_specs=(stream, row, row) + masters,
        out_specs=(stream,) + masters,
        check_vma=False,
    )
```

time: 860 us -> 646 us (0.75)
  waiting for transfers between devices: 452 us -> 229 us
  Pallas kernels: 0 us -> 199 us
  local copies, waits for them, and re-layouts: 114 us -> 40.5 us
  matrix products: 73.8 us -> 1.81 us
  starting transfers between devices: 79.5 us -> 129 us
  other arithmetic: 69.8 us -> 21.3 us
  blocking collectives: 42.1 us -> 0 us
    all_gather x12 -> x3, waiting for transfers between devices: 216 us -> 4.92 us  [gathered(): return lax.all_gather(block, 'fsdp', axis=0, tiled=False)]
    pallas_call x0 -> x35, Pallas kernels: none -> 199 us  [the longest x31 179 us: call(): pl.pallas_call(body, out_shape=shapes, in_specs=[anywhere] * skipped + [s...]
    reduce_scatter x6 -> x4, waiting for transfers between devices: 85.7 us -> 0.01 us  [scattered(): return lax.psum_scatter(operand, 'fsdp', scatter_dimension=0, tiled=False)]
    ppermute x54 -> x90, waiting for transfers between devices: 130 us -> 188 us  [hop(): return lax.ppermute(value, 'ctx', [(i, i ^ step) for i in range(count)])]
    ppermute x54 -> x90, starting transfers between devices: 64.4 us -> 111 us  [hop(): return lax.ppermute(value, 'ctx', [(i, i ^ step) for i in range(count)])]
    all_to_all x2 -> x0, blocking collectives: 42.1 us -> none  [reduced(): total = lax.all_to_all(total, 'ctx', 0, 0, tiled=True)]
    dot_general x24 -> x0, matrix products: 41.5 us -> none  [the longest x8 18.8 us: dot_rows(): lax.dot_general(left, right, (((0,), (0,)), ((), ())), preferred_element_...]
    slice x36 -> x6, local copies, waits for them, and re-layouts: 36.7 us -> 4.7 us  [the longest x2 2.43 us: shards(): own[:, lift_rows:]]
  transfers between devices with their start and end apart: 98 -> 126, of which waited for: 61 -> 56; matrix products, arithmetic and copies ran while one was open for 23% -> 6% of each run, Pallas kernels for 0% -> 27%
where the time goes in v2:
time: 646 us; the launch traced here: 637 us
  waiting for transfers between devices  229 us (35%)
  Pallas kernels  199 us (31%)
  starting transfers between devices  129 us (20%)
  local copies, waits for them, and re-layouts  40.5 us (6%)
  other arithmetic  21.3 us (3%)
  between operations  15.8 us (2%)
    ppermute x90, waiting for transfers between devices, hop(): return lax.ppermute(value, 'ctx', [(i, i ^ step) for i in range(count)])  188 us
    pallas_call x31, Pallas kernels, call(): pl.pallas_call(body, out_shape=shapes, in_specs=[anywhere] * skipped + [s...  179 us
    ppermute x90, starting transfers between devices, hop(): return lax.ppermute(value, 'ctx', [(i, i ^ step) for i in range(count)])  111 us
    unnamed x231, local copies, waits for them, and re-layouts  27.8 us
    ppermute x3, waiting for transfers between devices, gathered_direct(): lax.ppermute(block, 'fsdp', [(i, i ^ k) for i in range(depth)])  27.8 us
    pallas_call x2, Pallas kernels, settle(): pl.pallas_call(kernel, grid_spec=pltpu.PrefetchScalarGridSpec(num_scalar_...  13.5 us
  transfers between devices with their start and end apart: 126, of which 56 were waited for; matrix products, arithmetic and copies ran while one was open for 6% of the time, Pallas kernels for 27%

profile of v2, /device:TPU:0, one launch (start us, length us, event | category | flops | bytes accessed | tf_op | source)
XLA Modules:
  0.0 636.8 jit_solution(4755171739749910846)
XLA Ops:
  37.9 22.8 %collective-permute-done.6 = bf16[784,256]{1,0:T(8,128)(2,1)S(1)} collective-permute-done((bf16[784,256]{1,0:T(8,128)(2,1)S(1)}, bf16[784,256]{1,0:T(8,128)(2,1)S(1)}, u32[]{:S(2)}, u32[]{:S(2)}) %collective-permute-start.6) | collective-permute-done | bytes 401440 | tf_op jit(solution)/shard_map/ppermute | solution.py:509
  63.6 5.8 collective-permute-done.4.refs_3_
  84.2 12.3 %shard_map.230 = (bf16[512,1024]{1,0:T(8,128)(2,1)}, f32[512,1024]{1,0:T(8,128)}, bf16[512,512]{1,0:T(8,128)(2,1)}, bf16[512,256]{1,0:T(8,128)(2,1)}, bf16[512,512]{1,0:T(8,128)(2,1)}, /*index=5*/f32[512,4]{1,0:T(8,128)}) custom-call(bf16[128,1024]{1,0:T(8,128)(2,1)} %copy-done.20, bf16[128,1024]{1,0:T(8,128)(2,1)} %copy-done.49, ...), custom_call_target="tpu_custom_call" | custom-call | flops 13799999488 | bytes 9260032 | tf_op jit(solution)/shard_map/pallas_call | solution.py:118
  105.2 5.3 collective-permute-done.13.refs_1_
  110.5 6.3 collective-permute-done.14.refs_2_
  148.6 6.5 %shard_map.234 = (bf16[512,1024]{1,0:T(8,128)(2,1)}, f32[512,768]{1,0:T(8,128)}, f32[512,768]{1,0:T(8,128)}, bf16[512,768]{1,0:T(8,128)(2,1)}) custom-call(bf16[128,1024]{1,0:T(8,128)(2,1)} %get-tuple-element.227.refs_0_, bf16[128,1024]{1,0:T(8,128)(2,1)} %copy-done.82, bf16[128,1024]{1,0:T(8,128)(2,1)} %copy-done.86, bf16[128,1024]{1,0:T(8,128)(2,1)} %copy-done.90, ...), custom_call_target="tpu_custom_call" | custom-call | flops 6899999744 | bytes 10747904 | tf_op jit(solution)/shard_map/pallas_call | solution.py:118
  178.8 6.3 collective-permute-done.30.refs_2_
  203.9 12.0 %shard_map.237 = (bf16[512,1024]{1,0:T(8,128)(2,1)}, f32[512,1024]{1,0:T(8,128)}, bf16[512,512]{1,0:T(8,128)(2,1)}, bf16[512,256]{1,0:T(8,128)(2,1)}, bf16[512,512]{1,0:T(8,128)(2,1)}, /*index=5*/f32[512,4]{1,0:T(8,128)}) custom-call(bf16[4,256,256]{2,1,0:T(8,128)(2,1)} %copy-done.39, bf16[128,1024]{1,0:T(8,128)(2,1)} %get-tuple-element.244.refs_1_, ...), custom_call_target="tpu_custom_call" | custom-call | flops 13799999488 | bytes 9255936 | tf_op jit(solution)/shard_map/pallas_call | solution.py:118
  263.3 6.4 %shard_map.240 = (bf16[512,1024]{1,0:T(8,128)(2,1)}, f32[512,768]{1,0:T(8,128)}, f32[512,768]{1,0:T(8,128)}, bf16[512,768]{1,0:T(8,128)(2,1)}) custom-call(bf16[128,1024]{1,0:T(8,128)(2,1)} %get-tuple-element.252.refs_0_, bf16[128,1024]{1,0:T(8,128)(2,1)} %copy-done.69, bf16[128,1024]{1,0:T(8,128)(2,1)} %copy-done.76, bf16[128,1024]{1,0:T(8,128)(2,1)} %copy-done.83, ...), custom_call_target="tpu_custom_call" | custom-call | flops 6899999744 | bytes 10747904 | tf_op jit(solution)/shard_map/pallas_call | solution.py:118
  276.2 8.9 %shard_map.242 = (bf16[128,1024]{1,0:T(8,128)(2,1)}, bf16[128,1024]{1,0:T(8,128)(2,1)}, bf16[128,1024]{1,0:T(8,128)(2,1)}, bf16[128,1024]{1,0:T(8,128)(2,1)}, bf...) custom-call(bf16[128,1024]{1,0:T(8,128)(2,1)} %get-tuple-element.418.refs_0_.refs_5_, bf16[128,1024]{1,0:T(8,128)(2,1)} %copy-done.73, ...), custom_call_target="tpu_custom_call" | custom-call | flops 10350000128 | bytes 14155776 | tf_op jit(solution)/shard_map/pallas_call | solution.py:118
  285.1 6.5 %shard_map.243 = (f32[4,768,256]{2,1,0:T(8,128)}, bf16[4,768,256]{2,1,0:T(8,128)(2,1)}, f32[4,384,256]{2,1,0:T(8,128)}, bf16[4,384,256]{2,1,0:T(8,128)(2,1)}) custom-call(bf16[512,1024]{1,0:T(8,128)(2,1)} %get-tuple-element.258.refs_0_, bf16[512,1536]{1,0:T(8,128)(2,1)} %get-tuple-element.265.refs_1_, bf16[512,768]{1,0:T(8,128)(2,1)} %get-tuple-element.259.refs_1_.refs_2_, ...), custom_call_target="tpu_custom_call" | custom-call | flops 6899999744 | bytes 11534336 | tf_op jit(solution)/shard_map/pallas_call | solution.py:118
  328.2 18.6 %shard_map.246 = (bf16[128,1024]{1,0:T(8,128)(2,1)}, bf16[128,1024]{1,0:T(8,128)(2,1)}, bf16[128,1024]{1,0:T(8,128)(2,1)}, bf16[128,1024]{1,0:T(8,128)(2,1)}, bf...) custom-call(bf16[4,768,256]{2,1,0:T(8,128)(2,1)} %get-tuple-element.271.refs_0_.refs_1, ...), custom_call_target="tpu_custom_call" | custom-call | flops 20700000256 | bytes 11878400 | tf_op jit(solution)/shard_map/pallas_call | solution.py:118
  387.2 7.5 %collective-permute-done.79.refs_5_ = bf16[256,256]{1,0:T(8,128)(2,1)S(1)} collective-permute-done((bf16[256,256]{1,0:T(8,128)(2,1)}, bf16[256,256]{1,0:T(8,128)(2,1)S(1)}, u32[]{:S(2)}, u32[]{:S(2)}) %collective-permute-start.79) | collective-permute-done | bytes 131104 | tf_op jit(solution)/shard_map/ppermute | solution.py:28
  400.6 9.2 %shard_map.251 = (bf16[128,1024]{1,0:T(8,128)(2,1)}, bf16[128,1024]{1,0:T(8,128)(2,1)}, bf16[128,1024]{1,0:T(8,128)(2,1)}, bf16[128,1024]{1,0:T(8,128)(2,1)}, bf...) custom-call(bf16[4,512,256]{2,1,0:T(8,128)(2,1)} %get-tuple-element.305.refs_0_.refs_1_, ...), custom_call_target="tpu_custom_call" | custom-call | flops 10350000128 | bytes 14155776 | tf_op jit(solution)/shard_map/pallas_call | solution.py:118
  409.8 6.8 %shard_map.252 = (f32[4,768,256]{2,1,0:T(8,128)}, bf16[4,768,256]{2,1,0:T(8,128)(2,1)}, f32[4,384,256]{2,1,0:T(8,128)}, bf16[4,384,256]{2,1,0:T(8,128)(2,1)}) custom-call(bf16[512,1024]{1,0:T(8,128)(2,1)} %get-tuple-element.234.refs_0_, bf16[512,1536]{1,0:T(8,128)(2,1)} %get-tuple-element.330.refs_1_, bf16[512,768]{1,0:T(8,128)(2,1)} %get-tuple-element.235.refs_1_.refs_2_, ...), custom_call_target="tpu_custom_call" | custom-call | flops 6899999744 | bytes 11534336 | tf_op jit(solution)/shard_map/pallas_call | solution.py:118
  458.7 6.0 collective-permute-done.84.refs_2_
  471.1 18.4 %shard_map.256 = (bf16[128,1024]{1,0:T(8,128)(2,1)}, bf16[128,1024]{1,0:T(8,128)(2,1)}, bf16[128,1024]{1,0:T(8,128)(2,1)}, bf16[128,1024]{1,0:T(8,128)(2,1)}, bf...) custom-call(bf16[4,768,256]{2,1,0:T(8,128)(2,1)} %get-tuple-element.336.refs_0_.refs_1, ...), custom_call_target="tpu_custom_call" | custom-call | flops 20700000256 | bytes 11878400 | tf_op jit(solution)/shard_map/pallas_call | solution.py:118
  508.6 6.3 collective-permute-done.94.refs_4_
  539.3 8.1 %collective-permute-done.97 = bf16[1152,256]{1,0:T(8,128)(2,1)S(1)} collective-permute-done((bf16[1152,256]{1,0:T(8,128)(2,1)}, bf16[1152,256]{1,0:T(8,128)(2,1)S(1)}, u32[]{:S(2)}, u32[]{:S(2)}) %collective-permute-start.97) | collective-permute-done | bytes 589856 | tf_op jit(solution)/shard_map/ppermute | solution.py:28
  547.4 12.2 %collective-permute-done.109 = bf16[1152,256]{1,0:T(8,128)(2,1)S(1)} collective-permute-done((bf16[1152,256]{1,0:T(8,128)(2,1)}, bf16[1152,256]{1,0:T(8,128)(2,1)S(1)}, u32[]{:S(2)}, u32[]{:S(2)}) %collective-permute-start.109) | collective-permute-done | bytes 589856 | tf_op jit(solution)/shard_map/ppermute | solution.py:28
  567.7 7.5 %shard_map.262 = (f32[256,3072]{1,0:T(8,128)}, f32[256,3072]{1,0:T(8,128)}, f32[2,384,1024]{2,1,0:T(8,128)}) custom-call(s32[2]{0:T(128)} %pad_add_fusion.where, bf16[4,1152,256]{2,1,0:T(8,128)(2,1)} %copy-done.1, bf16[4,1152,256]{2,1,0:T(8,128)(2,1)} %collective-permute-done.110.refs_1_, bf16[4,1152,256]{2,1,0:T(8,128)(2,1)} %copy-done, ...), custom_call_target="tpu_custom_call" | custom-call | bytes 14155776 | tf_op jit(solution)/shard_map/pallas_call | solution.py:801
  578.8 13.9 %collective-permute-done.116 = bf16[784,256]{1,0:T(8,128)(2,1)S(1)} collective-permute-done((bf16[784,256]{1,0:T(8,128)(2,1)S(1)}, bf16[784,256]{1,0:T(8,128)(2,1)S(1)}, u32[]{:S(2)}, u32[]{:S(2)}) %collective-permute-start.116) | collective-permute-done | bytes 401440 | tf_op jit(solution)/shard_map/ppermute | solution.py:28
  612.0 6.7 %collective-permute-done.99 = bf16[128,1024]{1,0:T(8,128)(2,1)S(1)} collective-permute-done((bf16[128,1024]{1,0:T(8,128)(2,1)}, bf16[128,1024]{1,0:T(8,128)(2,1)S(1)}, u32[]{:S(2)}, u32[]{:S(2)}) %collective-permute-start.99) | collective-permute-done | bytes 262176 | tf_op jit(solution)/shard_map/ppermute | solution.py:28
  621.5 6.0 shard_map.263
  (579 shorter events, 394.7 us)
Async XLA Ops:
  7.2 114.2 %all-gather.7.cloned.1.call-start = ((), (), s32[]{:S(2)}) async-start(), calls=%async_computation.8 | async-start | bytes 2949120 | tf_op jit(solution)/shard_map/all_gather | solution.py:504
  19.7 49.7 %collective-permute-start.19 = (bf16[1152,256]{1,0:T(8,128)(2,1)S(1)}, bf16[1152,256]{1,0:T(8,128)(2,1)S(1)}, u32[]{:S(2)}, u32[]{:S(2)}) collective-permute-start(bf16[1152,256]{1,0:T(8,128)(2,1)S(1)} %slice_bitcast_fusion), channel_id=1, source_target_pairs={{0,16},{16,0},{1,17},{17,1},{2,18},{18,2},{3,19},{19,3},{4,20},{20... | collective-permute-start | bytes 1769480 | tf_op jit(solution)/shard_map/ppermute | solution.py:23
  25.9 34.8 %collective-permute-start.6 = (bf16[784,256]{1,0:T(8,128)(2,1)S(1)}, bf16[784,256]{1,0:T(8,128)(2,1)S(1)}, u32[]{:S(2)}, u32[]{:S(2)}) collective-permute-start(bf16[784,256]{1,0:T(8,128)(2,1)S(1)} %get-tuple-element.416), channel_id=1, source_target_pairs={{0,2},{1,3},{2,0},{3,1},{4,6},{5,7},{6,4},{7,5},{8,10},{9,11},{10,... | collective-permute-start | bytes 1204232 | tf_op jit(solution)/shard_map/ppermute | solution.py:509
  26.0 37.2 %collective-permute-start.7 = (bf16[784,256]{1,0:T(8,128)(2,1)S(1)}, bf16[784,256]{1,0:T(8,128)(2,1)S(1)}, u32[]{:S(2)}, u32[]{:S(2)}) collective-permute-start(bf16[784,256]{1,0:T(8,128)(2,1)S(1)} %get-tuple-element.416), channel_id=1, source_target_pairs={{0,1},{1,0},{2,3},{3,2},{4,5},{5,4},{6,7},{7,6},{8,9},{9,8},{10,11... | collective-permute-start | bytes 1204232 | tf_op jit(solution)/shard_map/ppermute | solution.py:509
  29.6 34.0 %collective-permute-start.2 = (bf16[128,1024]{1,0:T(8,128)(2,1)S(1)}, bf16[128,1024]{1,0:T(8,128)(2,1)S(1)}, u32[]{:S(2)}, u32[]{:S(2)}) collective-permute-start(bf16[128,1024]{1,0:T(8,128)(2,1)S(1)} %get-tuple-element.211.refs_0_.refs_4_.refs_7_), channel_id=1, source_target_pairs={{0,4},{4,0},{8,12},{12,8},{1,5},{5,1},{9,13},{13,9},{2,6},{6,2},{1... | collective-permute-start | bytes 786440 | tf_op jit(solution)/shard_map/ppermute | solution.py:28
  36.2 27.3 %collective-permute-start.3 = (bf16[128,1024]{1,0:T(8,128)(2,1)S(1)}, bf16[128,1024]{1,0:T(8,128)(2,1)S(1)}, u32[]{:S(2)}, u32[]{:S(2)}) collective-permute-start(bf16[128,1024]{1,0:T(8,128)(2,1)S(1)} %get-tuple-element.211.refs_0_.refs_4_.refs_7_), channel_id=1, source_target_pairs={{0,8},{4,12},{8,0},{12,4},{1,9},{5,13},{9,1},{13,5},{2,10},{6,14},... | collective-permute-start | bytes 786440 | tf_op jit(solution)/shard_map/ppermute | solution.py:28
  70.5 88.9 %all-gather.9.cloned.1.call-start = ((), (), s32[]{:S(2)}) async-start(), calls=%async_computation.9 | async-start | bytes 2007040 | tf_op jit(solution)/shard_map/all_gather | solution.py:504
  121.4 113.3 %all-gather.11.cloned.1.call-start = ((), (), s32[]{:S(2)}) async-start(), calls=%async_computation.10 | async-start | bytes 2949120 | tf_op jit(solution)/shard_map/all_gather | solution.py:504
  159.5 42.5 %collective-permute-start.35 = (bf16[4,784,256]{2,1,0:T(8,128)(2,1)}, bf16[4,784,256]{2,1,0:T(8,128)(2,1)S(1)}, u32[]{:S(2)}, u32[]{:S(2)}) collective-permute-start(bf16[4,784,256]{2,1,0:T(8,128)(2,1)} %bitcast.186), channel_id=1, source_target_pairs={{0,16},{16,0},{1,17},{17,1},{2,18},{18,2},{3,19},{19,3},{4,20},{20... | collective-permute-start | bytes 4816904 | tf_op jit(solution)/shard_map/ppermute | solution.py:23
  159.5 292.2 %reduce-scatter.5.cloned.1.call-start = ((), (), s32[]{:S(2)}) async-start(), calls=%async_computation.4 | async-start | bytes 2949120 | tf_op jit(solution)/shard_map/reduce_scatter | solution.py:682
  173.8 28.2 %collective-permute-start.28 = (bf16[4,256,256]{2,1,0:T(8,128)(2,1)S(1)}, bf16[4,256,256]{2,1,0:T(8,128)(2,1)S(1)}, u32[]{:S(2)}, u32[]{:S(2)}) collective-permute-start(bf16[4,256,256]{2,1,0:T(8,128)(2,1)S(1)} %pad_maximum_fusion.8.refs_2_), channel_id=1, source_target_pairs={{0,16},{16,0},{1,17},{17,1},{2,18},{18,2},{3,19},{19,3},{4,20},{20... | collective-permute-start | bytes 1572872 | tf_op jit(solution)/shard_map/ppermute | solution.py:23
  234.8 27.1 %collective-permute-start.42 = (bf16[4,1152,256]{2,1,0:T(8,128)(2,1)}, bf16[4,1152,256]{2,1,0:T(8,128)(2,1)S(1)}, u32[]{:S(2)}, u32[]{:S(2)}) collective-permute-start(bf16[4,1152,256]{2,1,0:T(8,128)(2,1)} %bitcast.175), channel_id=1, source_target_pairs={{0,16},{16,0},{1,17},{17,1},{2,18},{18,2},{3,19},{19,3},{4,20},{20... | collective-permute-start | bytes 7077896 | tf_op jit(solution)/shard_map/ppermute | solution.py:23
  320.1 197.6 %reduce-scatter.9.cloned.1.call-start = ((), (), s32[]{:S(2)}) async-start(), calls=%async_computation.6 | async-start | bytes 2007040 | tf_op jit(solution)/shard_map/reduce_scatter | solution.py:682
  321.0 25.7 %collective-permute-start.58 = (bf16[128,1024]{1,0:T(8,128)(2,1)S(1)}, bf16[128,1024]{1,0:T(8,128)(2,1)S(1)}, u32[]{:S(2)}, u32[]{:S(2)}) collective-permute-start(bf16[128,1024]{1,0:T(8,128)(2,1)S(1)} %copy-done.48), channel_id=1, source_target_pairs={{0,4},{4,0},{8,12},{12,8},{1,5},{5,1},{9,13},{13,9},{2,6},{6,2},{1... | collective-permute-start | bytes 786440 | tf_op jit(solution)/shard_map/ppermute | solution.py:28
  372.5 27.3 %collective-permute-start.70 = (bf16[128,1024]{1,0:T(8,128)(2,1)}, bf16[128,1024]{1,0:T(8,128)(2,1)S(1)}, u32[]{:S(2)}, u32[]{:S(2)}) collective-permute-start(bf16[128,1024]{1,0:T(8,128)(2,1)} %get-tuple-element.315.refs_1_), channel_id=1, source_target_pairs={{0,8},{4,12},{8,0},{12,4},{1,9},{5,13},{9,1},{13,5},{2,10},{6,14},... | collective-permute-start | bytes 786440 | tf_op jit(solution)/shard_map/ppermute | solution.py:28
  399.5 129.6 %reduce-scatter.7.cloned.1.call-start = ((), (), s32[]{:S(2)}) async-start(), calls=%async_computation.5 | async-start | bytes 2949120 | tf_op jit(solution)/shard_map/reduce_scatter | solution.py:682
  445.2 130.1 %reduce-scatter.11.cloned.1.call-start = ((), (), s32[]{:S(2)}) async-start(), calls=%async_computation.7 | async-start | bytes 2007040 | tf_op jit(solution)/shard_map/reduce_scatter | solution.py:682
  465.3 28.9 %collective-permute-start.88 = (bf16[1152,256]{1,0:T(8,128)(2,1)S(1)}, bf16[1152,256]{1,0:T(8,128)(2,1)S(1)}, u32[]{:S(2)}, u32[]{:S(2)}) collective-permute-start(bf16[1152,256]{1,0:T(8,128)(2,1)S(1)} %bitcast.149), channel_id=1, source_target_pairs={{0,8},{4,12},{8,0},{12,4},{1,9},{5,13},{9,1},{13,5},{2,10},{6,14},... | collective-permute-start | bytes 1769480 | tf_op jit(solution)/shard_map/ppermute | solution.py:28
  467.0 27.2 %collective-permute-start.89 = (bf16[1152,256]{1,0:T(8,128)(2,1)S(1)}, bf16[1152,256]{1,0:T(8,128)(2,1)S(1)}, u32[]{:S(2)}, u32[]{:S(2)}) collective-permute-start(bf16[1152,256]{1,0:T(8,128)(2,1)S(1)} %bitcast.150), channel_id=1, source_target_pairs={{0,12},{4,8},{8,4},{12,0},{1,13},{5,9},{9,5},{13,1},{2,14},{6,10},... | collective-permute-start | bytes 1769480 | tf_op jit(solution)/shard_map/ppermute | solution.py:28
  530.5 29.0 %collective-permute-start.109 = (bf16[1152,256]{1,0:T(8,128)(2,1)}, bf16[1152,256]{1,0:T(8,128)(2,1)S(1)}, u32[]{:S(2)}, u32[]{:S(2)}) collective-permute-start(bf16[1152,256]{1,0:T(8,128)(2,1)} %bitcast.152), channel_id=1, source_target_pairs={{0,12},{4,8},{8,4},{12,0},{1,13},{5,9},{9,5},{13,1},{2,14},{6,10},... | collective-permute-start | bytes 1769480 | tf_op jit(solution)/shard_map/ppermute | solution.py:28
  532.0 27.5 %collective-permute-start.108 = (bf16[1152,256]{1,0:T(8,128)(2,1)}, bf16[1152,256]{1,0:T(8,128)(2,1)}, u32[]{:S(2)}, u32[]{:S(2)}) collective-permute-start(bf16[1152,256]{1,0:T(8,128)(2,1)} %bitcast.153), channel_id=1, source_target_pairs={{0,8},{4,12},{8,0},{12,4},{1,9},{5,13},{9,1},{13,5},{2,10},{6,14},... | collective-permute-start | bytes 1769480 | tf_op jit(solution)/shard_map/ppermute | solution.py:28
  537.8 27.6 %collective-permute-start.111 = (bf16[4,1152,256]{2,1,0:T(8,128)(2,1)S(1)}, bf16[4,1152,256]{2,1,0:T(8,128)(2,1)S(1)}, u32[]{:S(2)}, u32[]{:S(2)}) collective-permute-start(bf16[4,1152,256]{2,1,0:T(8,128)(2,1)S(1)} %pad_maximum_fusion.1.refs_2_), channel_id=1, source_target_pairs={{0,16},{1,17},{2,18},{3,19},{4,20},{5,21},{6,22},{7,23},{8,24},{9,... | collective-permute-start | bytes 7077896 | tf_op jit(solution)/shard_map/ppermute | solution.py:702
  563.8 28.8 %collective-permute-start.116 = (bf16[784,256]{1,0:T(8,128)(2,1)S(1)}, bf16[784,256]{1,0:T(8,128)(2,1)S(1)}, u32[]{:S(2)}, u32[]{:S(2)}) collective-permute-start(bf16[784,256]{1,0:T(8,128)(2,1)S(1)} %bitcast.161), channel_id=1, source_target_pairs={{0,8},{4,12},{8,0},{12,4},{1,9},{5,13},{9,1},{13,5},{2,10},{6,14},... | collective-permute-start | bytes 1204232 | tf_op jit(solution)/shard_map/ppermute | solution.py:28
  592.9 28.6 %collective-permute-start.118 = (bf16[4,784,256]{2,1,0:T(8,128)(2,1)S(1)}, bf16[4,784,256]{2,1,0:T(8,128)(2,1)}, u32[]{:S(2)}, u32[]{:S(2)}) collective-permute-start(bf16[4,784,256]{2,1,0:T(8,128)(2,1)S(1)} %pad_maximum_fusion.4.refs_2_), channel_id=1, source_target_pairs={{0,16},{1,17},{2,18},{3,19},{4,20},{5,21},{6,22},{7,23},{8,24},{9,... | collective-permute-start | bytes 4816904 | tf_op jit(solution)/shard_map/ppermute | solution.py:702
  (212 other events, 2043.4 us)
Sparse Core Ops, SparseCore 0:
  70.7 50.7 all-gather.6
  123.0 36.4 all-gather.8
  161.6 49.3 all-gather.10
  320.2 45.8 reduce-scatter.4
  399.6 34.0 reduce-scatter.8
  445.3 46.1 reduce-scatter.6
  537.6 34.2 reduce-scatter.10

commit v3 on v2

--- a/solution.py
+++ b/solution.py
@@ -11,6 +11,7 @@
 GAIN_ROWS = 16
 LANES = 256
 VMEM_LIMIT = 56 * 1024 * 1024
+VMEM_SLACK = 6 * 1024 * 1024
 FLOPS_PER_US = 1.15e9
 SCALE = HEAD_DIM ** (-0.5)
 epsilon = 1e-06
@@ -32,6 +33,15 @@
     return [own] + [hop(own, k) for k in range(1, lax.axis_size("ctx"))]
 
 
+def hops_split(own):
+    if lax.axis_size("ctx") != 4:
+        return hops(own)
+    one, two = own[: own.shape[0] // 2], own[own.shape[0] // 2 :]
+    one_near, two_near = hop(one, 1), hop(two, 2)
+    near = jnp.concatenate([one_near, hop(two, 1)]), jnp.concatenate([hop(one, 2), two_near])
+    return [own, *near, jnp.concatenate([hop(one_near, 2), hop(two_near, 1)])]
+
+
 def met(parts):
     return [parts[0]] + [hop(parts[k], k) for k in range(1, len(parts))]
 
@@ -104,13 +114,14 @@
         part[:, block] = value[span(i, rows)].astype(part.dtype)
 
 
-def call(kernel, operands, outputs, took, scratch=(), scalars=(), after=()):
+def call(kernel, operands, outputs, took, scratch=(), scalars=(), after=(), limit=0):
     vmem = pl.BlockSpec(memory_space=pltpu.VMEM)
     smem = pl.BlockSpec(memory_space=pltpu.SMEM)
     anywhere = pl.BlockSpec(memory_space=pl.ANY)
     shapes = [jax.ShapeDtypeStruct(shape, dtype) for shape, dtype in outputs]
     moved = sum(v.size * v.dtype.itemsize for v in [*operands, *shapes])
     skipped, used = len(after), len(scalars)
+    held = moved + sum(jnp.dtype(dtype).itemsize * shape[0] * shape[1] for shape, dtype in scratch)
 
     def body(*refs):
         kernel(*refs[skipped:])
@@ -121,14 +132,14 @@
         in_specs=[anywhere] * skipped + [smem] * used + [vmem] * len(operands),
         out_specs=[vmem] * len(shapes),
         scratch_shapes=[pltpu.VMEM(shape, dtype) for shape, dtype in scratch],
-        compiler_params=pltpu.CompilerParams(vmem_limit_bytes=VMEM_LIMIT),
+        compiler_params=pltpu.CompilerParams(vmem_limit_bytes=limit or held + VMEM_SLACK),
         cost_estimate=pl.CostEstimate(
             flops=int(took * FLOPS_PER_US), bytes_accessed=moved, transcendentals=0
         ),
     )(*after, *scalars, *operands)
 
 
-def add_kernel(count, rounded, *refs):
+def add_kernel(count, rounded, sends_rows, *refs):
     parts, (residual, gain, total, normed) = refs[:count], refs[count:]
     value = residual[...].astype(f32)
     for part in parts:
@@ -136,7 +147,7 @@
     if rounded:
         value = value.astype(low).astype(f32)
     total[...] = value
-    normed[...] = rms_scale(value, gain[...]).astype(low)
+    normed[...] = (value if sends_rows else rms_scale(value, gain[...])).astype(low)
 
 
 def add_back_kernel(count, rounded, *refs):
@@ -154,20 +165,20 @@
 def attention_forward_kernel(count, part, raw_rows, *refs):
     pieces, refs = refs[:count], refs[count:]
     if raw_rows:
-        gain, *refs = refs
+        gain, chosen, *refs = refs
     own_weight, far_weight, cosine, sine, query_gain, key_gain, start, place, place_row, *refs = refs
-    normed, raw, queries, keys, mixed, spread, values = refs
+    normed, raw, queries, keys, mixed, spread, *refs = refs
+    values = refs[-1]
     tokens = normed.shape[0]
     rows = pieces[0].shape[0]
     depth = own_weight.shape[0]
     halves = keys.shape[1] // HEAD_DIM
     group = queries.shape[1] // keys.shape[1]
     step = (group + 2) * HEAD_DIM
+    join(pieces, normed)
     if raw_rows:
-        for i, piece in enumerate(pieces):
-            normed[span(i, rows), :] = rms_scale(piece[...].astype(f32), gain[...]).astype(low)
-    else:
-        join(pieces, normed)
+        refs[0][...] = dot(chosen[:rows, :], normed[...]).astype(low)
+        normed[...] = rms_scale(normed[...].astype(f32), gain[...]).astype(low)
     for half, weight in enumerate((own_weight, far_weight)):
         for j, at in enumerate((0, part + GAIN_ROWS)):
             total = None
@@ -204,32 +215,46 @@
             spread[block, head : head + 1] = top + jnp.log(total)
 
 
-def rows_kernel(count, ordered, *refs):
-    index, left, own, far, *refs = refs
-    parts, whole = refs[:count], refs[count]
+def pick_kernel(first_row, index, own, *out):
+    for k, share in enumerate(out):
+        share[...] = own[index[0] ^ k, first_row:, :]
+
+
+def rows_kernel(count, ordered, dealt, *refs):
+    index, left, *refs = refs
+    if dealt:
+        chosen, *refs = refs
+    given = 1 if ordered else 2 * count
+    shares, parts, whole = refs[:given], refs[given : given + count], refs[given + count]
     if ordered:
-        whole[...] = own[...]
+        whole[...] = shares[0][...]
     else:
         size = whole.shape[0] // 2
         share = size // count
-        for half, value in enumerate((own, far)):
-            for k in range(count):
-                to = half * size + (index[0] ^ k) * share
-                to = pl.ds(pl.multiple_of(to, share), share)
-                for j in range(whole.shape[1] // LANES):
-                    whole[to, span(j, LANES)] = value[k, span(j, share), :]
+        for k, value in enumerate(shares):
+            to = k // count * size + (index[0] ^ (k % count)) * share
+            to = pl.ds(pl.multiple_of(to, share), share)
+            for j in range(whole.shape[1] // LANES):
+                whole[to, span(j, LANES)] = value[span(j, share), :]
 
     @pl.loop(0, whole.shape[1] // LANES)
     def _(j):
         block = chunk(j, LANES)
-        deal_out(parts, block, dot(left[...], whole[:, block]))
-
-
-def lift_kernel(count, part, *refs):
-    pieces, (own_weight, far_weight, normed, gate, lifted, product) = refs[:count], refs[count:]
+        value = dot(left[...], whole[:, block])
+        deal_out(parts, block, dot(chosen[...], value.astype(low)) if dealt else value)
+
+
+def lift_kernel(count, part, raw_rows, *refs):
+    pieces, refs = refs[:count], refs[count:]
+    if raw_rows:
+        gain, chosen, *refs = refs
+    own_weight, far_weight, normed, gate, lifted, product, *refs = refs
     half_size = product.shape[1] // 2
     depth = own_weight.shape[0]
     join(pieces, normed)
+    if raw_rows:
+        refs[0][...] = dot(chosen[: pieces[0].shape[0], :], normed[...]).astype(low)
+        normed[...] = rms_scale(normed[...].astype(f32), gain[...]).astype(low)
     for half, weight in enumerate((own_weight, far_weight)):
         both = []
         for j in range(2 * half_size // LANES):
@@ -271,13 +296,17 @@
         deal_out(parts, span(z, part), total)
 
 
-def attention_backward_kernel(count, part, *refs):
+def attention_backward_kernel(count, part, dealt, *refs):
     pieces, refs = refs[:count], refs[count:]
+    if dealt:
+        chosen, *refs = refs
     own_weight, far_weight, out, *refs = refs
     cosine, sine, query_gain, key_gain, start, place, place_row, *refs = refs
     raw, queries, keys, spread, *refs = refs
     parts, refs = refs[:count], refs[count:]
     branch, grad_raw, grad_query_gain, grad_key_gain, *refs = refs
+    if dealt:
+        dealt_branch, *refs = refs
     grad_mixed, values, grad_queries, grad_keys, grad_values = refs
     tokens, width = branch.shape
     rows = pieces[0].shape[0]
@@ -286,6 +315,8 @@
     group = queries.shape[1] // keys.shape[1]
     step = (group + 2) * HEAD_DIM
     join(pieces, branch)
+    if dealt:
+        dealt_branch[...] = dot(chosen[:rows, :], branch[...]).astype(low)
 
     @pl.loop(0, grad_mixed.shape[1] // LANES)
     def _(j):
@@ -344,6 +375,8 @@
                 grad = grad_raw[:, span(2 * half + j, LANES)]
                 term = dot_cols(grad, weight[z, at : at + part, :])
                 total = term if total is None else total + term
+        if dealt:
+            total = dot(chosen[...], total.astype(low))
         deal_out(parts, span(z, part), total)
 
 
@@ -374,21 +407,16 @@
         row[...] = (own_rows[at] + recv_rows[at].astype(f32)).astype(low)
 
 
-def layout_kernel(part, mid, index, *refs):
-    total, *refs = refs
-    refs = list(refs)
-    gains = refs.pop(0) if mid else None
+def layout_kernel(count, index, total, *refs):
     *rows, out = refs
-    depth = out.shape[0]
-    size = total.shape[1]
-    extra = GAIN_ROWS if mid else 0
-    for z in range(depth):
-        out[z, :part, :] = total[z, :part, :]
-        if mid:
-            out[z, part : part + extra, :] = gains[z]
-        out[z, part + extra : size + extra, :] = total[z, part:, :]
-    for k, row in enumerate(rows):
-        out[index[0] ^ k, size + extra :, :] = row[...]
+    at = total.shape[1]
+    out[:, :at, :] = total[...]
+    while rows:
+        group, rows = rows[:count], rows[count:]
+        size = group[0].shape[0]
+        for k, row in enumerate(group):
+            out[index[0] ^ k, at : at + size, :] = row[...]
+        at += size
 
 
 def shards(
@@ -494,7 +522,11 @@
     weights += [(value_weight, part, key_half, False)]
     weights += [(out_weight, out_share, width, True)] if aligned else []
     size = qkv_rows + (chunks * out_share if aligned else 0)
-    attention_blocks = by_layer(cut(qkv_cut_kernel, weights, [gain_block], size))
+    cuts = cut(qkv_cut_kernel, weights, [gain_block], size)
+    attention_blocks = by_layer(cuts)
+    line = jnp.arange(size, dtype=jnp.int32)[:, None]
+    gain_rows = (line >= part) & (line < part + GAIN_ROWS)
+    attention_blocks = jnp.where(gain_rows, cuts[1], attention_blocks[0]), attention_blocks[1]
     weights = [(gate_weight, part, hidden_half, False), (up_weight, part, hidden_half, False)]
     weights += [(down_weight, down_share, width, True)] if aligned else []
     size = lift_rows + (chunks * down_share if aligned else 0)
@@ -502,12 +534,6 @@
 
     def gathered(block):
         return lax.all_gather(block, "fsdp", axis=0, tiled=False)
-
-    def gathered_direct(block):
-        pieces = [block]
-        for k in range(1, depth):
-            pieces.append(lax.ppermute(block, "fsdp", [(i, i ^ k) for i in range(depth)]))
-        return jnp.stack(xored(pieces, lax.axis_index("fsdp")))
 
     def whole_rows(weight, size):
         full = lax.all_gather(weight[0].astype(low), "fsdp", axis=0, tiled=True)
@@ -518,10 +544,10 @@
         far = [lax.dynamic_slice_in_dim(v, (1 - core) * size, size, 0) for v in layers]
         return [jnp.concatenate(pair, axis=0) for pair in zip(own, far)]
 
-    def shared_rows(value):
-        sent = [lax.dynamic_index_in_dim(value, piece ^ k, 0, keepdims=False) for k in range(count)]
-        own = jnp.stack(met(sent))
-        return own, swap(own)
+    def picked_rows(own, first_row):
+        size = own.shape[1] - first_row
+        kernel = functools.partial(pick_kernel, first_row)
+        return call(kernel, [own], [((size, LANES), low)] * count, 1, scalars=[index])
 
     def split_gains(own):
         found, at = [], 0
@@ -546,6 +572,10 @@
     sine = jnp.concatenate([-sine, sine], axis=-1)
     places = [start[:, None], natural[:, None], natural[None, :]]
 
+    wanted = slots[natural]
+    wanted = ((wanted // rows) ^ piece) * rows + wanted % rows
+    chosen = (wanted[:, None] == order[None, :]).astype(low)
+
     own = lax.dynamic_index_in_dim(stream_in[0, 0], core, 0, keepdims=False)
     other = swap(lax.dynamic_index_in_dim(stream_in[0, 0], 1 - core, 0, keepdims=False))
     entering = jnp.where(first, own, other)
@@ -554,8 +584,8 @@
     wide, half_wide = (rows, width), (tokens, width)
     heads_wide, hidden_wide = 2 * query_half, 2 * hidden_half
 
-    def add(parts, residual, gain, rounded, after=()):
-        kernel = functools.partial(add_kernel, count, rounded)
+    def add(parts, residual, gain, rounded, sends_rows=False, after=()):
+        kernel = functools.partial(add_kernel, count, rounded, sends_rows)
         outputs = [(wide, f32), (wide, low)]
         return call(kernel, [*parts, residual, gain], outputs, 2, after=after)
 
@@ -569,21 +599,27 @@
         outputs = [(half_wide, low), ((tokens, 2 * (query_half + 2 * key_half)), f32)]
         outputs += [((tokens, heads_wide), low), ((tokens, 2 * key_half), low)]
         outputs += [((tokens, heads_wide), low), ((tokens, heads_wide // HEAD_DIM), f32)]
-        operands = [*pieces] + ([found[0]] if raw_rows else [])
+        operands = [*pieces] + ([found[0], chosen] if raw_rows else [])
+        outputs += [(wide, low)] if raw_rows else []
         operands += [*weights, cosine, sine, found[2], found[3], *places]
         return call(kernel, operands, outputs, 12, [((tokens, 2 * key_half), low)], after=after)
 
-    def rows_product(left, shares, after=()):
-        kernel = functools.partial(rows_kernel, count, not aligned)
+    def rows_product(left, shares, dealt=False, after=()):
+        kernel = functools.partial(rows_kernel, count, not aligned, dealt)
         outputs = [(wide, low)] * count + [((left.shape[1], width), low)]
-        *parts, whole = call(kernel, [left, *shares], outputs, 4, scalars=[index], after=after)
+        operands = [left] + ([chosen] if dealt else []) + [*shares]
+        *parts, whole = call(kernel, operands, outputs, 4, scalars=[index], after=after)
         return parts, whole
 
-    def lift_forward(pieces, weights, after=()):
-        kernel = functools.partial(lift_kernel, count, part)
+    def lift_forward(pieces, weights, gain=None, after=()):
+        kernel = functools.partial(lift_kernel, count, part, gain is not None)
         outputs = [(half_wide, low)] + [((tokens, hidden_wide), f32)] * 2
         outputs += [((tokens, hidden_wide), low)]
-        return call(kernel, [*pieces, *weights], outputs, 6, after=after)
+        operands = [*pieces]
+        if gain is not None:
+            operands += [gain, chosen]
+            outputs += [(wide, low)]
+        return call(kernel, [*operands, *weights], outputs, 6, after=after)
 
     def mlp_backward(pieces, weights, down, kept, after=()):
         kernel = functools.partial(mlp_backward_kernel, count, part)
@@ -592,19 +628,22 @@
         *parts, branch, both = call(kernel, operands, outputs, 9, after=after)
         return parts, branch, both
 
-    def attention_backward(pieces, weights, out, found, kept, after=()):
-        kernel = functools.partial(attention_backward_kernel, count, part)
+    def attention_backward(pieces, weights, out, found, kept, dealt=False, after=()):
+        kernel = functools.partial(attention_backward_kernel, count, part, dealt)
         normed, raw, queries, keys, mixed, spread = kept
         outputs = [(wide, low)] * count + [(half_wide, low), (raw.shape, low)]
         outputs += [((1, HEAD_DIM), f32)] * 2
+        outputs += [(wide, low)] if dealt else []
         scratch = [(queries.shape, low), (keys.shape, low), (queries.shape, f32)]
         scratch += [(keys.shape, f32)] * 2
-        operands = [*pieces, *weights, out, cosine, sine, found[2], found[3], *places]
+        operands = [*pieces] + ([chosen] if dealt else [])
+        operands += [*weights, out, cosine, sine, found[2], found[3], *places]
         operands += [raw, queries, keys, spread]
-        *parts, branch, grad_raw, query, key = call(
-            kernel, operands, outputs, 18, scratch, after=after
+        results = call(
+            kernel, operands, outputs, 18, scratch, after=after, limit=VMEM_LIMIT
         )
-        return parts, branch, grad_raw, (query, key)
+        parts, (branch, grad_raw, query, key, *rest) = results[:count], results[count:]
+        return (parts, branch, grad_raw, (query, key), *rest)
 
     def weight_grads(left, grads, inner, branch, after=()):
         kernel = functools.partial(weight_grads_kernel, part)
@@ -614,43 +653,53 @@
         operands = [left, grads, inner, branch]
         return call(kernel, operands, outputs, 6, [((width, tokens), low)], after=after)
 
-    own = gathered_direct(attention_blocks[0])
-    pieces = hops(tie(entering, attention_blocks[0]))
-    own = tie(own, pieces)
-    qkv_first = [own, swap(own)]
-    found_first = split_gains(own)
-    if aligned:
-        out_first = shared_rows(own[:, qkv_rows:])
-    else:
+    if not aligned:
         outs, downs = whole_rows(out_weight, query_half), whole_rows(down_weight, hidden_half)
-        out_first = [outs[0], outs[0]]
+
+    def arrived(value, pieces):
+        own = tie(value, pieces)
+        return [own, swap(own)]
+
+    def moving_rows(weights, first_row, whole):
+        return met(picked_rows(weights[0], first_row)) if aligned else [whole]
+
+    def with_far(shares):
+        return [*shares, *map(swap, shares)] if aligned else shares
+
+    pieces = hops(entering)
+    cotangents = hops(tie(cotangent, pieces[1]))
+    qkv_first = arrived(gathered(attention_blocks[0]), (pieces, cotangents))
+    found_own, found_far = split_gains(qkv_first[0]), split_gains(qkv_first[1])
+    found_first = [jnp.where(first, own, far) for own, far in zip(found_own, found_far)]
+    found_last = [jnp.where(first, far, own) for own, far in zip(found_own, found_far)]
+    shares = moving_rows(qkv_first, qkv_rows, None if aligned else outs[0])
     kept_attention_first = attention_forward(pieces, qkv_first, found_first, True)
-    kept_attention_first, out_first = beside(kept_attention_first, out_first)
-    parts, out_first = rows_product(kept_attention_first[4], out_first)
+    kept_attention_first, shares = beside(kept_attention_first, shares)
+    *kept_attention_first, dealt_entering = kept_attention_first
+    parts, out_first = rows_product(kept_attention_first[4], with_far(shares))
     middle_first, normed = add(met(parts), entering, found_first[1], False)
-    own = tie(gathered(tie(mlp_blocks[0], own)), normed)
-    lift_first = [own, swap(own)]
-    down_first = shared_rows(own[:, lift_rows:]) if aligned else [downs[0], downs[0]]
-    kept_mlp_first = lift_forward(hops(normed), lift_first)
-    kept_mlp_first, down_first = beside(kept_mlp_first, down_first)
-    parts, down_first = rows_product(kept_mlp_first[3], down_first)
-
-    own = tie(gathered(attention_blocks[1]), kept_mlp_first[3])
-    qkv_last = [own, swap(own)]
-    found_last = split_gains(own)
-    out_last = shared_rows(own[:, qkv_rows:]) if aligned else [outs[1], outs[1]]
+    pieces = hops(normed)
+    lift_first = arrived(gathered(mlp_blocks[0]), pieces)
+    shares = moving_rows(lift_first, lift_rows, None if aligned else downs[0])
+    kept_mlp_first = lift_forward(pieces, lift_first)
+    kept_mlp_first, shares = beside(kept_mlp_first, shares)
+    parts, down_first = rows_product(kept_mlp_first[3], with_far(shares))
+
     hidden_last, normed = add(met(parts), middle_first, found_last[0], True)
-    kept_attention_last = attention_forward(
-        hops(normed), qkv_last, found_last, False, after=[out_last[1]]
-    )
-    parts, out_last = rows_product(kept_attention_last[4], out_last)
-    middle_last, normed = add(met(parts), hidden_last, found_last[1], False)
-    own = tie(gathered(mlp_blocks[1]), normed)
-    lift_last = [own, swap(own)]
-    down_last = shared_rows(own[:, lift_rows:]) if aligned else [downs[1], downs[1]]
-    kept_mlp_last = lift_forward(hops(normed), lift_last)
-    kept_mlp_last, down_last = beside(kept_mlp_last, down_last)
-    last_parts, down_last = rows_product(kept_mlp_last[3], down_last)
+    pieces = hops(normed)
+    qkv_last = arrived(gathered(attention_blocks[1]), pieces)
+    shares = moving_rows(qkv_last, qkv_rows, None if aligned else outs[1])
+    kept_attention_last = attention_forward(pieces, qkv_last, found_last, False)
+    kept_attention_last, shares = beside(kept_attention_last, shares)
+    parts, out_last = rows_product(kept_attention_last[4], with_far(shares))
+    middle_last, sent = add(met(parts), hidden_last, found_last[1], False, True)
+    pieces = hops(sent)
+    lift_last = arrived(gathered(mlp_blocks[1]), pieces)
+    shares = moving_rows(lift_last, lift_rows, None if aligned else downs[1])
+    kept_mlp_last = lift_forward(pieces, lift_last, found_last[1])
+    kept_mlp_last, shares = beside(kept_mlp_last, shares)
+    *kept_mlp_last, dealt_middle = kept_mlp_last
+    last_parts, down_last = rows_product(kept_mlp_last[3], with_far(shares), True)
 
     def meet(grads, swapped):
         own, far, own_rows, far_rows = grads
@@ -662,24 +711,33 @@
         total, *rows_by = call(meet_kernel, operands, outputs, 4, scalars=[index])
         return total, rows_by
 
-    def met_gains(gains):
-        split = jnp.concatenate([gain.reshape(depth, -1) for gain in gains], axis=1)
-        split = split + swap(split.astype(low)).astype(f32)
-        split = jnp.pad(split, ((0, 0), (0, GAIN_ROWS * LANES - split.shape[1])))
-        return split.reshape(depth, GAIN_ROWS, LANES).astype(low)
-
-    def laid_out(total, rows_by, gains=None):
-        operands = [total] + ([] if gains is None else [gains])
-        size = total.shape[1] + (0 if gains is None else GAIN_ROWS)
-        if aligned:
-            operands += rows_by
-            size += rows_by[0].shape[0]
-        kernel = functools.partial(layout_kernel, part, gains is not None)
+    def laid_out(total, *rows_by):
+        if not aligned:
+            return total
+        size = total.shape[1] + sum(rows[0].shape[0] for rows in rows_by)
         outputs = [((depth, size, LANES), low)]
+        operands = [total] + [row for rows in rows_by for row in rows]
+        kernel = functools.partial(layout_kernel, count)
         return call(kernel, operands, outputs, 3, scalars=[index])[0]
+
+    def gains_reduced(from_first, from_last):
+        def by_pack(gains):
+            return jnp.concatenate([gain.reshape(depth, -1) for gain in gains], axis=1)
+
+        one, two = by_pack(from_first), by_pack(from_last)
+        total = jnp.where(first, one, two) + swap(jnp.where(first, two, one))
+        pack = lax.axis_index("fsdp")
+        summed = lax.dynamic_index_in_dim(total, pack, 0)
+        for k in range(1, depth):
+            sent = lax.dynamic_index_in_dim(total, pack ^ k, 0)
+            summed = summed + lax.ppermute(sent, "fsdp", [(i, i ^ k) for i in range(depth)])
+        return sum(hops(summed))
 
     def scattered(operand):
         return lax.psum_scatter(operand, "fsdp", scatter_dimension=0, tiled=False)
+
+    def met_rows(rows_by):
+        return met(rows_by) if aligned else rows_by
 
     def rows_fallback(rest):
         (rest,) = rest
@@ -690,103 +748,82 @@
         full = lax.dynamic_update_slice_in_dim(full, rest.astype(low), at, 0)
         return lax.psum(lax.psum_scatter(full, "fsdp", scatter_dimension=0, tiled=True), "ctx")
 
-    wanted = lax.dynamic_slice_in_dim(slots, piece * rows, rows, 0)
-    wanted = ((wanted // rows) ^ piece) * rows + wanted % rows
-    chosen = (wanted[:, None] == order[None, :]).astype(low)
-
-    def dealt(pieces):
-        return dot(chosen, jnp.concatenate(pieces, axis=0)).astype(low)
-
     def returned(pieces, layer):
         own = jnp.stack(pieces)
         return own, lax.ppermute(own, "section", [(1 - layer, layer)])
 
-    pieces = hops(cotangent)
-    parts, branch, both = mlp_backward(pieces, lift_last, down_last, kept_mlp_last)
-    parts = met(parts)
+    def meet_beside(grads, swapped, sent):
+        return beside(meet(grads, swapped), hops(sent))
+
+    parts, branch, both = mlp_backward(cotangents, lift_last, down_last, kept_mlp_last)
     mlp_grads = weight_grads(kept_mlp_last[0], both, kept_mlp_last[3], branch)
-    grad, sent, mlp_gain = add_back(
-        parts, cotangent, middle_last, found_last[1], False, after=[mlp_grads[1]]
-    )
+    mlp_grads, parts = beside(mlp_grads, met(parts))
     swapped = swap(mlp_grads[1]), swap(mlp_grads[3])
-    pieces = hops(sent)
-    mlp_total, mlp_rows = meet(mlp_grads, swapped)
-    results = attention_backward(
-        pieces, qkv_last, out_last, found_last, kept_attention_last, after=[mlp_total]
-    )
-    results, last_parts = beside(results, met(tie(last_parts, pieces[1])))
+    grad, sent, mlp_gain = add_back(parts, cotangent, middle_last, found_last[1], False)
+    (total, down_rows), pieces = meet_beside(mlp_grads, swapped, sent)
+
+    results = attention_backward(pieces, qkv_last, out_last, found_last, kept_attention_last, after=[total])
+    moving = met(tie(last_parts, pieces[1])), met_rows(down_rows)
+    results, (last_parts, moved) = beside(results, moving)
     parts, branch, grad_raw, head_gains = results
-    last = middle_last
+    last = dealt_middle.astype(f32)
     for value in last_parts:
         last = last + value.astype(f32)
     last = last.astype(low)
-    mlp_rows = met(mlp_rows)
-    parts = met(parts)
-    attention_grads = weight_grads(
-        kept_attention_last[0], grad_raw, kept_attention_last[4], branch
+    operand = laid_out(total, moved)
+    attention_grads = weight_grads(kept_attention_last[0], grad_raw, kept_attention_last[4], branch)
+    (attention_grads, operand), parts = beside((attention_grads, operand), met(parts))
+    mlp_last = scattered(operand)
+    swapped = swap(attention_grads[1]), swap(attention_grads[3])
+    grad, sent, gain = add_back(parts, grad, hidden_last, found_last[0], True)
+    gains_last = (gain, mlp_gain, *head_gains)
+    down_grad_last = None if aligned else rows_fallback(down_rows)
+    (total, out_rows), pieces = meet_beside(attention_grads, swapped, sent)
+
+    results = mlp_backward(pieces, lift_first, down_first, kept_mlp_first, after=[total])
+    results, moved = beside(results, met_rows(out_rows))
+    parts, branch, both = results
+    operand = laid_out(total, moved)
+    mlp_grads = weight_grads(kept_mlp_first[0], both, kept_mlp_first[3], branch)
+    (mlp_grads, operand, mlp_last), parts = beside((mlp_grads, operand, mlp_last), met(parts))
+    attention_last = scattered(operand)
+    out_grad_last = None if aligned else rows_fallback(out_rows)
+    swapped = swap(mlp_grads[1]), swap(mlp_grads[3])
+    grad, sent, mlp_gain = add_back(parts, grad, middle_first, found_first[1], False)
+    (total, down_rows), pieces = meet_beside(mlp_grads, swapped, sent)
+
+    results = attention_backward(
+        pieces, qkv_first, out_first, found_first, kept_attention_first, True, after=[total]
     )
-    mlp_operand = laid_out(mlp_total, mlp_rows)
-    mlp_last = scattered(mlp_operand)
-    grad, sent, gain = add_back(
-        parts, grad, hidden_last, found_last[0], True, after=[attention_grads[1], mlp_operand]
+    mlp_last = tie(mlp_last, pieces[1])
+    near = [hop(mlp_last, k) for k in range(1, count - 1)]
+    results, (near, moved) = beside(results, (near, met_rows(down_rows)))
+    parts, branch, grad_raw, head_gains, dealt_branch = results
+    operand = laid_out(total, moved)
+    mlp_first = scattered(operand)
+    attention_grads = weight_grads(kept_attention_first[0], grad_raw, kept_attention_first[4], branch)
+    (attention_grads, _), parts = beside((attention_grads, operand), met(parts))
+    swapped = swap(attention_grads[1]), swap(attention_grads[3])
+    down_grad_first = None if aligned else rows_fallback(down_rows)
+    total, out_rows = meet(attention_grads, swapped)
+    moved = met_rows(out_rows)
+    operand = laid_out(total, moved)
+    out_grad_first = None if aligned else rows_fallback(out_rows)
+    attention_last = hops_split(tie(attention_last, parts))
+    unused, grad, gain = add_back(
+        parts, dealt_branch, dealt_entering, found_first[0], True, after=[operand]
     )
-    gains = (gain, mlp_gain, *head_gains)
-    down_grad_last = None if aligned else rows_fallback(mlp_rows)
-
-    swapped = swap(attention_grads[1]), swap(attention_grads[3])
-    pieces = hops(sent)
-    attention_total, attention_rows = meet(attention_grads, swapped)
-    results = mlp_backward(
-        pieces, lift_first, down_first, kept_mlp_first, after=[attention_total]
+    gains_first = (gain, mlp_gain, *head_gains)
+    sums = gains_reduced(gains_first, gains_last)
+    mlp_last = [mlp_last, *near, hop(tie(mlp_last, operand), count - 1)]
+    mlp_first, operand = beside(mlp_first, operand)
+    attention_first = scattered(operand)
+    mlp_first, (grad, sums, mlp_last, attention_last) = beside(
+        mlp_first, (grad, sums, mlp_last, attention_last)
     )
-    results, last = beside(results, hops(tie(last, pieces[1])))
-    parts, branch, both = results
-    last = dealt(last)
-    attention_rows = met(attention_rows)
-    gains = met_gains(gains)
-    parts = met(parts)
-    attention_operand = laid_out(attention_total, attention_rows, gains)
-    mlp_grads = weight_grads(kept_mlp_first[0], both, kept_mlp_first[3], branch)
-    attention_last = scattered(attention_operand)
-    out_grad_last = None if aligned else rows_fallback(attention_rows)
-    grad, sent, mlp_gain = add_back(
-        parts,
-        grad,
-        middle_first,
-        found_first[1],
-        False,
-        after=[mlp_grads[1], attention_operand, mlp_last],
-    )
-    swapped = swap(mlp_grads[1]), swap(mlp_grads[3])
-    pieces = hops(sent)
-    mlp_total, mlp_rows = meet(mlp_grads, swapped)
-    results = attention_backward(
-        pieces, qkv_first, out_first, found_first, kept_attention_first, after=[mlp_total]
-    )
-    results, mlp_last = beside(results, hops(tie(mlp_last, pieces[1])))
-    parts, branch, grad_raw, head_gains = results
-    mlp_rows = met(mlp_rows)
-    parts = met(parts)
-    mlp_operand = laid_out(mlp_total, mlp_rows)
-    attention_grads = weight_grads(
-        kept_attention_first[0], grad_raw, kept_attention_first[4], branch
-    )
-    mlp_first = scattered(mlp_operand)
-    swapped = swap(attention_grads[1]), swap(attention_grads[3])
-    attention_total, attention_rows = meet(attention_grads, swapped)
-    attention_rows = met(attention_rows)
-    down_grad_first = None if aligned else rows_fallback(mlp_rows)
-    grad, sent, gain = add_back(
-        parts, grad, entering, found_first[0], True, after=[attention_grads[1], mlp_operand]
-    )
-    gains = met_gains((gain, mlp_gain, *head_gains))
-    attention_operand = laid_out(attention_total, attention_rows, gains)
-    attention_first = scattered(attention_operand)
-    out_grad_first = None if aligned else rows_fallback(attention_rows)
-    attention_last = hops(tie(attention_last, sent))
-    mlp_first = hops(tie(mlp_first, attention_last[1]))
-    grad = dealt(hops(tie(sent, mlp_first[1])))
+    mlp_first = hops_split(mlp_first)
     mlp_last, attention_last = returned(mlp_last, 1), returned(attention_last, 1)
+    attention_first = hops_split(tie(attention_first, mlp_first))
     mlp_first = returned(mlp_first, 0)
 
     def settle(kernel, from_first, from_last, outputs):
@@ -846,21 +883,15 @@
         halves_of(where, blocks, body)
 
     def attention_settle_kernel(where, *refs):
-        blocks, (query, key, value, sums, *out) = refs[:4], refs[4:]
-
-        @pl.when(pl.program_id(0) == 0)
-        def _():
-            sums[...] = jnp.zeros_like(sums)
+        blocks, (query, key, value, *out) = refs[:4], refs[4:]
 
         def body(half, block):
             query[:, span(half, query_half)] = block[0, :part, :].astype(f32)
-            both = block[0, part + GAIN_ROWS : qkv_rows, :].astype(f32)
+            both = block[0, part : 2 * part, :].astype(f32)
             key[:, span(half, key_half)] = both[:, :key_half]
             value[:, span(half, key_half)] = both[:, key_half:]
-            if half == 0:
-                sums[...] += block[0, part : part + GAIN_ROWS, :].astype(f32)
             if aligned:
-                place_rows(block, qkv_rows, half, out[0])
+                place_rows(block, 2 * part, half, out[0])
 
         halves_of(where, blocks, body)
 
@@ -871,15 +902,12 @@
         return ((2, size, width), (2, size // count, width), lambda i: (0, i, 0))
 
     outputs = [column_output(hidden_half)] * 2 + ([row_output(hidden_half)] if aligned else [])
-    grad_gate, grad_up, *grad_down = settle(
-        mlp_settle_kernel, mlp_first, mlp_last, outputs
-    )
-    attention_first = returned(hops(tie(attention_first, grad_gate)), 0)
+    settled = settle(mlp_settle_kernel, mlp_first, mlp_last, outputs)
+    (grad_gate, grad_up, *grad_down), attention_first = beside(settled, attention_first)
     outputs = [column_output(query_half)] + [column_output(key_half)] * 2
-    outputs += [((GAIN_ROWS, LANES), (GAIN_ROWS, LANES), lambda i: (0, 0))]
     outputs += [row_output(query_half)] if aligned else []
-    grad_query, grad_key, grad_value, sums, *grad_out = settle(
-        attention_settle_kernel, attention_first, attention_last, outputs
+    grad_query, grad_key, grad_value, *grad_out = settle(
+        attention_settle_kernel, returned(attention_first, 0), attention_last, outputs
     )
     if aligned:
         grad_out, grad_down = grad_out[0].reshape(-1, width), grad_down[0].reshape(-1, width)
@@ -889,7 +917,6 @@
             own = jnp.where(first, one, two).astype(f32)
             pair.append(own + swap(jnp.where(first, two, one)).astype(f32))
         grad_out, grad_down = pair
-    sums = sums.reshape(1, -1)
     split, at = [], 0
     for size in sizes:
         split.append(sums[:, at : at + size])

time: 646 us -> 578 us (0.89)
  Pallas kernels: 199 us -> 129 us
  waiting for transfers between devices: 229 us -> 190 us
  local copies, waits for them, and re-layouts: 40.5 us -> 74.1 us
    pallas_call x31 -> x35, Pallas kernels: 179 us -> 110 us  [call(): pl.pallas_call(body, out_shape=shapes, in_specs=[anywhere] * skipped + [s...]
    ppermute x90 -> x96, waiting for transfers between devices: 188 us -> 150 us  [hop(): return lax.ppermute(value, 'ctx', [(i, i ^ step) for i in range(count)])]
    ppermute x3, waiting for transfers between devices: 27.8 us -> 0.64 us  [gains_reduced(): lax.ppermute(sent, 'fsdp', [(i, i ^ k) for i in range(depth)])]
    unnamed x231 -> x295, local copies, waits for them, and re-layouts: 27.8 us -> 54.6 us
    reduce_scatter x4, waiting for transfers between devices: 0.01 us -> 14.4 us  [scattered(): return lax.psum_scatter(operand, 'fsdp', scatter_dimension=0, tiled=False)]
    all_gather x3 -> x4, waiting for transfers between devices: 4.92 us -> 16.9 us  [gathered(): return lax.all_gather(block, 'fsdp', axis=0, tiled=False)]
    ppermute x90 -> x96, starting transfers between devices: 111 us -> 112 us  [hop(): return lax.ppermute(value, 'ctx', [(i, i ^ step) for i in range(count)])]
  transfers between devices with their start and end apart: 126 -> 144, of which waited for: 56 -> 63; matrix products, arithmetic and copies ran while one was open for 6% -> 7% of each run, Pallas kernels for 27% -> 20%
where the time goes in v3:
time: 578 us; the launch traced here: 569 us
  waiting for transfers between devices  190 us (33%)
  starting transfers between devices  132 us (23%)
  Pallas kernels  129 us (22%)
  local copies, waits for them, and re-layouts  74.1 us (13%)
  other arithmetic  26.9 us (5%)
  between operations  16.5 us (3%)
    ppermute x96, waiting for transfers between devices, hop(): return lax.ppermute(value, 'ctx', [(i, i ^ step) for i in range(count)])  150 us
    ppermute x96, starting transfers between devices, hop(): return lax.ppermute(value, 'ctx', [(i, i ^ step) for i in range(count)])  112 us
    pallas_call x35, Pallas kernels, call(): pl.pallas_call(body, out_shape=shapes, in_specs=[anywhere] * skipped + [s...  110 us
    unnamed x295, local copies, waits for them, and re-layouts  54.6 us
    all_gather x4, waiting for transfers between devices, gathered(): return lax.all_gather(block, 'fsdp', axis=0, tiled=False)  16.9 us
    reduce_scatter x4, waiting for transfers between devices, scattered(): return lax.psum_scatter(operand, 'fsdp', scatter_dimension=0, tiled=False)  14.4 us
    pallas_call x2, Pallas kernels, settle(): pl.pallas_call(kernel, grid_spec=pltpu.PrefetchScalarGridSpec(num_scalar_...  13.5 us
  transfers between devices with their start and end apart: 144, of which 63 were waited for; matrix products, arithmetic and copies ran while one was open for 7% of the time, Pallas kernels for 20%

profile of v3, /device:TPU:0, one launch (start us, length us, event | category | flops | bytes accessed | tf_op | source)
XLA Modules:
  0.0 569.3 jit_solution(13455198880386331538)
XLA Ops:
  28.3 5.5 collective-permute-done.1.refs_1_
  45.1 6.8 %collective-permute-done.6.refs_2_ = bf16[128,1024]{1,0:T(8,128)(2,1)S(1)} collective-permute-done((bf16[128,1024]{1,0:T(8,128)(2,1)S(1)}, bf16[128,1024]{1,0:T(8,128)(2,1)S(1)}, u32[]{:S(2)}, u32[]{:S(2)}) %collective-permute-start.6) | collective-permute-done | bytes 262176 | tf_op jit(solution)/shard_map/ppermute | solution.py:29
  51.9 6.3 %all-gather.9.cloned.1.call-done = bf16[3136,256]{1,0:T(8,128)(2,1)} async-done(((bf16[784,256]{1,0:T(8,128)(2,1)}), bf16[3136,256]{1,0:T(8,128)(2,1)}) %all-gather.9.cloned.1.call-update) | async-done | bytes 1605648 | tf_op jit(solution)/shard_map/all_gather | solution.py:536
  77.0 10.5 %shard_map.230 = (bf16[512,1024]{1,0:T(8,128)(2,1)S(1)}, f32[512,1024]{1,0:T(8,128)S(1)}, bf16[512,512]{1,0:T(8,128)(2,1)S(1)}, bf16[512,256]{1,0:T(8,128)(2,1)S...) custom-call(bf16[128,1024]{1,0:T(8,128)(2,1)S(1)} %get-tuple-element.659.refs_0_.refs_4_, ...), custom_call_target="tpu_custom_call" | custom-call | flops 13799999488 | bytes 10046464 | tf_op jit(solution)/shard_map/pallas_call | solution.py:129
  96.8 5.6 collective-permute-done.16.refs_1_
  102.4 6.3 %collective-permute-done.17.refs_2_ = bf16[128,1024]{1,0:T(8,128)(2,1)S(1)} collective-permute-done((bf16[128,1024]{1,0:T(8,128)(2,1)S(1)}, bf16[128,1024]{1,0:T(8,128)(2,1)S(1)}, u32[]{:S(2)}, u32[]{:S(2)}) %collective-permute-start.17) | collective-permute-done | bytes 262176 | tf_op jit(solution)/shard_map/ppermute | solution.py:29
  146.9 5.6 collective-permute-done.31.refs_1_
  152.5 6.1 %collective-permute-done.32.refs_2_ = bf16[128,1024]{1,0:T(8,128)(2,1)S(1)} collective-permute-done((bf16[128,1024]{1,0:T(8,128)(2,1)S(1)}, bf16[128,1024]{1,0:T(8,128)(2,1)S(1)}, u32[]{:S(2)}, u32[]{:S(2)}) %collective-permute-start.32) | collective-permute-done | bytes 262176 | tf_op jit(solution)/shard_map/ppermute | solution.py:29
  163.2 5.8 %collective-permute-done.34.refs_1_ = bf16[128,1024]{1,0:T(8,128)(2,1)S(1)} collective-permute-done((bf16[128,1024]{1,0:T(8,128)(2,1)S(1)}, bf16[128,1024]{1,0:T(8,128)(2,1)S(1)}, u32[]{:S(2)}, u32[]{:S(2)}) %collective-permute-start.34) | collective-permute-done | bytes 262176 | tf_op jit(solution)/shard_map/ppermute | solution.py:29
  178.6 10.7 %shard_map.239 = (bf16[512,1024]{1,0:T(8,128)(2,1)S(1)}, f32[512,1024]{1,0:T(8,128)S(1)}, bf16[512,512]{1,0:T(8,128)(2,1)S(1)}, bf16[512,256]{1,0:T(8,128)(2,1)S...) custom-call(bf16[128,1024]{1,0:T(8,128)(2,1)S(1)} %get-tuple-element.375.refs_0_, ...), custom_call_target="tpu_custom_call" | custom-call | flops 13799999488 | bytes 9255936 | tf_op jit(solution)/shard_map/pallas_call | solution.py:129
  197.3 5.6 collective-permute-done.45.refs_1_
  203.0 6.2 %collective-permute-done.46.refs_2_ = bf16[128,1024]{1,0:T(8,128)(2,1)S(1)} collective-permute-done((bf16[128,1024]{1,0:T(8,128)(2,1)S(1)}, bf16[128,1024]{1,0:T(8,128)(2,1)S(1)}, u32[]{:S(2)}, u32[]{:S(2)}) %collective-permute-start.46) | collective-permute-done | bytes 262176 | tf_op jit(solution)/shard_map/ppermute | solution.py:29
  213.6 8.3 %all-gather.15.cloned.1.call-done = bf16[4608,256]{1,0:T(8,128)(2,1)} async-done(((bf16[1152,256]{1,0:T(8,128)(2,1)}), bf16[4608,256]{1,0:T(8,128)(2,1)}) %all-gather.15.cloned.1.call-update) | async-done | bytes 2359312 | tf_op jit(solution)/shard_map/all_gather | solution.py:536
  271.6 5.8 %collective-permute-done.65.refs_3_ = bf16[128,1024]{1,0:T(8,128)(2,1)S(1)} collective-permute-done((bf16[128,1024]{1,0:T(8,128)(2,1)S(1)}, bf16[128,1024]{1,0:T(8,128)(2,1)S(1)}, u32[]{:S(2)}, u32[]{:S(2)}) %collective-permute-start.65) | collective-permute-done | bytes 262176 | tf_op jit(solution)/shard_map/ppermute | solution.py:29
  286.8 18.6 %shard_map.250 = (bf16[128,1024]{1,0:T(8,128)(2,1)}, bf16[128,1024]{1,0:T(8,128)(2,1)}, bf16[128,1024]{1,0:T(8,128)(2,1)}, bf16[128,1024]{1,0:T(8,128)(2,1)}, bf...) custom-call(bf16[4,768,256]{2,1,0:T(8,128)(2,1)} %copy-done.37, ...), custom_call_target="tpu_custom_call" | custom-call | flops 20700000256 | bytes 11878400 | tf_op jit(solution)/shard_map/pallas_call | solution.py:129
  327.2 5.4 collective-permute-done.78.refs_2_
  340.8 5.8 %shard_map.255 = (bf16[128,1024]{1,0:T(8,128)(2,1)S(1)}, bf16[128,1024]{1,0:T(8,128)(2,1)}, bf16[128,1024]{1,0:T(8,128)(2,1)}, bf16[128,1024]{1,0:T(8,128)(2,1)}...) custom-call(bf16[4,512,256]{2,1,0:T(8,128)(2,1)S(1)} %get-tuple-element.502.refs_0_.refs_1_, ...), custom_call_target="tpu_custom_call" | custom-call | flops 10350000128 | bytes 14155776 | tf_op jit(solution)/shard_map/pallas_call | solution.py:129
  379.3 5.9 %collective-permute-done.90.refs_3_ = bf16[128,1024]{1,0:T(8,128)(2,1)S(1)} collective-permute-done((bf16[128,1024]{1,0:T(8,128)(2,1)S(1)}, bf16[128,1024]{1,0:T(8,128)(2,1)S(1)}, u32[]{:S(2)}, u32[]{:S(2)}) %collective-permute-start.90) | collective-permute-done | bytes 262176 | tf_op jit(solution)/shard_map/ppermute | solution.py:29
  391.5 20.9 %shard_map.260 = (bf16[128,1024]{1,0:T(8,128)(2,1)}, bf16[128,1024]{1,0:T(8,128)(2,1)}, bf16[128,1024]{1,0:T(8,128)(2,1)}, bf16[128,1024]{1,0:T(8,128)(2,1)}, bf...) custom-call(bf16[4,768,256]{2,1,0:T(8,128)(2,1)} %copy-done.39, ...), custom_call_target="tpu_custom_call" | custom-call | flops 20700000256 | bytes 12664832 | tf_op jit(solution)/shard_map/pallas_call | solution.py:129
  474.9 7.4 %collective-permute-done.118 = bf16[384,256]{1,0:T(8,128)(2,1)S(1)} collective-permute-done((bf16[384,256]{1,0:T(8,128)(2,1)}, bf16[384,256]{1,0:T(8,128)(2,1)S(1)}, u32[]{:S(2)}, u32[]{:S(2)}) %collective-permute-start.118) | collective-permute-done | bytes 196640 | tf_op jit(solution)/shard_map/ppermute | solution.py:29
  498.4 5.3 collective-permute-done.123
  513.7 10.3 %reduce-scatter.11.cloned.1.call-done = bf16[1,768,256]{2,1,0:T(8,128)(2,1)} async-done(((bf16[4,768,256]{2,1,0:T(8,128)(2,1)}), bf16[1,768,256]{2,1,0:T(8,128)(2,1)}) %reduce-scatter.11.cloned.1.call-update) | async-done | bytes 393232 | tf_op jit(solution)/shard_map/reduce_scatter | solution.py:737
  532.1 7.5 %shard_map.266 = (f32[256,3072]{1,0:T(8,128)}, f32[256,3072]{1,0:T(8,128)}, f32[2,384,1024]{2,1,0:T(8,128)}) custom-call(s32[2]{0:T(128)} %pad_add_fusion.where, bf16[4,1152,256]{2,1,0:T(8,128)(2,1)} %pad_maximum_fusion.refs_0_, bf16[4,1152,256]{2,1,0:T(8,128)(2,1)} %collective-permute-done.126.refs_1_, bf16[4,1152,256]{2,1,0:T(8,128)(2,1)} %copy-done.104, ...), custom_call_target="tpu_custom_call" | custom-call | bytes 14155776 | tf_op jit(solution)/shard_map/pallas_call | solution.py:838
  556.1 5.9 %shard_map.267 = (f32[256,2048]{1,0:T(8,128)}, f32[256,1024]{1,0:T(8,128)}, f32[256,1024]{1,0:T(8,128)}, f32[2,256,1024]{2,1,0:T(8,128)}) custom-call(s32[2]{0:T(128)} %pad_add_fusion.where, bf16[4,768,256]{2,1,0:T(8,128)(2,1)} %copy-done.106, bf16[4,768,256]{2,1,0:T(8,128)(2,1)} %copy-done.111, bf16[4,768,256]{2,1,0:T(8,128)(2,1)} %copy-done.105, ...), custom_call_target="tpu_custom_call" | custom-call | bytes 9437184 | tf_op jit(solution)/shard_map/pallas_call | solution.py:838
  (684 shorter events, 364.7 us)
Async XLA Ops:
  7.2 51.0 %all-gather.9.cloned.1.call-start = ((), (), s32[]{:S(2)}) async-start(), calls=%async_computation.8 | async-start | bytes 2007040 | tf_op jit(solution)/shard_map/all_gather | solution.py:536
  17.8 97.9 %all-gather.11.cloned.1.call-start = ((), (), s32[]{:S(2)}) async-start(), calls=%async_computation.9 | async-start | bytes 2949120 | tf_op jit(solution)/shard_map/all_gather | solution.py:536
  40.8 22.9 %collective-permute-start.22 = (bf16[1152,256]{1,0:T(8,128)(2,1)}, bf16[1152,256]{1,0:T(8,128)(2,1)}, u32[]{:S(2)}, u32[]{:S(2)}) collective-permute-start(bf16[1152,256]{1,0:T(8,128)(2,1)} %slice_bitcast_fusion), channel_id=1, source_target_pairs={{0,16},{16,0},{1,17},{17,1},{2,18},{18,2},{3,19},{19,3},{4,20},{20... | collective-permute-start | bytes 1769480 | tf_op jit(solution)/shard_map/ppermute | solution.py:24
  66.0 97.2 %all-gather.13.cloned.1.call-start = ((), (), s32[]{:S(2)}) async-start(), calls=%async_computation.10 | async-start | bytes 2007040 | tf_op jit(solution)/shard_map/all_gather | solution.py:536
  124.3 97.6 %all-gather.15.cloned.1.call-start = ((), (), s32[]{:S(2)}) async-start(), calls=%async_computation.11 | async-start | bytes 2949120 | tf_op jit(solution)/shard_map/all_gather | solution.py:536
  173.3 190.6 %reduce-scatter.5.cloned.1.call-start = ((), (), s32[]{:S(2)}) async-start(), calls=%async_computation.4 | async-start | bytes 2949120 | tf_op jit(solution)/shard_map/reduce_scatter | solution.py:737
  278.0 27.3 %collective-permute-start.67 = (bf16[128,1024]{1,0:T(8,128)(2,1)S(1)}, bf16[128,1024]{1,0:T(8,128)(2,1)S(1)}, u32[]{:S(2)}, u32[]{:S(2)}) collective-permute-start(bf16[128,1024]{1,0:T(8,128)(2,1)S(1)} %get-tuple-element.466), channel_id=1, source_target_pairs={{0,4},{4,0},{8,12},{12,8},{1,5},{5,1},{9,13},{13,9},{2,6},{6,2},{1... | collective-permute-start | bytes 786440 | tf_op jit(solution)/shard_map/ppermute | solution.py:29
  279.5 25.9 %collective-permute-start.68 = (bf16[128,1024]{1,0:T(8,128)(2,1)S(1)}, bf16[128,1024]{1,0:T(8,128)(2,1)S(1)}, u32[]{:S(2)}, u32[]{:S(2)}) collective-permute-start(bf16[128,1024]{1,0:T(8,128)(2,1)S(1)} %get-tuple-element.467), channel_id=1, source_target_pairs={{0,8},{4,12},{8,0},{12,4},{1,9},{5,13},{9,1},{13,5},{2,10},{6,14},... | collective-permute-start | bytes 786440 | tf_op jit(solution)/shard_map/ppermute | solution.py:29
  280.0 25.4 %collective-permute-start.69 = (bf16[128,1024]{1,0:T(8,128)(2,1)S(1)}, bf16[128,1024]{1,0:T(8,128)(2,1)S(1)}, u32[]{:S(2)}, u32[]{:S(2)}) collective-permute-start(bf16[128,1024]{1,0:T(8,128)(2,1)S(1)} %get-tuple-element.468), channel_id=1, source_target_pairs={{0,12},{4,8},{8,4},{12,0},{1,13},{5,9},{9,5},{13,1},{2,14},{6,10},... | collective-permute-start | bytes 786440 | tf_op jit(solution)/shard_map/ppermute | solution.py:29
  281.5 23.8 %collective-permute-start.71 = (bf16[384,256]{1,0:T(8,128)(2,1)S(1)}, bf16[384,256]{1,0:T(8,128)(2,1)S(1)}, u32[]{:S(2)}, u32[]{:S(2)}) collective-permute-start(bf16[384,256]{1,0:T(8,128)(2,1)S(1)} %get-tuple-element.471), channel_id=1, source_target_pairs={{0,8},{4,12},{8,0},{12,4},{1,9},{5,13},{9,1},{13,5},{2,10},{6,14},... | collective-permute-start | bytes 589832 | tf_op jit(solution)/shard_map/ppermute | solution.py:29
  285.3 20.1 %collective-permute-start.72 = (bf16[384,256]{1,0:T(8,128)(2,1)S(1)}, bf16[384,256]{1,0:T(8,128)(2,1)S(1)}, u32[]{:S(2)}, u32[]{:S(2)}) collective-permute-start(bf16[384,256]{1,0:T(8,128)(2,1)S(1)} %get-tuple-element.472), channel_id=1, source_target_pairs={{0,12},{4,8},{8,4},{12,0},{1,13},{5,9},{9,5},{13,1},{2,14},{6,10},... | collective-permute-start | bytes 589832 | tf_op jit(solution)/shard_map/ppermute | solution.py:29
  318.0 113.1 %reduce-scatter.9.cloned.1.call-start = ((), (), s32[]{:S(2)}) async-start(), calls=%async_computation.6 | async-start | bytes 1966080 | tf_op jit(solution)/shard_map/reduce_scatter | solution.py:737
  364.4 119.6 %reduce-scatter.7.cloned.1.call-start = ((), (), s32[]{:S(2)}) async-start(), calls=%async_computation.5 | async-start | bytes 2949120 | tf_op jit(solution)/shard_map/reduce_scatter | solution.py:737
  385.9 26.4 %collective-permute-start.92 = (bf16[1152,256]{1,0:T(8,128)(2,1)S(1)}, bf16[1152,256]{1,0:T(8,128)(2,1)S(1)}, u32[]{:S(2)}, u32[]{:S(2)}) collective-permute-start(bf16[1152,256]{1,0:T(8,128)(2,1)S(1)} %bitcast.129), channel_id=1, source_target_pairs={{0,4},{4,0},{8,12},{12,8},{1,5},{5,1},{9,13},{13,9},{2,6},{6,2},{1... | collective-permute-start | bytes 1769480 | tf_op jit(solution)/shard_map/ppermute | solution.py:29
  387.0 25.4 %collective-permute-start.93 = (bf16[1152,256]{1,0:T(8,128)(2,1)S(1)}, bf16[1152,256]{1,0:T(8,128)(2,1)S(1)}, u32[]{:S(2)}, u32[]{:S(2)}) collective-permute-start(bf16[1152,256]{1,0:T(8,128)(2,1)S(1)} %bitcast.130), channel_id=1, source_target_pairs={{0,8},{4,12},{8,0},{12,4},{1,9},{5,13},{9,1},{13,5},{2,10},{6,14},... | collective-permute-start | bytes 1769480 | tf_op jit(solution)/shard_map/ppermute | solution.py:29
  388.0 24.4 %collective-permute-start.94 = (bf16[384,256]{1,0:T(8,128)(2,1)S(1)}, bf16[384,256]{1,0:T(8,128)(2,1)S(1)}, u32[]{:S(2)}, u32[]{:S(2)}) collective-permute-start(bf16[384,256]{1,0:T(8,128)(2,1)S(1)} %get-tuple-element.572), channel_id=1, source_target_pairs={{0,4},{4,0},{8,12},{12,8},{1,5},{5,1},{9,13},{13,9},{2,6},{6,2},{1... | collective-permute-start | bytes 589832 | tf_op jit(solution)/shard_map/ppermute | solution.py:29
  389.4 22.9 %collective-permute-start.95 = (bf16[384,256]{1,0:T(8,128)(2,1)S(1)}, bf16[384,256]{1,0:T(8,128)(2,1)S(1)}, u32[]{:S(2)}, u32[]{:S(2)}) collective-permute-start(bf16[384,256]{1,0:T(8,128)(2,1)S(1)} %get-tuple-element.573), channel_id=1, source_target_pairs={{0,8},{4,12},{8,0},{12,4},{1,9},{5,13},{9,1},{13,5},{2,10},{6,14},... | collective-permute-start | bytes 589832 | tf_op jit(solution)/shard_map/ppermute | solution.py:29
  390.0 22.4 %collective-permute-start.96 = (bf16[384,256]{1,0:T(8,128)(2,1)S(1)}, bf16[384,256]{1,0:T(8,128)(2,1)S(1)}, u32[]{:S(2)}, u32[]{:S(2)}) collective-permute-start(bf16[384,256]{1,0:T(8,128)(2,1)S(1)} %get-tuple-element.574), channel_id=1, source_target_pairs={{0,12},{4,8},{8,4},{12,0},{1,13},{5,9},{9,5},{13,1},{2,14},{6,10},... | collective-permute-start | bytes 589832 | tf_op jit(solution)/shard_map/ppermute | solution.py:29
  415.6 108.4 %reduce-scatter.11.cloned.1.call-start = ((), (), s32[]{:S(2)}) async-start(), calls=%async_computation.7 | async-start | bytes 1966080 | tf_op jit(solution)/shard_map/reduce_scatter | solution.py:737
  432.9 18.7 %collective-permute-start.113 = (bf16[384,256]{1,0:T(8,128)(2,1)}, bf16[384,256]{1,0:T(8,128)(2,1)}, u32[]{:S(2)}, u32[]{:S(2)}) collective-permute-start(bf16[384,256]{1,0:T(8,128)(2,1)} %get-tuple-element.664), channel_id=1, source_target_pairs={{0,4},{4,0},{8,12},{12,8},{1,5},{5,1},{9,13},{13,9},{2,6},{6,2},{1... | collective-permute-start | bytes 589832 | tf_op jit(solution)/shard_map/ppermute | solution.py:29
  453.9 19.3 %collective-permute-start.117 = (bf16[384,256]{1,0:T(8,128)(2,1)}, bf16[384,256]{1,0:T(8,128)(2,1)}, u32[]{:S(2)}, u32[]{:S(2)}) collective-permute-start(bf16[384,256]{1,0:T(8,128)(2,1)} %collective-permute-done.113), channel_id=1, source_target_pairs={{0,8},{4,12},{8,0},{12,4},{1,9},{5,13},{9,1},{13,5},{2,10},{6,14},... | collective-permute-start | bytes 589832 | tf_op jit(solution)/shard_map/ppermute | solution.py:29
  461.6 22.5 %collective-permute-start.112 = (bf16[1152,256]{1,0:T(8,128)(2,1)S(1)}, bf16[1152,256]{1,0:T(8,128)(2,1)S(1)}, u32[]{:S(2)}, u32[]{:S(2)}) collective-permute-start(bf16[1152,256]{1,0:T(8,128)(2,1)S(1)} %bitcast.131), channel_id=1, source_target_pairs={{0,12},{4,8},{8,4},{12,0},{1,13},{5,9},{9,5},{13,1},{2,14},{6,10},... | collective-permute-start | bytes 1769480 | tf_op jit(solution)/shard_map/ppermute | solution.py:29
  492.2 36.5 %collective-permute-start.127 = (bf16[4,1152,256]{2,1,0:T(8,128)(2,1)S(1)}, bf16[4,1152,256]{2,1,0:T(8,128)(2,1)}, u32[]{:S(2)}, u32[]{:S(2)}) collective-permute-start(bf16[4,1152,256]{2,1,0:T(8,128)(2,1)S(1)} %pad_maximum_fusion.1.refs_2_), channel_id=1, source_target_pairs={{0,16},{1,17},{2,18},{3,19},{4,20},{5,21},{6,22},{7,23},{8,24},{9,... | collective-permute-start | bytes 7077896 | tf_op jit(solution)/shard_map/ppermute | solution.py:753
  530.7 23.0 %collective-permute-start.135 = (bf16[4,768,256]{2,1,0:T(8,128)(2,1)S(1)}, bf16[4,768,256]{2,1,0:T(8,128)(2,1)S(1)}, u32[]{:S(2)}, u32[]{:S(2)}) collective-permute-start(bf16[4,768,256]{2,1,0:T(8,128)(2,1)S(1)} %pad_maximum_fusion.3.refs_2_), channel_id=1, source_target_pairs={{0,16},{1,17},{2,18},{3,19},{4,20},{5,21},{6,22},{7,23},{8,24},{9,... | collective-permute-start | bytes 4718600 | tf_op jit(solution)/shard_map/ppermute | solution.py:753
  (262 other events, 2773.7 us)
Sparse Core Ops, SparseCore 0:
  17.9 40.2 all-gather.8
  66.1 49.4 all-gather.10
  124.4 35.6 all-gather.12
  173.4 48.5 all-gather.14
  318.1 45.7 reduce-scatter.4
  366.6 34.7 reduce-scatter.8
  415.7 46.5 reduce-scatter.6
  490.4 33.6 reduce-scatter.10

commit v4 on v3

--- a/solution.py
+++ b/solution.py
@@ -139,6 +139,29 @@
     )(*after, *scalars, *operands)
 
 
+def mark_kernel(out):
+    out[...] = jnp.zeros_like(out)
+
+
+def mark(*values, took=200):
+    return call(mark_kernel, [], [((8, 128), f32)], took, after=values)[0]
+
+
+def window(values, at, size):
+    base = at // 128 * 128
+    block = values[:, base : base + LANES]
+    return pltpu.roll(block, LANES - (at - base), 1) if at != base else block
+
+
+def side_by_side(left, right, size):
+    if size == LANES:
+        return jnp.concatenate([left, right], axis=1)
+    lane = lax.broadcasted_iota(jnp.int32, (left.shape[0], 128), 1)
+    turned = pltpu.roll(right, size - 128, 1)
+    middle = jnp.where(lane < size - 128, left[:, 128:], turned[:, :128])
+    return jnp.concatenate([left[:, :128], middle, turned[:, 128:]], axis=1)
+
+
 def add_kernel(count, rounded, sends_rows, *refs):
     parts, (residual, gain, total, normed) = refs[:count], refs[count:]
     value = residual[...].astype(f32)
@@ -150,8 +173,11 @@
     normed[...] = (value if sends_rows else rms_scale(value, gain[...])).astype(low)
 
 
-def add_back_kernel(count, rounded, *refs):
-    parts, (upstream, middle, gain, total, sent, grad_gain) = refs[:count], refs[count:]
+def add_back_kernel(count, rounded, packs, *refs):
+    parts, (upstream, middle, gain, *refs) = refs[:count], refs[count:]
+    if packs:
+        mlp_gains, query_gains, key_gains, *refs = refs
+    total, sent, grad_gain, *packed = refs
     grad = parts[0][...].astype(f32)
     for part in parts[1:]:
         grad = grad + part[...].astype(f32)
@@ -160,6 +186,14 @@
     sent[...] = grad.astype(low)
     total[...] = grad.astype(low).astype(f32) if rounded else grad
     grad_gain[...] = gains
+    if packs:
+        (packed,) = packed
+        packed[...] = jnp.zeros_like(packed)
+        for z in range(packed.shape[0]):
+            packed[z, 0:1, :] = gains[:, span(z, LANES)]
+            packed[z, 1:2, :] = mlp_gains[:, span(z, LANES)]
+            packed[z, 2:3, :HEAD_DIM] = query_gains[...]
+            packed[z, 2:3, HEAD_DIM:] = key_gains[...]
 
 
 def attention_forward_kernel(count, part, raw_rows, *refs):
@@ -203,16 +237,22 @@
     def _(i):
         block = chunk(i, rows)
         visible = (place_row[...] >= start[block, :]) & (place_row[...] <= place[block, :])
-        for head in range(halves * group):
-            own, at = span(head // group, HEAD_DIM), span(head, HEAD_DIM)
-            scores = dot_cols(queries[block, at], keys[:, own]) * SCALE
+        visible = jnp.concatenate([visible] * group, axis=0)
+        for half in range(halves):
+            own = span(half, HEAD_DIM)
+            heads = range(half * group, (half + 1) * group)
+            query = jnp.concatenate([queries[block, span(h, HEAD_DIM)] for h in heads], axis=0)
+            scores = dot_cols(query, keys[:, own]) * SCALE
             scores = jnp.where(visible, scores, -1e30)
             top = jnp.max(scores, axis=-1, keepdims=True)
             raised = jnp.exp(scores - top)
             total = jnp.sum(raised, axis=-1, keepdims=True)
             probs = (raised * (1.0 / total)).astype(low)
-            mixed[block, at] = dot(probs, values[:, own]).astype(low)
-            spread[block, head : head + 1] = top + jnp.log(total)
+            value = dot(probs, values[:, own]).astype(low)
+            log_total = top + jnp.log(total)
+            for g, head in enumerate(heads):
+                mixed[block, span(head, HEAD_DIM)] = value[span(g, rows)]
+                spread[block, head : head + 1] = log_total[span(g, rows)]
 
 
 def pick_kernel(first_row, index, own, *out):
@@ -220,22 +260,45 @@
         share[...] = own[index[0] ^ k, first_row:, :]
 
 
-def rows_kernel(count, ordered, dealt, *refs):
-    index, left, *refs = refs
+def gather_shares(count, index, shares, whole):
+    size = whole.shape[0] // 2
+    share = size // count
+    for k, value in enumerate(shares):
+        to = k // count * size + (index[0] ^ (k % count)) * share
+        to = pl.ds(pl.multiple_of(to, share), share)
+        for j in range(whole.shape[1] // LANES):
+            whole[to, span(j, LANES)] = value[span(j, share), :]
+
+
+def gather_strided(index, own, far, whole):
+    depth, core = own.shape[0], index[1]
+    chunks = whole.shape[1] // LANES
+    share = whole.shape[0] // depth
+    half = share // 2
+    at = own.shape[1] - chunks * half
+    for z in range(depth):
+        place = (z // (depth // 2) ^ core) * (depth // 2) + z % (depth // 2)
+        for value, carried in ((own, core), (far, 1 - core)):
+            to = pl.ds(pl.multiple_of(place * share + carried * half, 32), half)
+            for j in range(chunks):
+                whole[to, span(j, LANES)] = value[z, at + j * half : at + (j + 1) * half, :]
+
+
+def gather_rows(form, count, index, given, whole):
+    if form == "whole":
+        whole[...] = given[0][...]
+    elif form == "shares":
+        gather_shares(count, index, given, whole)
+    else:
+        gather_strided(index, *given, whole)
+
+
+def rows_kernel(count, form, dealt, index, left, *refs):
     if dealt:
         chosen, *refs = refs
-    given = 1 if ordered else 2 * count
-    shares, parts, whole = refs[:given], refs[given : given + count], refs[given + count]
-    if ordered:
-        whole[...] = shares[0][...]
-    else:
-        size = whole.shape[0] // 2
-        share = size // count
-        for k, value in enumerate(shares):
-            to = k // count * size + (index[0] ^ (k % count)) * share
-            to = pl.ds(pl.multiple_of(to, share), share)
-            for j in range(whole.shape[1] // LANES):
-                whole[to, span(j, LANES)] = value[span(j, share), :]
+    given, refs = refs[: -count - 1], refs[-count - 1 :]
+    parts, whole = refs[:count], refs[count]
+    gather_rows(form, count, index, given, whole)
 
     @pl.loop(0, whole.shape[1] // LANES)
     def _(j):
@@ -271,10 +334,24 @@
         product[:, at] = (one * jax.nn.sigmoid(one) * two).astype(low)
 
 
-def mlp_backward_kernel(count, part, *refs):
+def mlp_forward_kernel(count, part, form, index, *refs):
     pieces, refs = refs[:count], refs[count:]
-    own_weight, far_weight, down, gate, lifted, *refs = refs
-    parts, (branch, grad_both) = refs[:count], refs[count:]
+    weights, refs = refs[:2], refs[2:]
+    given, refs = (weights, refs) if form == "strided" else (refs[:1], refs[1:])
+    kept, (*parts, whole) = refs[:4], refs[4:]
+    lift_kernel(count, part, False, *pieces, *weights, *kept)
+    rows_kernel(count, form, False, index, kept[3], *given, *parts, whole)
+
+
+def mlp_backward_kernel(count, part, form, index, *refs):
+    pieces, refs = refs[:count], refs[count:]
+    own_weight, far_weight, gate, lifted, *refs = refs
+    if form == "strided":
+        given = [own_weight, far_weight]
+    else:
+        given, refs = refs[:1], refs[1:]
+    parts, (branch, grad_both, down) = refs[:count], refs[count:]
+    gather_rows(form, count, index, given, down)
     size = gate.shape[1] // 2
     depth = own_weight.shape[0]
     join(pieces, branch)
@@ -333,16 +410,22 @@
     def _(i):
         block = chunk(i, rows)
         visible = (place_row[...] >= start[block, :]) & (place_row[...] <= place[block, :])
-        for head in range(halves * group):
-            own, at = span(head // group, HEAD_DIM), span(head, HEAD_DIM)
-            query, grad = queries[block, at], grad_mixed[block, at]
+        visible = jnp.concatenate([visible] * group, axis=0)
+        for half in range(halves):
+            own = span(half, HEAD_DIM)
+            heads = range(half * group, (half + 1) * group)
+            query = jnp.concatenate([queries[block, span(h, HEAD_DIM)] for h in heads], axis=0)
+            grad = jnp.concatenate([grad_mixed[block, span(h, HEAD_DIM)] for h in heads], axis=0)
+            log_total = jnp.concatenate([spread[block, h : h + 1] for h in heads], axis=0)
             scores = dot_cols(query, keys[:, own]) * SCALE
             scores = jnp.where(visible, scores, -1e30)
-            probs = jnp.exp(scores - spread[block, head : head + 1])
+            probs = jnp.exp(scores - log_total)
             grad_probs = dot_cols(grad, values[:, own])
             weighted = jnp.sum(probs * grad_probs, axis=-1, keepdims=True)
             grad_scores = (probs * (grad_probs - weighted)).astype(low)
-            grad_queries[block, at] = dot(grad_scores, keys[:, own]) * SCALE
+            grad_query = dot(grad_scores, keys[:, own]) * SCALE
+            for g, head in enumerate(heads):
+                grad_queries[block, span(head, HEAD_DIM)] = grad_query[span(g, rows)]
             grad_keys[:, own] += dot_rows(grad_scores, query) * SCALE
             grad_values[:, own] += dot_rows(probs.astype(low), grad)
 
@@ -380,11 +463,11 @@
         deal_out(parts, span(z, part), total)
 
 
-def weight_grads_kernel(part, left, grads, inner, branch, own, far, own_rows, far_rows, turned):
-    depth, count = own.shape[0], own_rows.shape[0]
+def weight_grads_kernel(part, strided, index, left, grads, inner, branch, own, far, *refs):
+    *rows_out, turned = refs
+    depth = own.shape[0]
     chunks = grads.shape[1] // (2 * LANES)
     size = inner.shape[1] // 2
-    share = size // count
     for z in range(depth):
         turned[span(z, part), :] = left[:, span(z, part)].T
     for half, target in enumerate((own, far)):
@@ -392,12 +475,30 @@
             total = dot(turned[...], grads[:, span(half * chunks + j, LANES)])
             for z in range(depth):
                 target[z, span(j, part), :] = total[span(z, part)].astype(target.dtype)
-    for half, target in enumerate((own_rows, far_rows)):
+    for half in range(2):
         rows = inner[:, span(half, size)].T
         for j in range(branch.shape[1] // LANES):
             total = dot(rows, branch[:, span(j, LANES)])
-            for k in range(count):
-                target[k, span(j, share), :] = total[span(k, share)].astype(target.dtype)
+            if strided:
+                share = size // (depth // 2)
+                carried = share // 2
+                at = slice(chunks * part + j * carried, chunks * part + (j + 1) * carried)
+                for i in range(depth // 2):
+                    z = (index[1] ^ half) * (depth // 2) + i
+                    block = total[span(i, share)]
+                    one, two = block[:carried], block[carried:]
+                    own[z, at, :] = jnp.where(index[1] == 0, one, two)
+                    far[z, at, :] = jnp.where(index[1] == 0, two, one).astype(far.dtype)
+            else:
+                target = rows_out[half]
+                count = target.shape[0]
+                share = size // count
+                for k in range(count):
+                    target[k, span(j, share), :] = total[span(k, share)].astype(target.dtype)
+
+
+def sum_kernel(own, recv, total):
+    total[...] = (own[...] + recv[...].astype(f32)).astype(low)
 
 
 def meet_kernel(index, own, recv, own_rows, recv_rows, total, *rows):
@@ -407,16 +508,14 @@
         row[...] = (own_rows[at] + recv_rows[at].astype(f32)).astype(low)
 
 
-def layout_kernel(count, index, total, *refs):
+def layout_kernel(index, total, gains, far_gains, *refs):
     *rows, out = refs
     at = total.shape[1]
+    end = at + rows[0].shape[0]
     out[:, :at, :] = total[...]
-    while rows:
-        group, rows = rows[:count], rows[count:]
-        size = group[0].shape[0]
-        for k, row in enumerate(group):
-            out[index[0] ^ k, at : at + size, :] = row[...]
-        at += size
+    for k, row in enumerate(rows):
+        out[index[0] ^ k, at:end, :] = row[...]
+    out[:, end:, :] = (gains[...] + far_gains[...]).astype(low)
 
 
 def shards(
@@ -446,16 +545,23 @@
     key_half = key_weight.shape[2] // (2 * count)
     hidden_half = gate_weight.shape[2] // (2 * count)
     part = query_weight.shape[1]
-    aligned = depth == count
+    aligned = depth == count == 4
     out_share, down_share = query_half // count, hidden_half // count
-    index = piece.astype(jnp.int32).reshape(1)
+    index = jnp.stack([piece, core]).astype(jnp.int32)
     chunks = width // LANES
     qkv_rows = 2 * part + GAIN_ROWS
     lift_rows = 2 * hidden_half // LANES * part
 
+    own = lax.dynamic_index_in_dim(stream_in[0, 0], core, 0, keepdims=False)
+    other = swap(lax.dynamic_index_in_dim(stream_in[0, 0], 1 - core, 0, keepdims=False))
+    entering = jnp.where(first, own, other)
+    cotangent = jnp.where(first, other, own)
+
+    entering_pieces = hops(entering)
+
     where = jnp.stack([piece, core]).astype(jnp.int32)
 
-    def cut(kernel, weights, constants, size):
+    def cut(kernel, weights, constants, size, after=None):
         def half(i, where):
             return jnp.where(i == 0, 1 - where[1], where[1])
 
@@ -465,9 +571,18 @@
         def shares(i, where):
             return 0, half(i, where) * count + where[0], 0
 
+        def even(i, where):
+            return 0, 0, half(i, where) * 2
+
+        def odd(i, where):
+            return 0, 0, half(i, where) * 2 + 1
+
+        def carried(i, where):
+            return 0, where[0] * 2 + half(i, where), 0
+
+        maps = {"columns": columns, "shares": shares, "even": even, "odd": odd, "carried": carried}
         in_specs = [
-            pl.BlockSpec((1, height, breadth), shares if by_rows else columns)
-            for _, height, breadth, by_rows in weights
+            pl.BlockSpec((1, height, breadth), maps[which]) for _, height, breadth, which in weights
         ]
         in_specs += [pl.BlockSpec(v.shape, lambda i, where: (0, 0)) for v in constants]
         return pl.pallas_call(
@@ -483,7 +598,7 @@
             cost_estimate=pl.CostEstimate(
                 flops=int(3 * FLOPS_PER_US), bytes_accessed=12 * size * LANES, transcendentals=0
             ),
-        )(where, *[weight for weight, *_ in weights], *constants)
+        )(tie(where, after), *[weight for weight, *_ in weights], *constants)
 
     def place_shares(weight, out, at):
         share = weight.shape[1]
@@ -500,13 +615,25 @@
         if aligned:
             place_shares(rest[0], out, qkv_rows)
 
-    def mlp_cut_kernel(where, gate, up, *refs):
-        *rest, out = refs
+    def mlp_cut_kernel(where, gate, up, out):
         both = jnp.concatenate([gate[0].astype(low), up[0].astype(low)], axis=1)
         for j in range(2 * hidden_half // LANES):
             out[0, span(j, part), :] = both[:, span(j, LANES)]
-        if aligned:
-            place_shares(rest[0], out, lift_rows)
+
+    def strided_cut_kernel(where, gate, gate_next, up, up_next, down, out):
+        share = hidden_half // 2
+
+        for c in range(count):
+
+            @pl.when(where[0] == c)
+            def _(c=c):
+                sides = [window(v[0], c * share, share) for v in (gate, gate_next, up, up_next)]
+                both = [side_by_side(*sides[:2], share), side_by_side(*sides[2:], share)]
+                both = jnp.concatenate(both, axis=1).astype(low)
+                for j in range(2 * hidden_half // LANES):
+                    out[0, span(j, part), :] = both[:, span(j, LANES)]
+
+        place_shares(down, out, lift_rows)
 
     gains = (attention_gain[0], mlp_gain[0], query_gain[0], key_gain[0])
     sizes = [gain.shape[0] for gain in gains]
@@ -518,19 +645,25 @@
         mine, other = cuts[1], swap(cuts[0])
         return jnp.where(first, mine, other), jnp.where(first, other, mine)
 
-    weights = [(query_weight, part, query_half, False), (key_weight, part, key_half, False)]
-    weights += [(value_weight, part, key_half, False)]
-    weights += [(out_weight, out_share, width, True)] if aligned else []
+    weights = [(query_weight, part, query_half, "columns"), (key_weight, part, key_half, "columns")]
+    weights += [(value_weight, part, key_half, "columns")]
+    weights += [(out_weight, out_share, width, "shares")] if aligned else []
     size = qkv_rows + (chunks * out_share if aligned else 0)
     cuts = cut(qkv_cut_kernel, weights, [gain_block], size)
     attention_blocks = by_layer(cuts)
     line = jnp.arange(size, dtype=jnp.int32)[:, None]
     gain_rows = (line >= part) & (line < part + GAIN_ROWS)
     attention_blocks = jnp.where(gain_rows, cuts[1], attention_blocks[0]), attention_blocks[1]
-    weights = [(gate_weight, part, hidden_half, False), (up_weight, part, hidden_half, False)]
-    weights += [(down_weight, down_share, width, True)] if aligned else []
-    size = lift_rows + (chunks * down_share if aligned else 0)
-    mlp_blocks = by_layer(cut(mlp_cut_kernel, weights, [], size))
+    if aligned:
+        block = 2 * hidden_half
+        weights = [(gate_weight, part, block, "even"), (gate_weight, part, block, "odd")]
+        weights += [(up_weight, part, block, "even"), (up_weight, part, block, "odd")]
+        weights += [(down_weight, down_share, width, "carried")]
+        size = lift_rows + chunks * down_share
+        mlp_blocks = by_layer(cut(strided_cut_kernel, weights, [], size, entering_pieces[1]))
+    else:
+        weights = [(gate_weight, part, hidden_half, "columns"), (up_weight, part, hidden_half, "columns")]
+        mlp_blocks = by_layer(cut(mlp_cut_kernel, weights, [], lift_rows))
 
     def gathered(block):
         return lax.all_gather(block, "fsdp", axis=0, tiled=False)
@@ -572,14 +705,10 @@
     sine = jnp.concatenate([-sine, sine], axis=-1)
     places = [start[:, None], natural[:, None], natural[None, :]]
 
-    wanted = slots[natural]
+    wanted = slots.reshape(count, rows)
+    wanted = jnp.concatenate(xored([wanted[j] for j in range(count)], piece))
     wanted = ((wanted // rows) ^ piece) * rows + wanted % rows
     chosen = (wanted[:, None] == order[None, :]).astype(low)
-
-    own = lax.dynamic_index_in_dim(stream_in[0, 0], core, 0, keepdims=False)
-    other = swap(lax.dynamic_index_in_dim(stream_in[0, 0], 1 - core, 0, keepdims=False))
-    entering = jnp.where(first, own, other)
-    cotangent = jnp.where(first, other, own)
 
     wide, half_wide = (rows, width), (tokens, width)
     heads_wide, hidden_wide = 2 * query_half, 2 * hidden_half
@@ -589,10 +718,13 @@
         outputs = [(wide, f32), (wide, low)]
         return call(kernel, [*parts, residual, gain], outputs, 2, after=after)
 
-    def add_back(parts, upstream, middle, gain, rounded, after=()):
-        kernel = functools.partial(add_back_kernel, count, rounded)
+    def add_back(parts, upstream, middle, gain, rounded, gains=(), after=()):
+        packs = aligned and len(gains) > 0
+        kernel = functools.partial(add_back_kernel, count, rounded, packs)
         outputs = [(wide, f32), (wide, low), ((1, width), f32)]
-        return call(kernel, [*parts, upstream, middle, gain], outputs, 2, after=after)
+        outputs += [((depth, GAIN_ROWS, LANES), f32)] if packs else []
+        operands = [*parts, upstream, middle, gain] + (list(gains) if packs else [])
+        return call(kernel, operands, outputs, 2, after=after)
 
     def attention_forward(pieces, weights, found, raw_rows, after=()):
         kernel = functools.partial(attention_forward_kernel, count, part, raw_rows)
@@ -604,10 +736,10 @@
         operands += [*weights, cosine, sine, found[2], found[3], *places]
         return call(kernel, operands, outputs, 12, [((tokens, 2 * key_half), low)], after=after)
 
-    def rows_product(left, shares, dealt=False, after=()):
-        kernel = functools.partial(rows_kernel, count, not aligned, dealt)
+    def rows_product(form, left, given, dealt=False, after=()):
+        kernel = functools.partial(rows_kernel, count, form, dealt)
         outputs = [(wide, low)] * count + [((left.shape[1], width), low)]
-        operands = [left] + ([chosen] if dealt else []) + [*shares]
+        operands = [left] + ([chosen] if dealt else []) + [*given]
         *parts, whole = call(kernel, operands, outputs, 4, scalars=[index], after=after)
         return parts, whole
 
@@ -621,12 +753,23 @@
             outputs += [(wide, low)]
         return call(kernel, [*operands, *weights], outputs, 6, after=after)
 
-    def mlp_backward(pieces, weights, down, kept, after=()):
-        kernel = functools.partial(mlp_backward_kernel, count, part)
+    def mlp_forward(pieces, weights, form, down):
+        kernel = functools.partial(mlp_forward_kernel, count, part, form)
+        outputs = [(half_wide, low)] + [((tokens, hidden_wide), f32)] * 2
+        outputs += [((tokens, hidden_wide), low)] + [(wide, low)] * count
+        outputs += [((hidden_wide, width), low)]
+        operands = [*pieces, *weights] + ([] if form == "strided" else [down])
+        *results, whole = call(kernel, operands, outputs, 8, scalars=[index])
+        return results[:4], results[4:], whole
+
+    def mlp_backward(pieces, weights, form, down, kept, after=()):
+        kernel = functools.partial(mlp_backward_kernel, count, part, form)
         outputs = [(wide, low)] * count + [(half_wide, low), ((tokens, 2 * hidden_wide), low)]
-        operands = [*pieces, *weights, down, kept[1], kept[2]]
-        *parts, branch, both = call(kernel, operands, outputs, 9, after=after)
-        return parts, branch, both
+        outputs += [((hidden_wide, width), low)]
+        operands = [*pieces, *weights, kept[1], kept[2]] + ([] if form == "strided" else [down])
+        results = call(kernel, operands, outputs, 6, scalars=[index], after=after)
+        parts, (branch, both, whole) = results[:count], results[count:]
+        return parts, branch, both, whole
 
     def attention_backward(pieces, weights, out, found, kept, dealt=False, after=()):
         kernel = functools.partial(attention_backward_kernel, count, part, dealt)
@@ -640,24 +783,28 @@
         operands += [*weights, out, cosine, sine, found[2], found[3], *places]
         operands += [raw, queries, keys, spread]
         results = call(
-            kernel, operands, outputs, 18, scratch, after=after, limit=VMEM_LIMIT
+            kernel, operands, outputs, 18, scratch, after=after
         )
         parts, (branch, grad_raw, query, key, *rest) = results[:count], results[count:]
         return (parts, branch, grad_raw, (query, key), *rest)
 
-    def weight_grads(left, grads, inner, branch, after=()):
-        kernel = functools.partial(weight_grads_kernel, part)
-        shape = (depth, grads.shape[1] // (2 * LANES) * part, LANES)
+    def weight_grads(left, grads, inner, branch, strided=False, after=()):
+        kernel = functools.partial(weight_grads_kernel, part, strided)
+        size = grads.shape[1] // (2 * LANES) * part
         row_shape = (count, inner.shape[1] // (2 * count) * chunks, LANES)
-        outputs = [(shape, f32), (shape, low), (row_shape, f32), (row_shape, low)]
+        if strided:
+            size += row_shape[1]
+        outputs = [((depth, size, LANES), f32), ((depth, size, LANES), low)]
+        outputs += [] if strided else [(row_shape, f32), (row_shape, low)]
         operands = [left, grads, inner, branch]
-        return call(kernel, operands, outputs, 6, [((width, tokens), low)], after=after)
+        scratch = [((width, tokens), low)]
+        return call(kernel, operands, outputs, 6, scratch, scalars=[index], after=after)
 
     if not aligned:
         outs, downs = whole_rows(out_weight, query_half), whole_rows(down_weight, hidden_half)
 
-    def arrived(value, pieces):
-        own = tie(value, pieces)
+    def arrived(value, after):
+        own = tie(value, after)
         return [own, swap(own)]
 
     def moving_rows(weights, first_row, whole):
@@ -666,9 +813,11 @@
     def with_far(shares):
         return [*shares, *map(swap, shares)] if aligned else shares
 
-    pieces = hops(entering)
+    out_form, down_form = ("shares", "strided") if aligned else ("whole", "whole")
+    pieces = entering_pieces
     cotangents = hops(tie(cotangent, pieces[1]))
-    qkv_first = arrived(gathered(attention_blocks[0]), (pieces, cotangents))
+    early = pieces, cotangents, mlp_blocks, attention_blocks[1], chosen, cosine, sine, places
+    qkv_first = arrived(gathered(attention_blocks[0]), early)
     found_own, found_far = split_gains(qkv_first[0]), split_gains(qkv_first[1])
     found_first = [jnp.where(first, own, far) for own, far in zip(found_own, found_far)]
     found_last = [jnp.where(first, far, own) for own, far in zip(found_own, found_far)]
@@ -676,14 +825,13 @@
     kept_attention_first = attention_forward(pieces, qkv_first, found_first, True)
     kept_attention_first, shares = beside(kept_attention_first, shares)
     *kept_attention_first, dealt_entering = kept_attention_first
-    parts, out_first = rows_product(kept_attention_first[4], with_far(shares))
+    parts, out_first = rows_product(out_form, kept_attention_first[4], with_far(shares))
     middle_first, normed = add(met(parts), entering, found_first[1], False)
     pieces = hops(normed)
     lift_first = arrived(gathered(mlp_blocks[0]), pieces)
-    shares = moving_rows(lift_first, lift_rows, None if aligned else downs[0])
-    kept_mlp_first = lift_forward(pieces, lift_first)
-    kept_mlp_first, shares = beside(kept_mlp_first, shares)
-    parts, down_first = rows_product(kept_mlp_first[3], with_far(shares))
+    kept_mlp_first, parts, down_first = mlp_forward(
+        pieces, lift_first, down_form, None if aligned else downs[0]
+    )
 
     hidden_last, normed = add(met(parts), middle_first, found_last[0], True)
     pieces = hops(normed)
@@ -691,15 +839,11 @@
     shares = moving_rows(qkv_last, qkv_rows, None if aligned else outs[1])
     kept_attention_last = attention_forward(pieces, qkv_last, found_last, False)
     kept_attention_last, shares = beside(kept_attention_last, shares)
-    parts, out_last = rows_product(kept_attention_last[4], with_far(shares))
+    parts, out_last = rows_product(out_form, kept_attention_last[4], with_far(shares))
     middle_last, sent = add(met(parts), hidden_last, found_last[1], False, True)
     pieces = hops(sent)
     lift_last = arrived(gathered(mlp_blocks[1]), pieces)
-    shares = moving_rows(lift_last, lift_rows, None if aligned else downs[1])
-    kept_mlp_last = lift_forward(pieces, lift_last, found_last[1])
-    kept_mlp_last, shares = beside(kept_mlp_last, shares)
-    *kept_mlp_last, dealt_middle = kept_mlp_last
-    last_parts, down_last = rows_product(kept_mlp_last[3], with_far(shares), True)
+    *kept_mlp_last, dealt_middle = lift_forward(pieces, lift_last, found_last[1])
 
     def meet(grads, swapped):
         own, far, own_rows, far_rows = grads
@@ -711,14 +855,13 @@
         total, *rows_by = call(meet_kernel, operands, outputs, 4, scalars=[index])
         return total, rows_by
 
-    def laid_out(total, *rows_by):
+    def laid_out(total, rows_by, packed):
         if not aligned:
             return total
-        size = total.shape[1] + sum(rows[0].shape[0] for rows in rows_by)
+        size = total.shape[1] + rows_by[0].shape[0] + GAIN_ROWS
         outputs = [((depth, size, LANES), low)]
-        operands = [total] + [row for rows in rows_by for row in rows]
-        kernel = functools.partial(layout_kernel, count)
-        return call(kernel, operands, outputs, 3, scalars=[index])[0]
+        operands = [total, packed[0], swap(packed[0]), *rows_by]
+        return call(layout_kernel, operands, outputs, 3, scalars=[index])[0]
 
     def gains_reduced(from_first, from_last):
         def by_pack(gains):
@@ -752,95 +895,112 @@
         own = jnp.stack(pieces)
         return own, lax.ppermute(own, "section", [(1 - layer, layer)])
 
-    def meet_beside(grads, swapped, sent):
-        return beside(meet(grads, swapped), hops(sent))
-
-    parts, branch, both = mlp_backward(cotangents, lift_last, down_last, kept_mlp_last)
-    mlp_grads = weight_grads(kept_mlp_last[0], both, kept_mlp_last[3], branch)
-    mlp_grads, parts = beside(mlp_grads, met(parts))
-    swapped = swap(mlp_grads[1]), swap(mlp_grads[3])
+    def mlp_meet(grads, swapped):
+        if aligned:
+            return call(sum_kernel, [grads[0], swapped[0]], [(grads[0].shape, low)], 2)
+        return meet(grads, swapped)
+
+    down_whole = None if aligned else downs[1]
+    parts, branch, both, whole = mlp_backward(cotangents, lift_last, down_form, down_whole, kept_mlp_last)
+    mlp_grads = weight_grads(kept_mlp_last[0], both, kept_mlp_last[3], branch, aligned)
+    last_parts, unused = rows_product("whole", kept_mlp_last[3], [whole], True, after=[both])
+    (mlp_grads, last_parts), parts = beside((mlp_grads, last_parts), met(parts))
+    swapped = [swap(v) for v in mlp_grads[1::2]]
     grad, sent, mlp_gain = add_back(parts, cotangent, middle_last, found_last[1], False)
-    (total, down_rows), pieces = meet_beside(mlp_grads, swapped, sent)
-
-    results = attention_backward(pieces, qkv_last, out_last, found_last, kept_attention_last, after=[total])
-    moving = met(tie(last_parts, pieces[1])), met_rows(down_rows)
-    results, (last_parts, moved) = beside(results, moving)
+    (total, *down_rows), pieces = beside(mlp_meet(mlp_grads, swapped), hops(sent))
+    mlp_last = scattered(total)
+
+    results = attention_backward(
+        pieces, qkv_last, out_last, found_last, kept_attention_last, after=[mark(total)]
+    )
+    results, last_parts = beside(results, met(tie(last_parts, pieces[1])))
     parts, branch, grad_raw, head_gains = results
     last = dealt_middle.astype(f32)
     for value in last_parts:
         last = last + value.astype(f32)
     last = last.astype(low)
-    operand = laid_out(total, moved)
     attention_grads = weight_grads(kept_attention_last[0], grad_raw, kept_attention_last[4], branch)
-    (attention_grads, operand), parts = beside((attention_grads, operand), met(parts))
-    mlp_last = scattered(operand)
+    attention_grads, parts = beside(attention_grads, met(parts))
     swapped = swap(attention_grads[1]), swap(attention_grads[3])
-    grad, sent, gain = add_back(parts, grad, hidden_last, found_last[0], True)
+    grad, sent, gain, *packed = add_back(
+        parts, grad, hidden_last, found_last[0], True, (mlp_gain, *head_gains)
+    )
     gains_last = (gain, mlp_gain, *head_gains)
-    down_grad_last = None if aligned else rows_fallback(down_rows)
-    (total, out_rows), pieces = meet_beside(attention_grads, swapped, sent)
-
-    results = mlp_backward(pieces, lift_first, down_first, kept_mlp_first, after=[total])
-    results, moved = beside(results, met_rows(out_rows))
-    parts, branch, both = results
-    operand = laid_out(total, moved)
-    mlp_grads = weight_grads(kept_mlp_first[0], both, kept_mlp_first[3], branch)
-    (mlp_grads, operand, mlp_last), parts = beside((mlp_grads, operand, mlp_last), met(parts))
+    down_grad_last = None if aligned else rows_fallback(*down_rows)
+    total, out_rows = meet(attention_grads, swapped)
+    moved, pieces = beside(met_rows(out_rows), hops(sent))
+    operand, mlp_last = beside(laid_out(total, moved, packed), mlp_last)
     attention_last = scattered(operand)
+
+    near = [hop(mlp_last, k) for k in range(1, count - 1)]
+    results = mlp_backward(
+        pieces, lift_first, "whole", down_first, kept_mlp_first, after=[mark(operand, mlp_last)]
+    )
+    parts, branch, both, unused = results
+    mlp_grads = weight_grads(kept_mlp_first[0], both, kept_mlp_first[3], branch, aligned)
+    mlp_grads, parts = beside(mlp_grads, met(parts))
     out_grad_last = None if aligned else rows_fallback(out_rows)
-    swapped = swap(mlp_grads[1]), swap(mlp_grads[3])
+    swapped = [swap(v) for v in mlp_grads[1::2]]
     grad, sent, mlp_gain = add_back(parts, grad, middle_first, found_first[1], False)
-    (total, down_rows), pieces = meet_beside(mlp_grads, swapped, sent)
-
+    (total, *down_rows), pieces = beside(mlp_meet(mlp_grads, swapped), hops(sent))
+    total, attention_last = beside(total, attention_last)
+    mlp_first = scattered(total)
+
+    attention_last = hops(tie(attention_last, pieces[1]))
     results = attention_backward(
-        pieces, qkv_first, out_first, found_first, kept_attention_first, True, after=[total]
+        pieces,
+        qkv_first,
+        out_first,
+        found_first,
+        kept_attention_first,
+        True,
+        after=[mark(total, attention_last[0])],
     )
-    mlp_last = tie(mlp_last, pieces[1])
-    near = [hop(mlp_last, k) for k in range(1, count - 1)]
-    results, (near, moved) = beside(results, (near, met_rows(down_rows)))
+    results, near, attention_last = lax.optimization_barrier((results, near, attention_last))
     parts, branch, grad_raw, head_gains, dealt_branch = results
-    operand = laid_out(total, moved)
-    mlp_first = scattered(operand)
     attention_grads = weight_grads(kept_attention_first[0], grad_raw, kept_attention_first[4], branch)
-    (attention_grads, _), parts = beside((attention_grads, operand), met(parts))
+    attention_grads, parts = beside(attention_grads, met(parts))
     swapped = swap(attention_grads[1]), swap(attention_grads[3])
-    down_grad_first = None if aligned else rows_fallback(down_rows)
-    total, out_rows = meet(attention_grads, swapped)
+    unused, grad, gain, *packed = add_back(
+        parts, dealt_branch, dealt_entering, found_first[0], True, (mlp_gain, *head_gains)
+    )
+    down_grad_first = None if aligned else rows_fallback(*down_rows)
+    (total, out_rows), mlp_first = beside(meet(attention_grads, swapped), mlp_first)
+    mlp_first = hops(mlp_first)
     moved = met_rows(out_rows)
-    operand = laid_out(total, moved)
+    operand = laid_out(total, moved, packed)
     out_grad_first = None if aligned else rows_fallback(out_rows)
-    attention_last = hops_split(tie(attention_last, parts))
-    unused, grad, gain = add_back(
-        parts, dealt_branch, dealt_entering, found_first[0], True, after=[operand]
-    )
     gains_first = (gain, mlp_gain, *head_gains)
-    sums = gains_reduced(gains_first, gains_last)
-    mlp_last = [mlp_last, *near, hop(tie(mlp_last, operand), count - 1)]
-    mlp_first, operand = beside(mlp_first, operand)
     attention_first = scattered(operand)
-    mlp_first, (grad, sums, mlp_last, attention_last) = beside(
-        mlp_first, (grad, sums, mlp_last, attention_last)
-    )
-    mlp_first = hops_split(mlp_first)
+    point = mark(operand)
+    sums = None if aligned else gains_reduced(gains_first, gains_last)
+    mlp_last = [mlp_last, *near, hop(tie(mlp_last, point), count - 1)]
     mlp_last, attention_last = returned(mlp_last, 1), returned(attention_last, 1)
-    attention_first = hops_split(tie(attention_first, mlp_first))
+    attention_first = hops(tie(attention_first, mlp_first))
     mlp_first = returned(mlp_first, 0)
-
-    def settle(kernel, from_first, from_last, outputs):
+    own = jnp.where(first, grad, last)
+    other = swap(jnp.where(first, last, grad))
+    boundary = jnp.where(first, jnp.stack([own, other]), jnp.stack([other, own]))
+
+    def settle(kernel, from_first, from_last, outputs, at_once=1, after=()):
         size = from_first[0].shape[1]
 
         def block_of(layer):
             def at(i, where):
-                return jnp.where(where[1] == layer, i ^ where[0], 0), 0, 0
-
-            return pl.BlockSpec((1, size, LANES), at)
+                return jnp.where(where[1] == layer, i ^ (where[0] // at_once), 0), 0, 0
+
+            return pl.BlockSpec((at_once, size, LANES), at)
+
+        def body(where, *refs):
+            kernel(where, *refs[:4], *refs[4 + len(after) :])
 
         return pl.pallas_call(
-            kernel,
+            body,
             grid_spec=pltpu.PrefetchScalarGridSpec(
                 num_scalar_prefetch=1,
-                grid=(count,),
-                in_specs=[block_of(0), block_of(0), block_of(1), block_of(1)],
+                grid=(count // at_once,),
+                in_specs=[block_of(0), block_of(0), block_of(1), block_of(1)]
+                + [pl.BlockSpec(memory_space=pl.ANY)] * len(after),
                 out_specs=[
                     pl.BlockSpec(block, functools.partial(lambda at, i, where: at(i), at))
                     for _, block, at in outputs
@@ -851,7 +1011,7 @@
             cost_estimate=pl.CostEstimate(
                 flops=0, bytes_accessed=12 * count * size * LANES, transcendentals=0
             ),
-        )(where, *from_first, *from_last)
+        )(where, *from_first, *from_last, *after)
 
     def halves_of(where, blocks, body):
         @pl.when(where[1] == 0)
@@ -870,20 +1030,46 @@
             out[half, :, span(j, LANES)] = block[0, at + j * share : at + (j + 1) * share, :].astype(f32)
 
     def mlp_settle_kernel(where, *refs):
-        blocks, (gate, up, *down) = refs[:4], refs[4:]
+        blocks, (gate, up) = refs[:4], refs[4:]
 
         def body(half, block):
             both = [block[0, span(j, part), :].astype(f32) for j in range(2 * hidden_half // LANES)]
             both = jnp.concatenate(both, axis=1)
             gate[:, span(half, hidden_half)] = both[:, :hidden_half]
             up[:, span(half, hidden_half)] = both[:, hidden_half:]
-            if aligned:
-                place_rows(block, lift_rows, half, down[0])
+
+        halves_of(where, blocks, body)
+
+    def strided_settle_kernel(where, *refs):
+        blocks, (gate, up, down) = refs[:4], refs[4:]
+        share = hidden_half // 2
+        step = pl.program_id(0)
+
+        def body(half, block):
+            pair = []
+            for side in range(2):
+                at = (where[0] % 2) ^ side
+                both = [block[at, span(j, part), :].astype(f32) for j in range(2 * hidden_half // LANES)]
+                pair.append(jnp.concatenate(both, axis=1))
+                for j in range(chunks):
+                    rows_at = slice(lift_rows + j * down_share, lift_rows + (j + 1) * down_share)
+                    down[2 * side + half, :, span(j, LANES)] = block[at, rows_at, :].astype(f32)
+            for target, start in ((gate, 0), (up, hidden_half)):
+                for i in range(2):
+                    sides = [window(v[:, start : start + hidden_half], i * share, share) for v in pair]
+                    to = (2 * half + i) * 2 * hidden_half + step * hidden_half
+                    to = pl.ds(pl.multiple_of(to, 128), hidden_half)
+                    target[:, to] = side_by_side(*sides, share)
 
         halves_of(where, blocks, body)
 
     def attention_settle_kernel(where, *refs):
         blocks, (query, key, value, *out) = refs[:4], refs[4:]
+        if aligned:
+
+            @pl.when(pl.program_id(0) == 0)
+            def _():
+                out[1][...] = jnp.zeros_like(out[1])
 
         def body(half, block):
             query[:, span(half, query_half)] = block[0, :part, :].astype(f32)
@@ -892,6 +1078,8 @@
             value[:, span(half, key_half)] = both[:, key_half:]
             if aligned:
                 place_rows(block, 2 * part, half, out[0])
+                if half == 0:
+                    out[1][...] += block[0, 2 * part + chunks * out_share :, :].astype(f32)
 
         halves_of(where, blocks, body)
 
@@ -901,14 +1089,32 @@
     def row_output(size):
         return ((2, size, width), (2, size // count, width), lambda i: (0, i, 0))
 
-    outputs = [column_output(hidden_half)] * 2 + ([row_output(hidden_half)] if aligned else [])
-    settled = settle(mlp_settle_kernel, mlp_first, mlp_last, outputs)
+    if aligned:
+        whole_columns = (part, 2 * count * hidden_half)
+        outputs = [(whole_columns, whole_columns, lambda i: (0, 0))] * 2
+        outputs += [((2 * count, down_share, width), (count, down_share, width), lambda i: (i, 0, 0))]
+        settled = settle(strided_settle_kernel, mlp_first, mlp_last, outputs, 2, [other])
+    else:
+        settled = settle(mlp_settle_kernel, mlp_first, mlp_last, [column_output(hidden_half)] * 2)
     (grad_gate, grad_up, *grad_down), attention_first = beside(settled, attention_first)
     outputs = [column_output(query_half)] + [column_output(key_half)] * 2
-    outputs += [row_output(query_half)] if aligned else []
+    if aligned:
+        outputs += [row_output(query_half)]
+        outputs += [((GAIN_ROWS, LANES), (GAIN_ROWS, LANES), lambda i: (0, 0))]
     grad_query, grad_key, grad_value, *grad_out = settle(
         attention_settle_kernel, returned(attention_first, 0), attention_last, outputs
     )
+    if aligned:
+        sums = grad_out[1]
+        at = lax.axis_index("fsdp") * sizes[2]
+        head_sums = [lax.dynamic_slice_in_dim(sums[2:3], at + k * HEAD_DIM, sizes[2], 1) for k in range(2)]
+        split = [sums[0:1], sums[1:2], *head_sums]
+    else:
+        split, at = [], 0
+        for size in sizes:
+            split.append(sums[:, at : at + size])
+            at += size
+
     if aligned:
         grad_out, grad_down = grad_out[0].reshape(-1, width), grad_down[0].reshape(-1, width)
     else:
@@ -917,14 +1123,6 @@
             own = jnp.where(first, one, two).astype(f32)
             pair.append(own + swap(jnp.where(first, two, one)).astype(f32))
         grad_out, grad_down = pair
-    split, at = [], 0
-    for size in sizes:
-        split.append(sums[:, at : at + size])
-        at += size
-
-    own = jnp.where(first, grad, last)
-    other = swap(jnp.where(first, last, grad))
-    boundary = jnp.where(first, jnp.stack([own, other]), jnp.stack([other, own]))
     return (
         boundary[None, None],
         split[0],

time: 578 us -> 520 us (0.90)
  local copies, waits for them, and re-layouts: 74.1 us -> 36.6 us
  starting transfers between devices: 132 us -> 103 us
  waiting for transfers between devices: 190 us -> 207 us
  other arithmetic: 26.9 us -> 16 us
    ppermute x96 -> x72, starting transfers between devices: 112 us -> 86.9 us  [hop(): return lax.ppermute(value, 'ctx', [(i, i ^ step) for i in range(count)])]
    unnamed x295 -> x278, local copies, waits for them, and re-layouts: 54.6 us -> 30.3 us
    reduce_scatter x4, waiting for transfers between devices: 14.4 us -> 0.01 us  [scattered(): return lax.psum_scatter(operand, 'fsdp', scatter_dimension=0, tiled=False)]
    ppermute x96 -> x72, waiting for transfers between devices: 150 us -> 161 us  [hop(): return lax.ppermute(value, 'ctx', [(i, i ^ step) for i in range(count)])]
    all_gather x4, waiting for transfers between devices: 16.9 us -> 26.4 us  [gathered(): return lax.all_gather(block, 'fsdp', axis=0, tiled=False)]
    ppermute x33 -> x24, waiting for transfers between devices: 7.82 us -> 16.1 us  [swap(): return lax.ppermute(value, 'section', [(0, 1), (1, 0)])]
    pallas_call x35 -> x33, Pallas kernels: 110 us -> 111 us  [call(): pl.pallas_call(body, out_shape=shapes, in_specs=[anywhere] * skipped + [s...]
  transfers between devices with their start and end apart: 144 -> 108, of which waited for: 63 -> 50; matrix products, arithmetic and copies ran while one was open for 7% -> 4% of each run, Pallas kernels for 20% -> 23%
where the time goes in v4:
time: 520 us; the launch traced here: 512 us
  waiting for transfers between devices  207 us (40%)
  Pallas kernels  132 us (25%)
  starting transfers between devices  103 us (20%)
  local copies, waits for them, and re-layouts  36.6 us (7%)
  between operations  16.4 us (3%)
  other arithmetic  16 us (3%)
    ppermute x72, waiting for transfers between devices, hop(): return lax.ppermute(value, 'ctx', [(i, i ^ step) for i in range(count)])  161 us
    pallas_call x33, Pallas kernels, call(): pl.pallas_call(body, out_shape=shapes, in_specs=[anywhere] * skipped + [s...  111 us
    ppermute x72, starting transfers between devices, hop(): return lax.ppermute(value, 'ctx', [(i, i ^ step) for i in range(count)])  86.9 us
    unnamed x278, local copies, waits for them, and re-layouts  30.3 us
    all_gather x4, waiting for transfers between devices, gathered(): return lax.all_gather(block, 'fsdp', axis=0, tiled=False)  26.4 us
    ppermute x24, waiting for transfers between devices, swap(): return lax.ppermute(value, 'section', [(0, 1), (1, 0)])  16.1 us
    pallas_call x2, Pallas kernels, settle(): pl.pallas_call(body, grid_spec=pltpu.PrefetchScalarGridSpec(num_scalar_pr...  14 us
  transfers between devices with their start and end apart: 108, of which 50 were waited for; matrix products, arithmetic and copies ran while one was open for 4% of the time, Pallas kernels for 23%

profile of v4, /device:TPU:0, one launch (start us, length us, event | category | flops | bytes accessed | tf_op | source)
XLA Modules:
  0.0 511.9 jit_solution(12654799418137995254)
XLA Ops:
  22.2 6.8 %collective-permute-done.1.refs_1_ = bf16[128,1024]{1,0:T(8,128)(2,1)S(1)} collective-permute-done((bf16[128,1024]{1,0:T(8,128)(2,1)S(1)}, bf16[128,1024]{1,0:T(8,128)(2,1)S(1)}, u32[]{:S(2)}, u32[]{:S(2)}) %collective-permute-start.1) | collective-permute-done | bytes 262176 | tf_op jit(solution)/shard_map/ppermute | solution.py:29
  44.5 6.7 %collective-permute-done.2.refs_2_ = bf16[128,1024]{1,0:T(8,128)(2,1)S(1)} collective-permute-done((bf16[128,1024]{1,0:T(8,128)(2,1)S(1)}, bf16[128,1024]{1,0:T(8,128)(2,1)S(1)}, u32[]{:S(2)}, u32[]{:S(2)}) %collective-permute-start.2) | collective-permute-done | bytes 262176 | tf_op jit(solution)/shard_map/ppermute | solution.py:29
  52.8 9.4 %collective-permute-done.6.refs_3_ = bf16[128,1024]{1,0:T(8,128)(2,1)S(1)} collective-permute-done((bf16[128,1024]{1,0:T(8,128)(2,1)S(1)}, bf16[128,1024]{1,0:T(8,128)(2,1)S(1)}, u32[]{:S(2)}, u32[]{:S(2)}) %collective-permute-start.6) | collective-permute-done | bytes 262176 | tf_op jit(solution)/shard_map/ppermute | solution.py:29
  73.9 8.5 %shard_map.231 = (bf16[512,1024]{1,0:T(8,128)(2,1)S(1)}, f32[512,1024]{1,0:T(8,128)S(1)}, bf16[512,512]{1,0:T(8,128)(2,1)S(1)}, bf16[512,256]{1,0:T(8,128)(2,1)S...) custom-call(bf16[128,1024]{1,0:T(8,128)(2,1)S(1)} %get-tuple-element.526.refs_0_.refs_4_, ...), custom_call_target="tpu_custom_call" | custom-call | flops 13799999488 | bytes 10046464 | tf_op jit(solution)/shard_map/pallas_call | solution.py:129
  91.7 5.6 %collective-permute-done.17.refs_1_ = bf16[128,1024]{1,0:T(8,128)(2,1)S(1)} collective-permute-done((bf16[128,1024]{1,0:T(8,128)(2,1)S(1)}, bf16[128,1024]{1,0:T(8,128)(2,1)S(1)}, u32[]{:S(2)}, u32[]{:S(2)}) %collective-permute-start.17) | collective-permute-done | bytes 262176 | tf_op jit(solution)/shard_map/ppermute | solution.py:29
  97.3 6.7 %collective-permute-done.18.refs_2_ = bf16[128,1024]{1,0:T(8,128)(2,1)S(1)} collective-permute-done((bf16[128,1024]{1,0:T(8,128)(2,1)S(1)}, bf16[128,1024]{1,0:T(8,128)(2,1)S(1)}, u32[]{:S(2)}, u32[]{:S(2)}) %collective-permute-start.18) | collective-permute-done | bytes 262176 | tf_op jit(solution)/shard_map/ppermute | solution.py:29
  108.6 6.1 %all-gather.11.cloned.1.call-done = bf16[4608,256]{1,0:T(8,128)(2,1)} async-done(((bf16[1152,256]{1,0:T(8,128)(2,1)}), bf16[4608,256]{1,0:T(8,128)(2,1)}) %all-gather.11.cloned.1.call-update) | async-done | bytes 2359312 | tf_op jit(solution)/shard_map/all_gather | solution.py:669
  126.1 5.6 %shard_map.235 = (bf16[512,1024]{1,0:T(8,128)(2,1)S(1)}, f32[512,768]{1,0:T(8,128)S(1)}, f32[512,768]{1,0:T(8,128)S(1)}, bf16[512,768]{1,0:T(8,128)(2,1)S(1)}, b...) custom-call(s32[2]{0:T(128)S(1)} %copy-done.8, ...), custom_call_target="tpu_custom_call" | custom-call | flops 9200000000 | bytes 13369344 | tf_op jit(solution)/shard_map/pallas_call | solution.py:129
  135.3 5.7 %collective-permute-done.24.refs_1_ = bf16[128,1024]{1,0:T(8,128)(2,1)S(1)} collective-permute-done((bf16[128,1024]{1,0:T(8,128)(2,1)S(1)}, bf16[128,1024]{1,0:T(8,128)(2,1)S(1)}, u32[]{:S(2)}, u32[]{:S(2)}) %collective-permute-start.24) | collective-permute-done | bytes 262176 | tf_op jit(solution)/shard_map/ppermute | solution.py:29
  150.5 7.2 %all-gather.13.cloned.1.call-done = bf16[3136,256]{1,0:T(8,128)(2,1)} async-done(((bf16[784,256]{1,0:T(8,128)(2,1)}), bf16[3136,256]{1,0:T(8,128)(2,1)}) %all-gather.13.cloned.1.call-update) | async-done | bytes 1605648 | tf_op jit(solution)/shard_map/all_gather | solution.py:669
  167.2 8.3 %shard_map.237 = (bf16[512,1024]{1,0:T(8,128)(2,1)S(1)}, f32[512,1024]{1,0:T(8,128)S(1)}, bf16[512,512]{1,0:T(8,128)(2,1)S(1)}, bf16[512,256]{1,0:T(8,128)(2,1)S...) custom-call(bf16[128,1024]{1,0:T(8,128)(2,1)S(1)} %get-tuple-element.296.refs_0_, ...), custom_call_target="tpu_custom_call" | custom-call | flops 13799999488 | bytes 9255936 | tf_op jit(solution)/shard_map/pallas_call | solution.py:129
  184.1 5.6 %collective-permute-done.38.refs_1_ = bf16[128,1024]{1,0:T(8,128)(2,1)S(1)} collective-permute-done((bf16[128,1024]{1,0:T(8,128)(2,1)S(1)}, bf16[128,1024]{1,0:T(8,128)(2,1)S(1)}, u32[]{:S(2)}, u32[]{:S(2)}) %collective-permute-start.38) | collective-permute-done | bytes 262176 | tf_op jit(solution)/shard_map/ppermute | solution.py:29
  189.8 5.3 %collective-permute-done.39.refs_2_ = bf16[128,1024]{1,0:T(8,128)(2,1)S(1)} collective-permute-done((bf16[128,1024]{1,0:T(8,128)(2,1)S(1)}, bf16[128,1024]{1,0:T(8,128)(2,1)S(1)}, u32[]{:S(2)}, u32[]{:S(2)}) %collective-permute-start.39) | collective-permute-done | bytes 262176 | tf_op jit(solution)/shard_map/ppermute | solution.py:29
  199.5 13.1 %all-gather.15.cloned.1.call-done = bf16[4608,256]{1,0:T(8,128)(2,1)} async-done(((bf16[1152,256]{1,0:T(8,128)(2,1)}), bf16[4608,256]{1,0:T(8,128)(2,1)}) %all-gather.15.cloned.1.call-update) | async-done | bytes 2359312 | tf_op jit(solution)/shard_map/all_gather | solution.py:669
  263.5 24.1 %shard_map.248 = (bf16[128,1024]{1,0:T(8,128)(2,1)S(1)}, bf16[128,1024]{1,0:T(8,128)(2,1)S(1)}, bf16[128,1024]{1,0:T(8,128)(2,1)S(1)}, bf16[128,1024]{1,0:T(8,12...) custom-call(f32[8,128]{1,0:T(8,128)S(1)} %shard_map.247.refs_0_, ...), custom_call_target="tpu_custom_call" | custom-call | flops 20700000256 | bytes 11878400 | tf_op jit(solution)/shard_map/pallas_call | solution.py:129
  328.1 6.1 %shard_map.254 = (bf16[128,1024]{1,0:T(8,128)(2,1)S(1)}, bf16[128,1024]{1,0:T(8,128)(2,1)S(1)}, bf16[128,1024]{1,0:T(8,128)(2,1)S(1)}, bf16[128,1024]{1,0:T(8,12...) custom-call(f32[8,128]{1,0:T(8,128)S(1)} %shard_map.253.refs_0_, ...), custom_call_target="tpu_custom_call" | custom-call | flops 6899999744 | bytes 15728640 | tf_op jit(solution)/shard_map/pallas_call | solution.py:129
  358.2 6.3 %collective-permute-done.72.refs_3_ = bf16[128,1024]{1,0:T(8,128)(2,1)S(1)} collective-permute-done((bf16[128,1024]{1,0:T(8,128)(2,1)S(1)}, bf16[128,1024]{1,0:T(8,128)(2,1)S(1)}, u32[]{:S(2)}, u32[]{:S(2)}) %collective-permute-start.72) | collective-permute-done | bytes 262176 | tf_op jit(solution)/shard_map/ppermute | solution.py:29
  369.4 16.0 %shard_map.259 = (bf16[128,1024]{1,0:T(8,128)(2,1)S(1)}, bf16[128,1024]{1,0:T(8,128)(2,1)S(1)}, bf16[128,1024]{1,0:T(8,128)(2,1)S(1)}, bf16[128,1024]{1,0:T(8,12...) custom-call(f32[8,128]{1,0:T(8,128)S(1)} %shard_map.258.refs_0_, ...), custom_call_target="tpu_custom_call" | custom-call | flops 20700000256 | bytes 12664832 | tf_op jit(solution)/shard_map/pallas_call | solution.py:129
  385.5 8.1 %collective-permute-done.77 = bf16[784,256]{1,0:T(8,128)(2,1)S(1)} collective-permute-done((bf16[784,256]{1,0:T(8,128)(2,1)S(1)}, bf16[784,256]{1,0:T(8,128)(2,1)S(1)}, u32[]{:S(2)}, u32[]{:S(2)}) %collective-permute-start.77) | collective-permute-done | bytes 401440 | tf_op jit(solution)/shard_map/ppermute | solution.py:29
  428.3 9.0 %collective-permute-done.89 = bf16[1152,256]{1,0:T(8,128)(2,1)S(1)} collective-permute-done((bf16[1152,256]{1,0:T(8,128)(2,1)}, bf16[1152,256]{1,0:T(8,128)(2,1)S(1)}, u32[]{:S(2)}, u32[]{:S(2)}) %collective-permute-start.89) | collective-permute-done | bytes 589856 | tf_op jit(solution)/shard_map/ppermute | solution.py:29
  443.3 6.5 %collective-permute-done.85 = bf16[1152,256]{1,0:T(8,128)(2,1)S(1)} collective-permute-done((bf16[1152,256]{1,0:T(8,128)(2,1)S(1)}, bf16[1152,256]{1,0:T(8,128)(2,1)S(1)}, u32[]{:S(2)}, u32[]{:S(2)}) %collective-permute-start.85) | collective-permute-done | bytes 589856 | tf_op jit(solution)/shard_map/ppermute | solution.py:29
  449.9 12.3 %collective-permute-done.87 = bf16[1152,256]{1,0:T(8,128)(2,1)S(1)} collective-permute-done((bf16[1152,256]{1,0:T(8,128)(2,1)S(1)}, bf16[1152,256]{1,0:T(8,128)(2,1)S(1)}, u32[]{:S(2)}, u32[]{:S(2)}) %collective-permute-start.87) | collective-permute-done | bytes 589856 | tf_op jit(solution)/shard_map/ppermute | solution.py:29
  477.0 8.0 %shard_map.263 = (f32[256,3072]{1,0:T(8,128)}, f32[256,3072]{1,0:T(8,128)}, f32[8,96,1024]{2,1,0:T(8,128)}) custom-call(s32[2]{0:T(128)} %pad_add_fusion.1.where.refs_0_.refs_1_, bf16[4,1152,256]{2,1,0:T(8,128)(2,1)} %pad_maximum_fusion.refs_0_, bf16[4,1152,256]{2,1,0:T(8,128)(2,1)} %collective-permute-done.88.refs_1_, ...), custom_call_target="tpu_custom_call" | custom-call | bytes 14155776 | tf_op jit(solution)/shard_map/pallas_call | solution.py:997
  496.7 6.0 %shard_map.265 = (f32[256,2048]{1,0:T(8,128)}, f32[256,1024]{1,0:T(8,128)}, f32[256,1024]{1,0:T(8,128)}, f32[2,256,1024]{2,1,0:T(8,128)}, f32[16,256]{1,0:T(8,128)}) custom-call(s32[2]{0:T(128)} %pad_add_fusion.1.where.refs_0_.refs_1_, bf16[4,784,256]{2,1,0:T(8,128)(2,1)} %pad_maximum_fusion.2.refs_0_, bf16[4,784,256]{2,1,0:T(8,128)(2,1)} %collective-permute-done.98.refs_1_, ...), custom_call_target="tpu_custom_call" | custom-call | bytes 9633792 | tf_op jit(solution)/shard_map/pallas_call | solution.py:997
  (557 shorter events, 292.5 us)
Async XLA Ops:
  7.2 55.0 %all-gather.9.cloned.1.call-start = ((), (), s32[]{:S(2)}) async-start(), calls=%async_computation.8 | async-start | bytes 2007040 | tf_op jit(solution)/shard_map/all_gather | solution.py:669
  19.3 95.4 %all-gather.11.cloned.1.call-start = ((), (), s32[]{:S(2)}) async-start(), calls=%async_computation.9 | async-start | bytes 2949120 | tf_op jit(solution)/shard_map/all_gather | solution.py:669
  40.0 22.1 %collective-permute-start.6 = (bf16[128,1024]{1,0:T(8,128)(2,1)S(1)}, bf16[128,1024]{1,0:T(8,128)(2,1)S(1)}, u32[]{:S(2)}, u32[]{:S(2)}) collective-permute-start(bf16[128,1024]{1,0:T(8,128)(2,1)S(1)} %get-tuple-element.264.refs_1_.refs_4_), channel_id=1, source_target_pairs={{0,8},{4,12},{8,0},{12,4},{1,9},{5,13},{9,1},{13,5},{2,10},{6,14},... | collective-permute-start | bytes 786440 | tf_op jit(solution)/shard_map/ppermute | solution.py:29
  41.8 20.3 %collective-permute-start.7 = (bf16[128,1024]{1,0:T(8,128)(2,1)S(1)}, bf16[128,1024]{1,0:T(8,128)(2,1)S(1)}, u32[]{:S(2)}, u32[]{:S(2)}) collective-permute-start(bf16[128,1024]{1,0:T(8,128)(2,1)S(1)} %get-tuple-element.264.refs_1_.refs_4_), channel_id=1, source_target_pairs={{0,12},{4,8},{8,4},{12,0},{1,13},{5,9},{9,5},{13,1},{2,14},{6,10},... | collective-permute-start | bytes 786440 | tf_op jit(solution)/shard_map/ppermute | solution.py:29
  62.3 95.4 %all-gather.13.cloned.1.call-start = ((), (), s32[]{:S(2)}) async-start(), calls=%async_computation.10 | async-start | bytes 2007040 | tf_op jit(solution)/shard_map/all_gather | solution.py:669
  119.6 93.0 %all-gather.15.cloned.1.call-start = ((), (), s32[]{:S(2)}) async-start(), calls=%async_computation.11 | async-start | bytes 2949120 | tf_op jit(solution)/shard_map/all_gather | solution.py:669
  161.4 163.2 %reduce-scatter.5.cloned.1.call-start = ((), (), s32[]{:S(2)}) async-start(), calls=%async_computation.4 | async-start | bytes 2949120 | tf_op jit(solution)/shard_map/reduce_scatter | solution.py:880
  259.6 104.9 %reduce-scatter.7.cloned.1.call-start = ((), (), s32[]{:S(2)}) async-start(), calls=%async_computation.5 | async-start | bytes 2007040 | tf_op jit(solution)/shard_map/reduce_scatter | solution.py:880
  259.8 27.7 %collective-permute-start.52 = (bf16[128,1024]{1,0:T(8,128)(2,1)S(1)}, bf16[128,1024]{1,0:T(8,128)(2,1)S(1)}, u32[]{:S(2)}, u32[]{:S(2)}) collective-permute-start(bf16[128,1024]{1,0:T(8,128)(2,1)S(1)} %get-tuple-element.369), channel_id=1, source_target_pairs={{0,4},{4,0},{8,12},{12,8},{1,5},{5,1},{9,13},{13,9},{2,6},{6,2},{1... | collective-permute-start | bytes 786440 | tf_op jit(solution)/shard_map/ppermute | solution.py:29
  260.6 27.0 %collective-permute-start.53 = (bf16[128,1024]{1,0:T(8,128)(2,1)S(1)}, bf16[128,1024]{1,0:T(8,128)(2,1)S(1)}, u32[]{:S(2)}, u32[]{:S(2)}) collective-permute-start(bf16[128,1024]{1,0:T(8,128)(2,1)S(1)} %get-tuple-element.370), channel_id=1, source_target_pairs={{0,8},{4,12},{8,0},{12,4},{1,9},{5,13},{9,1},{13,5},{2,10},{6,14},... | collective-permute-start | bytes 786440 | tf_op jit(solution)/shard_map/ppermute | solution.py:29
  262.1 25.5 %collective-permute-start.54 = (bf16[128,1024]{1,0:T(8,128)(2,1)S(1)}, bf16[128,1024]{1,0:T(8,128)(2,1)S(1)}, u32[]{:S(2)}, u32[]{:S(2)}) collective-permute-start(bf16[128,1024]{1,0:T(8,128)(2,1)S(1)} %get-tuple-element.371), channel_id=1, source_target_pairs={{0,12},{4,8},{8,4},{12,0},{1,13},{5,9},{9,5},{13,1},{2,14},{6,10},... | collective-permute-start | bytes 786440 | tf_op jit(solution)/shard_map/ppermute | solution.py:29
  324.6 88.8 %reduce-scatter.9.cloned.1.call-start = ((), (), s32[]{:S(2)}) async-start(), calls=%async_computation.6 | async-start | bytes 2949120 | tf_op jit(solution)/shard_map/reduce_scatter | solution.py:880
  351.9 33.6 %collective-permute-start.74 = (bf16[1152,256]{1,0:T(8,128)(2,1)}, bf16[1152,256]{1,0:T(8,128)(2,1)}, u32[]{:S(2)}, u32[]{:S(2)}) collective-permute-start(bf16[1152,256]{1,0:T(8,128)(2,1)} %bitcast.22.refs_1_), channel_id=1, source_target_pairs={{0,4},{4,0},{8,12},{12,8},{1,5},{5,1},{9,13},{13,9},{2,6},{6,2},{1... | collective-permute-start | bytes 1769480 | tf_op jit(solution)/shard_map/ppermute | solution.py:29
  353.2 32.2 %collective-permute-start.75 = (bf16[1152,256]{1,0:T(8,128)(2,1)}, bf16[1152,256]{1,0:T(8,128)(2,1)}, u32[]{:S(2)}, u32[]{:S(2)}) collective-permute-start(bf16[1152,256]{1,0:T(8,128)(2,1)} %bitcast.22.refs_1_), channel_id=1, source_target_pairs={{0,8},{4,12},{8,0},{12,4},{1,9},{5,13},{9,1},{13,5},{2,10},{6,14},... | collective-permute-start | bytes 1769480 | tf_op jit(solution)/shard_map/ppermute | solution.py:29
  365.2 103.1 %reduce-scatter.11.cloned.1.call-start = ((), (), s32[]{:S(2)}) async-start(), calls=%async_computation.7 | async-start | bytes 2007040 | tf_op jit(solution)/shard_map/reduce_scatter | solution.py:880
  365.7 19.7 %collective-permute-start.76 = (bf16[784,256]{1,0:T(8,128)(2,1)S(1)}, bf16[784,256]{1,0:T(8,128)(2,1)S(1)}, u32[]{:S(2)}, u32[]{:S(2)}) collective-permute-start(bf16[784,256]{1,0:T(8,128)(2,1)S(1)} %bitcast.98), channel_id=1, source_target_pairs={{0,4},{4,0},{8,12},{12,8},{1,5},{5,1},{9,13},{13,9},{2,6},{6,2},{1... | collective-permute-start | bytes 1204232 | tf_op jit(solution)/shard_map/ppermute | solution.py:29
  366.5 27.1 %collective-permute-start.77 = (bf16[784,256]{1,0:T(8,128)(2,1)S(1)}, bf16[784,256]{1,0:T(8,128)(2,1)S(1)}, u32[]{:S(2)}, u32[]{:S(2)}) collective-permute-start(bf16[784,256]{1,0:T(8,128)(2,1)S(1)} %bitcast.99), channel_id=1, source_target_pairs={{0,8},{4,12},{8,0},{12,4},{1,9},{5,13},{9,1},{13,5},{2,10},{6,14},... | collective-permute-start | bytes 1204232 | tf_op jit(solution)/shard_map/ppermute | solution.py:29
  367.9 25.7 %collective-permute-start.78 = (bf16[784,256]{1,0:T(8,128)(2,1)S(1)}, bf16[784,256]{1,0:T(8,128)(2,1)S(1)}, u32[]{:S(2)}, u32[]{:S(2)}) collective-permute-start(bf16[784,256]{1,0:T(8,128)(2,1)S(1)} %bitcast.100), channel_id=1, source_target_pairs={{0,12},{4,8},{8,4},{12,0},{1,13},{5,9},{9,5},{13,1},{2,14},{6,10},... | collective-permute-start | bytes 1204232 | tf_op jit(solution)/shard_map/ppermute | solution.py:29
  424.8 25.1 %collective-permute-start.85 = (bf16[1152,256]{1,0:T(8,128)(2,1)S(1)}, bf16[1152,256]{1,0:T(8,128)(2,1)S(1)}, u32[]{:S(2)}, u32[]{:S(2)}) collective-permute-start(bf16[1152,256]{1,0:T(8,128)(2,1)S(1)} %bitcast.126), channel_id=1, source_target_pairs={{0,4},{4,0},{8,12},{12,8},{1,5},{5,1},{9,13},{13,9},{2,6},{6,2},{1... | collective-permute-start | bytes 1769480 | tf_op jit(solution)/shard_map/ppermute | solution.py:29
  425.4 24.4 %collective-permute-start.86 = (bf16[1152,256]{1,0:T(8,128)(2,1)S(1)}, bf16[1152,256]{1,0:T(8,128)(2,1)S(1)}, u32[]{:S(2)}, u32[]{:S(2)}) collective-permute-start(bf16[1152,256]{1,0:T(8,128)(2,1)S(1)} %bitcast.127), channel_id=1, source_target_pairs={{0,8},{4,12},{8,0},{12,4},{1,9},{5,13},{9,1},{13,5},{2,10},{6,14},... | collective-permute-start | bytes 1769480 | tf_op jit(solution)/shard_map/ppermute | solution.py:29
  426.8 35.4 %collective-permute-start.87 = (bf16[1152,256]{1,0:T(8,128)(2,1)S(1)}, bf16[1152,256]{1,0:T(8,128)(2,1)S(1)}, u32[]{:S(2)}, u32[]{:S(2)}) collective-permute-start(bf16[1152,256]{1,0:T(8,128)(2,1)S(1)} %bitcast.128), channel_id=1, source_target_pairs={{0,12},{4,8},{8,4},{12,0},{1,13},{5,9},{9,5},{13,1},{2,14},{6,10},... | collective-permute-start | bytes 1769480 | tf_op jit(solution)/shard_map/ppermute | solution.py:29
  440.5 33.2 %collective-permute-start.90 = (bf16[4,1152,256]{2,1,0:T(8,128)(2,1)}, bf16[4,1152,256]{2,1,0:T(8,128)(2,1)}, u32[]{:S(2)}, u32[]{:S(2)}) collective-permute-start(bf16[4,1152,256]{2,1,0:T(8,128)(2,1)} %pad_maximum_fusion.1.refs_2_), channel_id=1, source_target_pairs={{0,16},{1,17},{2,18},{3,19},{4,20},{5,21},{6,22},{7,23},{8,24},{9,... | collective-permute-start | bytes 7077896 | tf_op jit(solution)/shard_map/ppermute | solution.py:896
  469.7 19.8 %collective-permute-start.96 = (bf16[784,256]{1,0:T(8,128)(2,1)}, bf16[784,256]{1,0:T(8,128)(2,1)S(1)}, u32[]{:S(2)}, u32[]{:S(2)}) collective-permute-start(bf16[784,256]{1,0:T(8,128)(2,1)} %bitcast.137), channel_id=1, source_target_pairs={{0,8},{4,12},{8,0},{12,4},{1,9},{5,13},{9,1},{13,5},{2,10},{6,14},... | collective-permute-start | bytes 1204232 | tf_op jit(solution)/shard_map/ppermute | solution.py:29
  473.7 19.4 %collective-permute-start.99 = (bf16[4,784,256]{2,1,0:T(8,128)(2,1)S(1)}, bf16[4,784,256]{2,1,0:T(8,128)(2,1)}, u32[]{:S(2)}, u32[]{:S(2)}) collective-permute-start(bf16[4,784,256]{2,1,0:T(8,128)(2,1)S(1)} %pad_maximum_fusion.3.refs_2_), channel_id=1, source_target_pairs={{0,16},{1,17},{2,18},{3,19},{4,20},{5,21},{6,22},{7,23},{8,24},{9,... | collective-permute-start | bytes 4816904 | tf_op jit(solution)/shard_map/ppermute | solution.py:896
  (219 other events, 2382.2 us)
Sparse Core Ops, SparseCore 0:
  19.5 40.0 all-gather.8
  62.4 52.2 all-gather.10
  119.7 37.9 all-gather.12
  161.5 51.0 all-gather.14
  259.7 46.0 reduce-scatter.4
  324.8 33.4 reduce-scatter.6
  364.7 45.9 reduce-scatter.8
  424.9 33.2 reduce-scatter.10

commit v5 on v4

--- a/solution.py
+++ b/solution.py
@@ -143,7 +143,7 @@
     out[...] = jnp.zeros_like(out)
 
 
-def mark(*values, took=200):
+def mark(*values, took=20):
     return call(mark_kernel, [], [((8, 128), f32)], took, after=values)[0]
 
 
@@ -557,11 +557,9 @@
     entering = jnp.where(first, own, other)
     cotangent = jnp.where(first, other, own)
 
-    entering_pieces = hops(entering)
-
     where = jnp.stack([piece, core]).astype(jnp.int32)
 
-    def cut(kernel, weights, constants, size, after=None):
+    def cut(kernel, weights, constants, size, after=()):
         def half(i, where):
             return jnp.where(i == 0, 1 - where[1], where[1])
 
@@ -585,8 +583,13 @@
             pl.BlockSpec((1, height, breadth), maps[which]) for _, height, breadth, which in weights
         ]
         in_specs += [pl.BlockSpec(v.shape, lambda i, where: (0, 0)) for v in constants]
+        in_specs += [pl.BlockSpec(memory_space=pl.ANY)] * len(after)
+
+        def body(where, *refs):
+            kernel(where, *refs[: len(refs) - 1 - len(after)], refs[-1])
+
         return pl.pallas_call(
-            kernel,
+            body,
             grid_spec=pltpu.PrefetchScalarGridSpec(
                 num_scalar_prefetch=1,
                 grid=(2,),
@@ -598,7 +601,7 @@
             cost_estimate=pl.CostEstimate(
                 flops=int(3 * FLOPS_PER_US), bytes_accessed=12 * size * LANES, transcendentals=0
             ),
-        )(tie(where, after), *[weight for weight, *_ in weights], *constants)
+        )(where, *[weight for weight, *_ in weights], *constants, *after)
 
     def place_shares(weight, out, at):
         share = weight.shape[1]
@@ -654,13 +657,14 @@
     line = jnp.arange(size, dtype=jnp.int32)[:, None]
     gain_rows = (line >= part) & (line < part + GAIN_ROWS)
     attention_blocks = jnp.where(gain_rows, cuts[1], attention_blocks[0]), attention_blocks[1]
+    point = mark(attention_blocks[0])
     if aligned:
         block = 2 * hidden_half
         weights = [(gate_weight, part, block, "even"), (gate_weight, part, block, "odd")]
         weights += [(up_weight, part, block, "even"), (up_weight, part, block, "odd")]
         weights += [(down_weight, down_share, width, "carried")]
         size = lift_rows + chunks * down_share
-        mlp_blocks = by_layer(cut(strided_cut_kernel, weights, [], size, entering_pieces[1]))
+        mlp_blocks = by_layer(cut(strided_cut_kernel, weights, [], size, [point]))
     else:
         weights = [(gate_weight, part, hidden_half, "columns"), (up_weight, part, hidden_half, "columns")]
         mlp_blocks = by_layer(cut(mlp_cut_kernel, weights, [], lift_rows))
@@ -740,7 +744,7 @@
         kernel = functools.partial(rows_kernel, count, form, dealt)
         outputs = [(wide, low)] * count + [((left.shape[1], width), low)]
         operands = [left] + ([chosen] if dealt else []) + [*given]
-        *parts, whole = call(kernel, operands, outputs, 4, scalars=[index], after=after)
+        *parts, whole = call(kernel, operands, outputs, 8, scalars=[index], after=after)
         return parts, whole
 
     def lift_forward(pieces, weights, gain=None, after=()):
@@ -751,7 +755,7 @@
         if gain is not None:
             operands += [gain, chosen]
             outputs += [(wide, low)]
-        return call(kernel, [*operands, *weights], outputs, 6, after=after)
+        return call(kernel, [*operands, *weights], outputs, 0.6, after=after)
 
     def mlp_forward(pieces, weights, form, down):
         kernel = functools.partial(mlp_forward_kernel, count, part, form)
@@ -759,7 +763,7 @@
         outputs += [((tokens, hidden_wide), low)] + [(wide, low)] * count
         outputs += [((hidden_wide, width), low)]
         operands = [*pieces, *weights] + ([] if form == "strided" else [down])
-        *results, whole = call(kernel, operands, outputs, 8, scalars=[index])
+        *results, whole = call(kernel, operands, outputs, 2.4, scalars=[index])
         return results[:4], results[4:], whole
 
     def mlp_backward(pieces, weights, form, down, kept, after=()):
@@ -767,7 +771,7 @@
         outputs = [(wide, low)] * count + [(half_wide, low), ((tokens, 2 * hidden_wide), low)]
         outputs += [((hidden_wide, width), low)]
         operands = [*pieces, *weights, kept[1], kept[2]] + ([] if form == "strided" else [down])
-        results = call(kernel, operands, outputs, 6, scalars=[index], after=after)
+        results = call(kernel, operands, outputs, 3.0, scalars=[index], after=after)
         parts, (branch, both, whole) = results[:count], results[count:]
         return parts, branch, both, whole
 
@@ -798,7 +802,7 @@
         outputs += [] if strided else [(row_shape, f32), (row_shape, low)]
         operands = [left, grads, inner, branch]
         scratch = [((width, tokens), low)]
-        return call(kernel, operands, outputs, 6, scratch, scalars=[index], after=after)
+        return call(kernel, operands, outputs, 3.0, scratch, scalars=[index], after=after)
 
     if not aligned:
         outs, downs = whole_rows(out_weight, query_half), whole_rows(down_weight, hidden_half)
@@ -814,14 +818,24 @@
         return [*shares, *map(swap, shares)] if aligned else shares
 
     out_form, down_form = ("shares", "strided") if aligned else ("whole", "whole")
-    pieces = entering_pieces
-    cotangents = hops(tie(cotangent, pieces[1]))
+    pieces = hops(tie(entering, point))
+    cotangents = hops(tie(cotangent, point))
     early = pieces, cotangents, mlp_blocks, attention_blocks[1], chosen, cosine, sine, places
-    qkv_first = arrived(gathered(attention_blocks[0]), early)
+    if aligned:
+        pack = lax.axis_index("fsdp")
+        out_rows = tie(attention_blocks[0][qkv_rows:], point)
+        out_rows = [out_rows] + [
+            lax.ppermute(out_rows, "fsdp", [(i, i ^ k) for i in range(depth)]) for k in range(1, depth)
+        ]
+        out_rows = xored(out_rows, piece ^ pack)
+        early = *early, out_rows
+        shares = met(out_rows)
+    else:
+        shares = [outs[0]]
+    qkv_first = arrived(gathered(attention_blocks[0][:qkv_rows]), early)
     found_own, found_far = split_gains(qkv_first[0]), split_gains(qkv_first[1])
     found_first = [jnp.where(first, own, far) for own, far in zip(found_own, found_far)]
     found_last = [jnp.where(first, far, own) for own, far in zip(found_own, found_far)]
-    shares = moving_rows(qkv_first, qkv_rows, None if aligned else outs[0])
     kept_attention_first = attention_forward(pieces, qkv_first, found_first, True)
     kept_attention_first, shares = beside(kept_attention_first, shares)
     *kept_attention_first, dealt_entering = kept_attention_first
@@ -946,7 +960,8 @@
     total, attention_last = beside(total, attention_last)
     mlp_first = scattered(total)
 
-    attention_last = hops(tie(attention_last, pieces[1]))
+    attention_last = tie(attention_last, pieces[1])
+    near_last = [hop(attention_last, k) for k in range(1, count - 1)]
     results = attention_backward(
         pieces,
         qkv_first,
@@ -954,27 +969,28 @@
         found_first,
         kept_attention_first,
         True,
-        after=[mark(total, attention_last[0])],
+        after=[mark(total, attention_last)],
     )
-    results, near, attention_last = lax.optimization_barrier((results, near, attention_last))
+    results, near, near_last = lax.optimization_barrier((results, near, near_last))
     parts, branch, grad_raw, head_gains, dealt_branch = results
-    attention_grads = weight_grads(kept_attention_first[0], grad_raw, kept_attention_first[4], branch)
-    attention_grads, parts = beside(attention_grads, met(parts))
-    swapped = swap(attention_grads[1]), swap(attention_grads[3])
+    grads = weight_grads(kept_attention_first[0], grad_raw, kept_attention_first[4], branch)
+    swapped = swap(grads[1]), swap(grads[3])
+    held, parts = beside((grads[0], grads[2]), met(parts))
     unused, grad, gain, *packed = add_back(
         parts, dealt_branch, dealt_entering, found_first[0], True, (mlp_gain, *head_gains)
     )
     down_grad_first = None if aligned else rows_fallback(*down_rows)
-    (total, out_rows), mlp_first = beside(meet(attention_grads, swapped), mlp_first)
-    mlp_first = hops(mlp_first)
-    moved = met_rows(out_rows)
+    total, out_rows = meet((held[0], grads[1], held[1], grads[3]), swapped)
+    moved, mlp_first = beside(met_rows(out_rows), mlp_first)
     operand = laid_out(total, moved, packed)
     out_grad_first = None if aligned else rows_fallback(out_rows)
     gains_first = (gain, mlp_gain, *head_gains)
     attention_first = scattered(operand)
     point = mark(operand)
     sums = None if aligned else gains_reduced(gains_first, gains_last)
-    mlp_last = [mlp_last, *near, hop(tie(mlp_last, point), count - 1)]
+    mlp_last = [mlp_last, *near, hop(tie(mlp_last, parts), count - 1)]
+    attention_last = [attention_last, *near_last, hop(tie(attention_last, parts), count - 1)]
+    mlp_first = hops(tie(mlp_first, point))
     mlp_last, attention_last = returned(mlp_last, 1), returned(attention_last, 1)
     attention_first = hops(tie(attention_first, mlp_first))
     mlp_first = returned(mlp_first, 0)

time: 520 us -> 508 us (0.977)
  waiting for transfers between devices: 207 us -> 184 us
  starting transfers between devices: 103 us -> 111 us
    ppermute x72, waiting for transfers between devices: 161 us -> 149 us  [hop(): return lax.ppermute(value, 'ctx', [(i, i ^ step) for i in range(count)])]
    all_gather x4, waiting for transfers between devices: 26.4 us -> 20.1 us  [gathered(): return lax.all_gather(block, 'fsdp', axis=0, tiled=False)]
    ppermute x0 -> x3, starting transfers between devices: none -> 5.68 us  [shards(): lax.ppermute(out_rows, 'fsdp', [(i, i ^ k) for i in range(depth)])]
    unnamed x278 -> x250, local copies, waits for them, and re-layouts: 30.3 us -> 33.9 us
  transfers between devices with their start and end apart: 108 -> 111, of which waited for: 50 -> 50; matrix products, arithmetic and copies ran while one was open for 4% -> 4% of each run, Pallas kernels for 23% -> 23%
where the time goes in v5:
time: 508 us; the launch traced here: 499 us
  waiting for transfers between devices  184 us (36%)
  Pallas kernels  128 us (25%)
  starting transfers between devices  111 us (22%)
  local copies, waits for them, and re-layouts  41.5 us (8%)
  other arithmetic  18.5 us (4%)
  between operations  16 us (3%)
    ppermute x72, waiting for transfers between devices, hop(): return lax.ppermute(value, 'ctx', [(i, i ^ step) for i in range(count)])  149 us
    pallas_call x33, Pallas kernels, call(): pl.pallas_call(body, out_shape=shapes, in_specs=[anywhere] * skipped + [s...  106 us
    ppermute x72, starting transfers between devices, hop(): return lax.ppermute(value, 'ctx', [(i, i ^ step) for i in range(count)])  86.9 us
    unnamed x250, local copies, waits for them, and re-layouts  33.9 us
    all_gather x4, waiting for transfers between devices, gathered(): return lax.all_gather(block, 'fsdp', axis=0, tiled=False)  20.1 us
    pallas_call x2, Pallas kernels, settle(): pl.pallas_call(body, grid_spec=pltpu.PrefetchScalarGridSpec(num_scalar_pr...  14 us
    ppermute x4, starting transfers between devices, returned(): return (own, lax.ppermute(own, 'section', [(1 - layer, layer)]))  11.7 us
    ppermute x24, waiting for transfers between devices, swap(): return lax.ppermute(value, 'section', [(0, 1), (1, 0)])  11.6 us
  transfers between devices with their start and end apart: 111, of which 50 were waited for; matrix products, arithmetic and copies ran while one was open for 4% of the time, Pallas kernels for 23%

profile of v5, /device:TPU:0, one launch (start us, length us, event | category | flops | bytes accessed | tf_op | source)
XLA Modules:
  0.0 499.4 jit_solution(5384206070848709974)
XLA Ops:
  53.8 6.2 %collective-permute-done.3.refs_2_ = bf16[128,1024]{1,0:T(8,128)(2,1)S(1)} collective-permute-done((bf16[128,1024]{1,0:T(8,128)(2,1)S(1)}, bf16[128,1024]{1,0:T(8,128)(2,1)S(1)}, u32[]{:S(2)}, u32[]{:S(2)}) %collective-permute-start.3) | collective-permute-done | bytes 262176 | tf_op jit(solution)/shard_map/ppermute | solution.py:29
  70.5 7.0 %shard_map.232 = (bf16[512,1024]{1,0:T(8,128)(2,1)S(1)}, f32[512,1024]{1,0:T(8,128)S(1)}, bf16[512,512]{1,0:T(8,128)(2,1)S(1)}, bf16[512,256]{1,0:T(8,128)(2,1)S...) custom-call(bf16[128,1024]{1,0:T(8,128)(2,1)S(1)} %get-tuple-element.258.refs_0_.refs_4_, ...), custom_call_target="tpu_custom_call" | custom-call | flops 13799999488 | bytes 8997888 | tf_op jit(solution)/shard_map/pallas_call | solution.py:129
  87.6 5.6 %collective-permute-done.20.refs_1_ = bf16[128,1024]{1,0:T(8,128)(2,1)S(1)} collective-permute-done((bf16[128,1024]{1,0:T(8,128)(2,1)S(1)}, bf16[128,1024]{1,0:T(8,128)(2,1)S(1)}, u32[]{:S(2)}, u32[]{:S(2)}) %collective-permute-start.20) | collective-permute-done | bytes 262176 | tf_op jit(solution)/shard_map/ppermute | solution.py:29
  93.2 5.9 %collective-permute-done.22.refs_3_ = bf16[128,1024]{1,0:T(8,128)(2,1)S(1)} collective-permute-done((bf16[128,1024]{1,0:T(8,128)(2,1)S(1)}, bf16[128,1024]{1,0:T(8,128)(2,1)S(1)}, u32[]{:S(2)}, u32[]{:S(2)}) %collective-permute-start.22) | collective-permute-done | bytes 262176 | tf_op jit(solution)/shard_map/ppermute | solution.py:29
  103.0 5.7 %collective-permute-done.23.refs_2_ = bf16[128,1024]{1,0:T(8,128)(2,1)S(1)} collective-permute-done((bf16[128,1024]{1,0:T(8,128)(2,1)S(1)}, bf16[128,1024]{1,0:T(8,128)(2,1)S(1)}, u32[]{:S(2)}, u32[]{:S(2)}) %collective-permute-start.23) | collective-permute-done | bytes 262176 | tf_op jit(solution)/shard_map/ppermute | solution.py:29
  122.6 5.3 %shard_map.235 = (bf16[512,1024]{1,0:T(8,128)(2,1)S(1)}, f32[512,768]{1,0:T(8,128)S(1)}, f32[512,768]{1,0:T(8,128)S(1)}, bf16[512,768]{1,0:T(8,128)(2,1)S(1)}, b...) custom-call(s32[2]{0:T(128)S(1)} %copy-done.5, ...), custom_call_target="tpu_custom_call" | custom-call | flops 2760000000 | bytes 13369344 | tf_op jit(solution)/shard_map/pallas_call | solution.py:129
  131.5 5.7 %collective-permute-done.27.refs_1_ = bf16[128,1024]{1,0:T(8,128)(2,1)S(1)} collective-permute-done((bf16[128,1024]{1,0:T(8,128)(2,1)S(1)}, bf16[128,1024]{1,0:T(8,128)(2,1)S(1)}, u32[]{:S(2)}, u32[]{:S(2)}) %collective-permute-start.27) | collective-permute-done | bytes 262176 | tf_op jit(solution)/shard_map/ppermute | solution.py:29
  137.2 6.0 %collective-permute-done.28.refs_2_ = bf16[128,1024]{1,0:T(8,128)(2,1)S(1)} collective-permute-done((bf16[128,1024]{1,0:T(8,128)(2,1)S(1)}, bf16[128,1024]{1,0:T(8,128)(2,1)S(1)}, u32[]{:S(2)}, u32[]{:S(2)}) %collective-permute-start.28) | collective-permute-done | bytes 262176 | tf_op jit(solution)/shard_map/ppermute | solution.py:29
  147.8 6.9 %all-gather.13.cloned.1.call-done = bf16[3136,256]{1,0:T(8,128)(2,1)} async-done(((bf16[784,256]{1,0:T(8,128)(2,1)}), bf16[3136,256]{1,0:T(8,128)(2,1)}) %all-gather.13.cloned.1.call-update) | async-done | bytes 1605648 | tf_op jit(solution)/shard_map/all_gather | solution.py:673
  164.3 8.2 %shard_map.237 = (bf16[512,1024]{1,0:T(8,128)(2,1)S(1)}, f32[512,1024]{1,0:T(8,128)S(1)}, bf16[512,512]{1,0:T(8,128)(2,1)S(1)}, bf16[512,256]{1,0:T(8,128)(2,1)S...) custom-call(bf16[128,1024]{1,0:T(8,128)(2,1)S(1)} %get-tuple-element.287.refs_0_, ...), custom_call_target="tpu_custom_call" | custom-call | flops 13799999488 | bytes 9255936 | tf_op jit(solution)/shard_map/pallas_call | solution.py:129
  181.1 5.6 %collective-permute-done.41.refs_1_ = bf16[128,1024]{1,0:T(8,128)(2,1)S(1)} collective-permute-done((bf16[128,1024]{1,0:T(8,128)(2,1)S(1)}, bf16[128,1024]{1,0:T(8,128)(2,1)S(1)}, u32[]{:S(2)}, u32[]{:S(2)}) %collective-permute-start.41) | collective-permute-done | bytes 262176 | tf_op jit(solution)/shard_map/ppermute | solution.py:29
  186.7 5.3 %collective-permute-done.42.refs_2_ = bf16[128,1024]{1,0:T(8,128)(2,1)S(1)} collective-permute-done((bf16[128,1024]{1,0:T(8,128)(2,1)S(1)}, bf16[128,1024]{1,0:T(8,128)(2,1)S(1)}, u32[]{:S(2)}, u32[]{:S(2)}) %collective-permute-start.42) | collective-permute-done | bytes 262176 | tf_op jit(solution)/shard_map/ppermute | solution.py:29
  196.6 10.4 %all-gather.15.cloned.1.call-done = bf16[4608,256]{1,0:T(8,128)(2,1)} async-done(((bf16[1152,256]{1,0:T(8,128)(2,1)}), bf16[4608,256]{1,0:T(8,128)(2,1)}) %all-gather.15.cloned.1.call-update) | async-done | bytes 2359312 | tf_op jit(solution)/shard_map/all_gather | solution.py:673
  255.1 24.2 %shard_map.248 = (bf16[128,1024]{1,0:T(8,128)(2,1)S(1)}, bf16[128,1024]{1,0:T(8,128)(2,1)S(1)}, bf16[128,1024]{1,0:T(8,128)(2,1)S(1)}, bf16[128,1024]{1,0:T(8,12...) custom-call(f32[8,128]{1,0:T(8,128)S(1)} %shard_map.247.refs_0_, ...), custom_call_target="tpu_custom_call" | custom-call | flops 20700000256 | bytes 11878400 | tf_op jit(solution)/shard_map/pallas_call | solution.py:129
  305.2 5.6 %collective-permute-done.68.refs_4_ = bf16[128,1024]{1,0:T(8,128)(2,1)S(1)} collective-permute-done((bf16[128,1024]{1,0:T(8,128)(2,1)S(1)}, bf16[128,1024]{1,0:T(8,128)(2,1)S(1)}, u32[]{:S(2)}, u32[]{:S(2)}) %collective-permute-start.68) | collective-permute-done | bytes 262176 | tf_op jit(solution)/shard_map/ppermute | solution.py:29
  321.4 6.1 %shard_map.254 = (bf16[128,1024]{1,0:T(8,128)(2,1)S(1)}, bf16[128,1024]{1,0:T(8,128)(2,1)S(1)}, bf16[128,1024]{1,0:T(8,128)(2,1)S(1)}, bf16[128,1024]{1,0:T(8,12...) custom-call(f32[8,128]{1,0:T(8,128)S(1)} %shard_map.253.refs_0_, ...), custom_call_target="tpu_custom_call" | custom-call | flops 3449999872 | bytes 15728640 | tf_op jit(solution)/shard_map/pallas_call | solution.py:129
  351.6 6.6 %collective-permute-done.75.refs_3_ = bf16[128,1024]{1,0:T(8,128)(2,1)S(1)} collective-permute-done((bf16[128,1024]{1,0:T(8,128)(2,1)}, bf16[128,1024]{1,0:T(8,128)(2,1)S(1)}, u32[]{:S(2)}, u32[]{:S(2)}) %collective-permute-start.75) | collective-permute-done | bytes 262176 | tf_op jit(solution)/shard_map/ppermute | solution.py:29
  363.1 15.5 %shard_map.259 = (bf16[128,1024]{1,0:T(8,128)(2,1)S(1)}, bf16[128,1024]{1,0:T(8,128)(2,1)S(1)}, bf16[128,1024]{1,0:T(8,128)(2,1)S(1)}, bf16[128,1024]{1,0:T(8,12...) custom-call(f32[8,128]{1,0:T(8,128)S(1)} %shard_map.258.refs_0_, ...), custom_call_target="tpu_custom_call" | custom-call | flops 20700000256 | bytes 11616256 | tf_op jit(solution)/shard_map/pallas_call | solution.py:129
  385.3 5.7 %collective-permute-done.81.refs_1_ = bf16[128,1024]{1,0:T(8,128)(2,1)S(1)} collective-permute-done((bf16[128,1024]{1,0:T(8,128)(2,1)S(1)}, bf16[128,1024]{1,0:T(8,128)(2,1)S(1)}, u32[]{:S(2)}, u32[]{:S(2)}) %collective-permute-start.81) | collective-permute-done | bytes 262176 | tf_op jit(solution)/shard_map/ppermute | solution.py:29
  426.7 6.5 %collective-permute-done.90 = bf16[1152,256]{1,0:T(8,128)(2,1)S(1)} collective-permute-done((bf16[1152,256]{1,0:T(8,128)(2,1)}, bf16[1152,256]{1,0:T(8,128)(2,1)S(1)}, u32[]{:S(2)}, u32[]{:S(2)}) %collective-permute-start.90) | collective-permute-done | bytes 589856 | tf_op jit(solution)/shard_map/ppermute | solution.py:29
  433.2 12.3 %collective-permute-done.92 = bf16[1152,256]{1,0:T(8,128)(2,1)S(1)} collective-permute-done((bf16[1152,256]{1,0:T(8,128)(2,1)}, bf16[1152,256]{1,0:T(8,128)(2,1)S(1)}, u32[]{:S(2)}, u32[]{:S(2)}) %collective-permute-start.92) | collective-permute-done | bytes 589856 | tf_op jit(solution)/shard_map/ppermute | solution.py:29
  464.2 6.2 %collective-permute-start.102 = (bf16[4,784,256]{2,1,0:T(8,128)(2,1)}, bf16[4,784,256]{2,1,0:T(8,128)(2,1)}, u32[]{:S(2)}, u32[]{:S(2)}) collective-permute-start(bf16[4,784,256]{2,1,0:T(8,128)(2,1)} %pad_maximum_fusion.3.refs_2_), channel_id=1, source_target_pairs={{0,16},{1,17},{2,18},{3,19},{4,20},{5,21},{6,22},{7,23},{8,24},{9,... | collective-permute-start | bytes 4816904 | tf_op jit(solution)/shard_map/ppermute | solution.py:910
  470.4 8.0 %shard_map.263 = (f32[256,3072]{1,0:T(8,128)}, f32[256,3072]{1,0:T(8,128)}, f32[8,96,1024]{2,1,0:T(8,128)}) custom-call(s32[2]{0:T(128)} %pad_add_fusion.1.where.refs_0_.refs_1_, bf16[4,1152,256]{2,1,0:T(8,128)(2,1)} %pad_maximum_fusion.refs_0_, bf16[4,1152,256]{2,1,0:T(8,128)(2,1)} %collective-permute-done.93.refs_1_, ...), custom_call_target="tpu_custom_call" | custom-call | bytes 14155776 | tf_op jit(solution)/shard_map/pallas_call | solution.py:1013
  484.2 6.0 %shard_map.265 = (f32[256,2048]{1,0:T(8,128)}, f32[256,1024]{1,0:T(8,128)}, f32[256,1024]{1,0:T(8,128)}, f32[2,256,1024]{2,1,0:T(8,128)}, f32[16,256]{1,0:T(8,128)}) custom-call(s32[2]{0:T(128)} %pad_add_fusion.1.where.refs_0_.refs_1_, bf16[4,784,256]{2,1,0:T(8,128)(2,1)} %copy-done.99, bf16[4,784,256]{2,1,0:T(8,128)(2,1)} %collective-permute-done.100.refs_1_, ...), custom_call_target="tpu_custom_call" | custom-call | bytes 9633792 | tf_op jit(solution)/shard_map/pallas_call | solution.py:1013
  (538 shorter events, 296.9 us)
Async XLA Ops:
  7.2 54.2 %all-gather.9.cloned.1.call-start = ((), (), s32[]{:S(2)}) async-start(), calls=%async_computation.8 | async-start | bytes 1351680 | tf_op jit(solution)/shard_map/all_gather | solution.py:673
  24.6 91.4 %all-gather.11.cloned.1.call-start = ((), (), s32[]{:S(2)}) async-start(), calls=%async_computation.9 | async-start | bytes 2949120 | tf_op jit(solution)/shard_map/all_gather | solution.py:673
  41.9 18.1 %collective-permute-start.3 = (bf16[128,1024]{1,0:T(8,128)(2,1)S(1)}, bf16[128,1024]{1,0:T(8,128)(2,1)S(1)}, u32[]{:S(2)}, u32[]{:S(2)}) collective-permute-start(bf16[128,1024]{1,0:T(8,128)(2,1)S(1)} %get-tuple-element.258.refs_0_.refs_4_), channel_id=1, source_target_pairs={{0,8},{4,12},{8,0},{12,4},{1,9},{5,13},{9,1},{13,5},{2,10},{6,14},... | collective-permute-start | bytes 786440 | tf_op jit(solution)/shard_map/ppermute | solution.py:29
  65.2 89.5 %all-gather.13.cloned.1.call-start = ((), (), s32[]{:S(2)}) async-start(), calls=%async_computation.10 | async-start | bytes 2007040 | tf_op jit(solution)/shard_map/all_gather | solution.py:673
  116.1 90.9 %all-gather.15.cloned.1.call-start = ((), (), s32[]{:S(2)}) async-start(), calls=%async_computation.11 | async-start | bytes 2949120 | tf_op jit(solution)/shard_map/all_gather | solution.py:673
  158.5 158.5 %reduce-scatter.5.cloned.1.call-start = ((), (), s32[]{:S(2)}) async-start(), calls=%async_computation.4 | async-start | bytes 2949120 | tf_op jit(solution)/shard_map/reduce_scatter | solution.py:894
  251.3 107.6 %reduce-scatter.7.cloned.1.call-start = ((), (), s32[]{:S(2)}) async-start(), calls=%async_computation.5 | async-start | bytes 2007040 | tf_op jit(solution)/shard_map/reduce_scatter | solution.py:894
  251.5 27.8 %collective-permute-start.55 = (bf16[128,1024]{1,0:T(8,128)(2,1)S(1)}, bf16[128,1024]{1,0:T(8,128)(2,1)S(1)}, u32[]{:S(2)}, u32[]{:S(2)}) collective-permute-start(bf16[128,1024]{1,0:T(8,128)(2,1)S(1)} %get-tuple-element.360), channel_id=1, source_target_pairs={{0,4},{4,0},{8,12},{12,8},{1,5},{5,1},{9,13},{13,9},{2,6},{6,2},{1... | collective-permute-start | bytes 786440 | tf_op jit(solution)/shard_map/ppermute | solution.py:29
  252.4 26.9 %collective-permute-start.56 = (bf16[128,1024]{1,0:T(8,128)(2,1)S(1)}, bf16[128,1024]{1,0:T(8,128)(2,1)S(1)}, u32[]{:S(2)}, u32[]{:S(2)}) collective-permute-start(bf16[128,1024]{1,0:T(8,128)(2,1)S(1)} %get-tuple-element.361), channel_id=1, source_target_pairs={{0,8},{4,12},{8,0},{12,4},{1,9},{5,13},{9,1},{13,5},{2,10},{6,14},... | collective-permute-start | bytes 786440 | tf_op jit(solution)/shard_map/ppermute | solution.py:29
  253.9 25.5 %collective-permute-start.57 = (bf16[128,1024]{1,0:T(8,128)(2,1)S(1)}, bf16[128,1024]{1,0:T(8,128)(2,1)S(1)}, u32[]{:S(2)}, u32[]{:S(2)}) collective-permute-start(bf16[128,1024]{1,0:T(8,128)(2,1)S(1)} %get-tuple-element.362), channel_id=1, source_target_pairs={{0,12},{4,8},{8,4},{12,0},{1,13},{5,9},{9,5},{13,1},{2,14},{6,10},... | collective-permute-start | bytes 786440 | tf_op jit(solution)/shard_map/ppermute | solution.py:29
  317.0 90.5 %reduce-scatter.9.cloned.1.call-start = ((), (), s32[]{:S(2)}) async-start(), calls=%async_computation.6 | async-start | bytes 2949120 | tf_op jit(solution)/shard_map/reduce_scatter | solution.py:894
  345.1 33.5 %collective-permute-start.77 = (bf16[1152,256]{1,0:T(8,128)(2,1)S(1)}, bf16[1152,256]{1,0:T(8,128)(2,1)}, u32[]{:S(2)}, u32[]{:S(2)}) collective-permute-start(bf16[1152,256]{1,0:T(8,128)(2,1)S(1)} %bitcast.101), channel_id=1, source_target_pairs={{0,4},{4,0},{8,12},{12,8},{1,5},{5,1},{9,13},{13,9},{2,6},{6,2},{1... | collective-permute-start | bytes 1769480 | tf_op jit(solution)/shard_map/ppermute | solution.py:29
  346.8 31.8 %collective-permute-start.78 = (bf16[1152,256]{1,0:T(8,128)(2,1)S(1)}, bf16[1152,256]{1,0:T(8,128)(2,1)}, u32[]{:S(2)}, u32[]{:S(2)}) collective-permute-start(bf16[1152,256]{1,0:T(8,128)(2,1)S(1)} %bitcast.102), channel_id=1, source_target_pairs={{0,8},{4,12},{8,0},{12,4},{1,9},{5,13},{9,1},{13,5},{2,10},{6,14},... | collective-permute-start | bytes 1769480 | tf_op jit(solution)/shard_map/ppermute | solution.py:29
  359.0 93.9 %reduce-scatter.11.cloned.1.call-start = ((), (), s32[]{:S(2)}) async-start(), calls=%async_computation.7 | async-start | bytes 2007040 | tf_op jit(solution)/shard_map/reduce_scatter | solution.py:894
  360.1 18.5 %collective-permute-start.79 = (bf16[784,256]{1,0:T(8,128)(2,1)S(1)}, bf16[784,256]{1,0:T(8,128)(2,1)S(1)}, u32[]{:S(2)}, u32[]{:S(2)}) collective-permute-start(bf16[784,256]{1,0:T(8,128)(2,1)S(1)} %bitcast.105), channel_id=1, source_target_pairs={{0,4},{4,0},{8,12},{12,8},{1,5},{5,1},{9,13},{13,9},{2,6},{6,2},{1... | collective-permute-start | bytes 1204232 | tf_op jit(solution)/shard_map/ppermute | solution.py:29
  360.5 18.3 %collective-permute-start.80 = (bf16[784,256]{1,0:T(8,128)(2,1)S(1)}, bf16[784,256]{1,0:T(8,128)(2,1)S(1)}, u32[]{:S(2)}, u32[]{:S(2)}) collective-permute-start(bf16[784,256]{1,0:T(8,128)(2,1)S(1)} %bitcast.106), channel_id=1, source_target_pairs={{0,8},{4,12},{8,0},{12,4},{1,9},{5,13},{9,1},{13,5},{2,10},{6,14},... | collective-permute-start | bytes 1204232 | tf_op jit(solution)/shard_map/ppermute | solution.py:29
  413.3 19.9 %collective-permute-start.90 = (bf16[1152,256]{1,0:T(8,128)(2,1)}, bf16[1152,256]{1,0:T(8,128)(2,1)S(1)}, u32[]{:S(2)}, u32[]{:S(2)}) collective-permute-start(bf16[1152,256]{1,0:T(8,128)(2,1)} %bitcast.129), channel_id=1, source_target_pairs={{0,4},{4,0},{8,12},{12,8},{1,5},{5,1},{9,13},{13,9},{2,6},{6,2},{1... | collective-permute-start | bytes 1769480 | tf_op jit(solution)/shard_map/ppermute | solution.py:29
  414.4 18.8 %collective-permute-start.91 = (bf16[1152,256]{1,0:T(8,128)(2,1)}, bf16[1152,256]{1,0:T(8,128)(2,1)S(1)}, u32[]{:S(2)}, u32[]{:S(2)}) collective-permute-start(bf16[1152,256]{1,0:T(8,128)(2,1)} %bitcast.130), channel_id=1, source_target_pairs={{0,8},{4,12},{8,0},{12,4},{1,9},{5,13},{9,1},{13,5},{2,10},{6,14},... | collective-permute-start | bytes 1769480 | tf_op jit(solution)/shard_map/ppermute | solution.py:29
  415.2 30.3 %collective-permute-start.92 = (bf16[1152,256]{1,0:T(8,128)(2,1)}, bf16[1152,256]{1,0:T(8,128)(2,1)S(1)}, u32[]{:S(2)}, u32[]{:S(2)}) collective-permute-start(bf16[1152,256]{1,0:T(8,128)(2,1)} %bitcast.131), channel_id=1, source_target_pairs={{0,12},{4,8},{8,4},{12,0},{1,13},{5,9},{9,5},{13,1},{2,14},{6,10},... | collective-permute-start | bytes 1769480 | tf_op jit(solution)/shard_map/ppermute | solution.py:29
  423.9 40.2 %collective-permute-start.95 = (bf16[4,1152,256]{2,1,0:T(8,128)(2,1)}, bf16[4,1152,256]{2,1,0:T(8,128)(2,1)}, u32[]{:S(2)}, u32[]{:S(2)}) collective-permute-start(bf16[4,1152,256]{2,1,0:T(8,128)(2,1)} %pad_maximum_fusion.1.refs_2_), channel_id=1, source_target_pairs={{0,16},{1,17},{2,18},{3,19},{4,20},{5,21},{6,22},{7,23},{8,24},{9,... | collective-permute-start | bytes 7077896 | tf_op jit(solution)/shard_map/ppermute | solution.py:910
  447.3 23.1 %collective-permute-start.93 = (bf16[4,1152,256]{2,1,0:T(8,128)(2,1)}, bf16[4,1152,256]{2,1,0:T(8,128)(2,1)}, u32[]{:S(2)}, u32[]{:S(2)}) collective-permute-start(bf16[4,1152,256]{2,1,0:T(8,128)(2,1)} %pad_maximum_fusion.refs_0_), channel_id=1, source_target_pairs={{16,0},{17,1},{18,2},{19,3},{20,4},{21,5},{22,6},{23,7},{24,8},{25... | collective-permute-start | bytes 7077896 | tf_op jit(solution)/shard_map/ppermute | solution.py:910
  452.9 25.6 %collective-permute-start.97 = (bf16[784,256]{1,0:T(8,128)(2,1)}, bf16[784,256]{1,0:T(8,128)(2,1)S(1)}, u32[]{:S(2)}, u32[]{:S(2)}) collective-permute-start(bf16[784,256]{1,0:T(8,128)(2,1)} %bitcast.137), channel_id=1, source_target_pairs={{0,4},{4,0},{8,12},{12,8},{1,5},{5,1},{9,13},{13,9},{2,6},{6,2},{1... | collective-permute-start | bytes 1204232 | tf_op jit(solution)/shard_map/ppermute | solution.py:29
  454.3 24.2 %collective-permute-start.98 = (bf16[784,256]{1,0:T(8,128)(2,1)}, bf16[784,256]{1,0:T(8,128)(2,1)S(1)}, u32[]{:S(2)}, u32[]{:S(2)}) collective-permute-start(bf16[784,256]{1,0:T(8,128)(2,1)} %bitcast.138), channel_id=1, source_target_pairs={{0,8},{4,12},{8,0},{12,4},{1,9},{5,13},{9,1},{13,5},{2,10},{6,14},... | collective-permute-start | bytes 1204232 | tf_op jit(solution)/shard_map/ppermute | solution.py:29
  460.4 18.1 %collective-permute-start.99 = (bf16[784,256]{1,0:T(8,128)(2,1)}, bf16[784,256]{1,0:T(8,128)(2,1)S(1)}, u32[]{:S(2)}, u32[]{:S(2)}) collective-permute-start(bf16[784,256]{1,0:T(8,128)(2,1)} %bitcast.139), channel_id=1, source_target_pairs={{0,12},{4,8},{8,4},{12,0},{1,13},{5,9},{9,5},{13,1},{2,14},{6,10},... | collective-permute-start | bytes 1204232 | tf_op jit(solution)/shard_map/ppermute | solution.py:29
  (208 other events, 1627.3 us)
Sparse Core Ops, SparseCore 0:
  24.8 29.9 all-gather.8
  65.3 50.7 all-gather.10
  118.2 36.4 all-gather.12
  158.6 48.3 all-gather.14
  251.5 46.2 reduce-scatter.4
  317.1 33.5 reduce-scatter.6
  359.1 45.6 reduce-scatter.8
  413.4 33.5 reduce-scatter.10

commit v6 on v5

--- a/solution.py
+++ b/solution.py
@@ -738,7 +738,7 @@
         operands = [*pieces] + ([found[0], chosen] if raw_rows else [])
         outputs += [(wide, low)] if raw_rows else []
         operands += [*weights, cosine, sine, found[2], found[3], *places]
-        return call(kernel, operands, outputs, 12, [((tokens, 2 * key_half), low)], after=after)
+        return call(kernel, operands, outputs, 6.0, [((tokens, 2 * key_half), low)], after=after)
 
     def rows_product(form, left, given, dealt=False, after=()):
         kernel = functools.partial(rows_kernel, count, form, dealt)
@@ -755,7 +755,7 @@
         if gain is not None:
             operands += [gain, chosen]
             outputs += [(wide, low)]
-        return call(kernel, [*operands, *weights], outputs, 0.6, after=after)
+        return call(kernel, [*operands, *weights], outputs, 6, after=after)
 
     def mlp_forward(pieces, weights, form, down):
         kernel = functools.partial(mlp_forward_kernel, count, part, form)
@@ -763,7 +763,7 @@
         outputs += [((tokens, hidden_wide), low)] + [(wide, low)] * count
         outputs += [((hidden_wide, width), low)]
         operands = [*pieces, *weights] + ([] if form == "strided" else [down])
-        *results, whole = call(kernel, operands, outputs, 2.4, scalars=[index])
+        *results, whole = call(kernel, operands, outputs, 8, scalars=[index])
         return results[:4], results[4:], whole
 
     def mlp_backward(pieces, weights, form, down, kept, after=()):
@@ -875,7 +875,7 @@
         size = total.shape[1] + rows_by[0].shape[0] + GAIN_ROWS
         outputs = [((depth, size, LANES), low)]
         operands = [total, packed[0], swap(packed[0]), *rows_by]
-        return call(layout_kernel, operands, outputs, 3, scalars=[index])[0]
+        return call(layout_kernel, operands, outputs, 0.9, scalars=[index])[0]
 
     def gains_reduced(from_first, from_last):
         def by_pack(gains):
@@ -975,7 +975,8 @@
     parts, branch, grad_raw, head_gains, dealt_branch = results
     grads = weight_grads(kept_attention_first[0], grad_raw, kept_attention_first[4], branch)
     swapped = swap(grads[1]), swap(grads[3])
-    held, parts = beside((grads[0], grads[2]), met(parts))
+    grads, parts = beside(grads, met(parts))
+    held = grads[0], grads[2]
     unused, grad, gain, *packed = add_back(
         parts, dealt_branch, dealt_entering, found_first[0], True, (mlp_gain, *head_gains)
     )
@@ -989,7 +990,7 @@
     point = mark(operand)
     sums = None if aligned else gains_reduced(gains_first, gains_last)
     mlp_last = [mlp_last, *near, hop(tie(mlp_last, parts), count - 1)]
-    attention_last = [attention_last, *near_last, hop(tie(attention_last, parts), count - 1)]
+    attention_last = [attention_last, *near_last, hop(tie(attention_last, point), count - 1)]
     mlp_first = hops(tie(mlp_first, point))
     mlp_last, attention_last = returned(mlp_last, 1), returned(attention_last, 1)
     attention_first = hops(tie(attention_first, mlp_first))

time: 508 us -> 504 us (level)
    unnamed x250 -> x242, local copies, waits for them, and re-layouts: 33.9 us -> 29.6 us
  transfers between devices with their start and end apart: 111 -> 111, of which waited for: 50 -> 49; matrix products, arithmetic and copies ran while one was open for 4% -> 4% of each run, Pallas kernels for 23% -> 23%
where the time goes in v6:
time: 504 us; the launch traced here: 496 us
  waiting for transfers between devices  185 us (37%)
  Pallas kernels  128 us (25%)
  starting transfers between devices  112 us (22%)
  local copies, waits for them, and re-layouts  37.2 us (7%)
  other arithmetic  17.6 us (3%)
  between operations  16.1 us (3%)
    ppermute x72, waiting for transfers between devices, hop(): return lax.ppermute(value, 'ctx', [(i, i ^ step) for i in range(count)])  151 us
    pallas_call x33, Pallas kernels, call(): pl.pallas_call(body, out_shape=shapes, in_specs=[anywhere] * skipped + [s...  106 us
    ppermute x72, starting transfers between devices, hop(): return lax.ppermute(value, 'ctx', [(i, i ^ step) for i in range(count)])  87.1 us
    unnamed x242, local copies, waits for them, and re-layouts  29.6 us
    all_gather x4, waiting for transfers between devices, gathered(): return lax.all_gather(block, 'fsdp', axis=0, tiled=False)  18.4 us
    pallas_call x2, Pallas kernels, settle(): pl.pallas_call(body, grid_spec=pltpu.PrefetchScalarGridSpec(num_scalar_pr...  14 us
    ppermute x4, starting transfers between devices, returned(): return (own, lax.ppermute(own, 'section', [(1 - layer, layer)]))  11.8 us
    ppermute x24, waiting for transfers between devices, swap(): return lax.ppermute(value, 'section', [(0, 1), (1, 0)])  11.6 us
  transfers between devices with their start and end apart: 111, of which 49 were waited for; matrix products, arithmetic and copies ran while one was open for 4% of the time, Pallas kernels for 23%

profile of v6, /device:TPU:0, one launch (start us, length us, event | category | flops | bytes accessed | tf_op | source)
XLA Modules:
  0.0 495.5 jit_solution(12332217049339960437)
XLA Ops:
  53.8 6.2 %collective-permute-done.3.refs_2_ = bf16[128,1024]{1,0:T(8,128)(2,1)S(1)} collective-permute-done((bf16[128,1024]{1,0:T(8,128)(2,1)S(1)}, bf16[128,1024]{1,0:T(8,128)(2,1)S(1)}, u32[]{:S(2)}, u32[]{:S(2)}) %collective-permute-start.3) | collective-permute-done | bytes 262176 | tf_op jit(solution)/shard_map/ppermute | solution.py:29
  70.5 7.0 %shard_map.232 = (bf16[512,1024]{1,0:T(8,128)(2,1)S(1)}, f32[512,1024]{1,0:T(8,128)S(1)}, bf16[512,512]{1,0:T(8,128)(2,1)S(1)}, bf16[512,256]{1,0:T(8,128)(2,1)S...) custom-call(bf16[128,1024]{1,0:T(8,128)(2,1)S(1)} %get-tuple-element.259.refs_0_.refs_4_, ...), custom_call_target="tpu_custom_call" | custom-call | flops 6899999744 | bytes 8997888 | tf_op jit(solution)/shard_map/pallas_call | solution.py:129
  86.7 5.6 %collective-permute-done.20.refs_1_ = bf16[128,1024]{1,0:T(8,128)(2,1)S(1)} collective-permute-done((bf16[128,1024]{1,0:T(8,128)(2,1)S(1)}, bf16[128,1024]{1,0:T(8,128)(2,1)S(1)}, u32[]{:S(2)}, u32[]{:S(2)}) %collective-permute-start.20) | collective-permute-done | bytes 262176 | tf_op jit(solution)/shard_map/ppermute | solution.py:29
  92.3 5.9 %collective-permute-done.22.refs_3_ = bf16[128,1024]{1,0:T(8,128)(2,1)S(1)} collective-permute-done((bf16[128,1024]{1,0:T(8,128)(2,1)S(1)}, bf16[128,1024]{1,0:T(8,128)(2,1)S(1)}, u32[]{:S(2)}, u32[]{:S(2)}) %collective-permute-start.22) | collective-permute-done | bytes 262176 | tf_op jit(solution)/shard_map/ppermute | solution.py:29
  102.1 5.7 %collective-permute-done.23.refs_2_ = bf16[128,1024]{1,0:T(8,128)(2,1)S(1)} collective-permute-done((bf16[128,1024]{1,0:T(8,128)(2,1)S(1)}, bf16[128,1024]{1,0:T(8,128)(2,1)S(1)}, u32[]{:S(2)}, u32[]{:S(2)}) %collective-permute-start.23) | collective-permute-done | bytes 262176 | tf_op jit(solution)/shard_map/ppermute | solution.py:29
  119.0 5.3 %shard_map.235 = (bf16[512,1024]{1,0:T(8,128)(2,1)S(1)}, f32[512,768]{1,0:T(8,128)S(1)}, f32[512,768]{1,0:T(8,128)S(1)}, bf16[512,768]{1,0:T(8,128)(2,1)S(1)}, b...) custom-call(s32[2]{0:T(128)S(1)} %copy-done.3, ...), custom_call_target="tpu_custom_call" | custom-call | flops 9200000000 | bytes 13369344 | tf_op jit(solution)/shard_map/pallas_call | solution.py:129
  128.0 5.7 %collective-permute-done.27.refs_1_ = bf16[128,1024]{1,0:T(8,128)(2,1)S(1)} collective-permute-done((bf16[128,1024]{1,0:T(8,128)(2,1)S(1)}, bf16[128,1024]{1,0:T(8,128)(2,1)S(1)}, u32[]{:S(2)}, u32[]{:S(2)}) %collective-permute-start.27) | collective-permute-done | bytes 262176 | tf_op jit(solution)/shard_map/ppermute | solution.py:29
  133.6 6.0 %collective-permute-done.28.refs_2_ = bf16[128,1024]{1,0:T(8,128)(2,1)S(1)} collective-permute-done((bf16[128,1024]{1,0:T(8,128)(2,1)S(1)}, bf16[128,1024]{1,0:T(8,128)(2,1)S(1)}, u32[]{:S(2)}, u32[]{:S(2)}) %collective-permute-start.28) | collective-permute-done | bytes 262176 | tf_op jit(solution)/shard_map/ppermute | solution.py:29
  144.2 6.9 %all-gather.13.cloned.1.call-done = bf16[3136,256]{1,0:T(8,128)(2,1)} async-done(((bf16[784,256]{1,0:T(8,128)(2,1)}), bf16[3136,256]{1,0:T(8,128)(2,1)}) %all-gather.13.cloned.1.call-update) | async-done | bytes 1605648 | tf_op jit(solution)/shard_map/all_gather | solution.py:673
  160.7 8.3 %shard_map.237 = (bf16[512,1024]{1,0:T(8,128)(2,1)S(1)}, f32[512,1024]{1,0:T(8,128)S(1)}, bf16[512,512]{1,0:T(8,128)(2,1)S(1)}, bf16[512,256]{1,0:T(8,128)(2,1)S...) custom-call(bf16[128,1024]{1,0:T(8,128)(2,1)S(1)} %get-tuple-element.288.refs_0_, ...), custom_call_target="tpu_custom_call" | custom-call | flops 6899999744 | bytes 9255936 | tf_op jit(solution)/shard_map/pallas_call | solution.py:129
  178.3 5.6 %collective-permute-done.41.refs_1_ = bf16[128,1024]{1,0:T(8,128)(2,1)S(1)} collective-permute-done((bf16[128,1024]{1,0:T(8,128)(2,1)S(1)}, bf16[128,1024]{1,0:T(8,128)(2,1)S(1)}, u32[]{:S(2)}, u32[]{:S(2)}) %collective-permute-start.41) | collective-permute-done | bytes 262176 | tf_op jit(solution)/shard_map/ppermute | solution.py:29
  193.7 11.3 %all-gather.15.cloned.1.call-done = bf16[4608,256]{1,0:T(8,128)(2,1)} async-done(((bf16[1152,256]{1,0:T(8,128)(2,1)}), bf16[4608,256]{1,0:T(8,128)(2,1)}) %all-gather.15.cloned.1.call-update) | async-done | bytes 2359312 | tf_op jit(solution)/shard_map/all_gather | solution.py:673
  253.2 24.2 %shard_map.248 = (bf16[128,1024]{1,0:T(8,128)(2,1)S(1)}, bf16[128,1024]{1,0:T(8,128)(2,1)S(1)}, bf16[128,1024]{1,0:T(8,128)(2,1)S(1)}, bf16[128,1024]{1,0:T(8,12...) custom-call(f32[8,128]{1,0:T(8,128)S(1)} %shard_map.247.refs_0_, ...), custom_call_target="tpu_custom_call" | custom-call | flops 20700000256 | bytes 11878400 | tf_op jit(solution)/shard_map/pallas_call | solution.py:129
  303.3 5.6 %collective-permute-done.68.refs_4_ = bf16[128,1024]{1,0:T(8,128)(2,1)S(1)} collective-permute-done((bf16[128,1024]{1,0:T(8,128)(2,1)S(1)}, bf16[128,1024]{1,0:T(8,128)(2,1)S(1)}, u32[]{:S(2)}, u32[]{:S(2)}) %collective-permute-start.68) | collective-permute-done | bytes 262176 | tf_op jit(solution)/shard_map/ppermute | solution.py:29
  319.4 6.1 %shard_map.254 = (bf16[128,1024]{1,0:T(8,128)(2,1)S(1)}, bf16[128,1024]{1,0:T(8,128)(2,1)S(1)}, bf16[128,1024]{1,0:T(8,128)(2,1)S(1)}, bf16[128,1024]{1,0:T(8,12...) custom-call(f32[8,128]{1,0:T(8,128)S(1)} %shard_map.253.refs_0_, ...), custom_call_target="tpu_custom_call" | custom-call | flops 3449999872 | bytes 15728640 | tf_op jit(solution)/shard_map/pallas_call | solution.py:129
  349.7 6.7 %collective-permute-done.75.refs_3_ = bf16[128,1024]{1,0:T(8,128)(2,1)S(1)} collective-permute-done((bf16[128,1024]{1,0:T(8,128)(2,1)}, bf16[128,1024]{1,0:T(8,128)(2,1)S(1)}, u32[]{:S(2)}, u32[]{:S(2)}) %collective-permute-start.75) | collective-permute-done | bytes 262176 | tf_op jit(solution)/shard_map/ppermute | solution.py:29
  361.1 15.5 %shard_map.259 = (bf16[128,1024]{1,0:T(8,128)(2,1)S(1)}, bf16[128,1024]{1,0:T(8,128)(2,1)S(1)}, bf16[128,1024]{1,0:T(8,128)(2,1)S(1)}, bf16[128,1024]{1,0:T(8,12...) custom-call(f32[8,128]{1,0:T(8,128)S(1)} %shard_map.258.refs_0_, ...), custom_call_target="tpu_custom_call" | custom-call | flops 20700000256 | bytes 11616256 | tf_op jit(solution)/shard_map/pallas_call | solution.py:129
  383.3 5.7 %collective-permute-done.81.refs_1_ = bf16[128,1024]{1,0:T(8,128)(2,1)S(1)} collective-permute-done((bf16[128,1024]{1,0:T(8,128)(2,1)S(1)}, bf16[128,1024]{1,0:T(8,128)(2,1)S(1)}, u32[]{:S(2)}, u32[]{:S(2)}) %collective-permute-start.81) | collective-permute-done | bytes 262176 | tf_op jit(solution)/shard_map/ppermute | solution.py:29
  411.8 5.4 %collective-permute-done.95 = bf16[1152,256]{1,0:T(8,128)(2,1)} collective-permute-done((bf16[1152,256]{1,0:T(8,128)(2,1)S(1)}, bf16[1152,256]{1,0:T(8,128)(2,1)}, u32[]{:S(2)}, u32[]{:S(2)}) %collective-permute-start.95) | collective-permute-done | bytes 589856 | tf_op jit(solution)/shard_map/ppermute | solution.py:29
  423.2 6.6 %collective-permute-done.91 = bf16[1152,256]{1,0:T(8,128)(2,1)S(1)} collective-permute-done((bf16[1152,256]{1,0:T(8,128)(2,1)}, bf16[1152,256]{1,0:T(8,128)(2,1)S(1)}, u32[]{:S(2)}, u32[]{:S(2)}) %collective-permute-start.91) | collective-permute-done | bytes 589856 | tf_op jit(solution)/shard_map/ppermute | solution.py:29
  429.8 12.2 %collective-permute-done.93 = bf16[1152,256]{1,0:T(8,128)(2,1)S(1)} collective-permute-done((bf16[1152,256]{1,0:T(8,128)(2,1)}, bf16[1152,256]{1,0:T(8,128)(2,1)S(1)}, u32[]{:S(2)}, u32[]{:S(2)}) %collective-permute-start.93) | collective-permute-done | bytes 589856 | tf_op jit(solution)/shard_map/ppermute | solution.py:29
  459.9 6.3 %collective-permute-start.102 = (bf16[4,784,256]{2,1,0:T(8,128)(2,1)}, bf16[4,784,256]{2,1,0:T(8,128)(2,1)}, u32[]{:S(2)}, u32[]{:S(2)}) collective-permute-start(bf16[4,784,256]{2,1,0:T(8,128)(2,1)} %pad_maximum_fusion.3.refs_2_), channel_id=1, source_target_pairs={{0,16},{1,17},{2,18},{3,19},{4,20},{5,21},{6,22},{7,23},{8,24},{9,... | collective-permute-start | bytes 4816904 | tf_op jit(solution)/shard_map/ppermute | solution.py:910
  466.2 8.0 %shard_map.264 = (f32[256,3072]{1,0:T(8,128)}, f32[256,3072]{1,0:T(8,128)}, f32[8,96,1024]{2,1,0:T(8,128)}) custom-call(s32[2]{0:T(128)} %pad_add_fusion.1.where.refs_0_.refs_1_, bf16[4,1152,256]{2,1,0:T(8,128)(2,1)} %pad_maximum_fusion.refs_0_, bf16[4,1152,256]{2,1,0:T(8,128)(2,1)} %collective-permute-done.94.refs_1_, ...), custom_call_target="tpu_custom_call" | custom-call | bytes 14155776 | tf_op jit(solution)/shard_map/pallas_call | solution.py:1014
  480.3 6.0 %shard_map.265 = (f32[256,2048]{1,0:T(8,128)}, f32[256,1024]{1,0:T(8,128)}, f32[256,1024]{1,0:T(8,128)}, f32[2,256,1024]{2,1,0:T(8,128)}, f32[16,256]{1,0:T(8,128)}) custom-call(s32[2]{0:T(128)} %pad_add_fusion.1.where.refs_0_.refs_1_, bf16[4,784,256]{2,1,0:T(8,128)(2,1)} %copy-done.95, bf16[4,784,256]{2,1,0:T(8,128)(2,1)} %collective-permute-done.100.refs_1_, ...), custom_call_target="tpu_custom_call" | custom-call | bytes 9633792 | tf_op jit(solution)/shard_map/pallas_call | solution.py:1014
  (530 shorter events, 291.8 us)
Async XLA Ops:
  7.2 54.3 %all-gather.9.cloned.1.call-start = ((), (), s32[]{:S(2)}) async-start(), calls=%async_computation.8 | async-start | bytes 1351680 | tf_op jit(solution)/shard_map/all_gather | solution.py:673
  24.6 87.8 %all-gather.11.cloned.1.call-start = ((), (), s32[]{:S(2)}) async-start(), calls=%async_computation.9 | async-start | bytes 2949120 | tf_op jit(solution)/shard_map/all_gather | solution.py:673
  41.9 18.1 %collective-permute-start.3 = (bf16[128,1024]{1,0:T(8,128)(2,1)S(1)}, bf16[128,1024]{1,0:T(8,128)(2,1)S(1)}, u32[]{:S(2)}, u32[]{:S(2)}) collective-permute-start(bf16[128,1024]{1,0:T(8,128)(2,1)S(1)} %get-tuple-element.259.refs_0_.refs_4_), channel_id=1, source_target_pairs={{0,8},{4,12},{8,0},{12,4},{1,9},{5,13},{9,1},{13,5},{2,10},{6,14},... | collective-permute-start | bytes 786440 | tf_op jit(solution)/shard_map/ppermute | solution.py:29
  61.5 89.6 %all-gather.13.cloned.1.call-start = ((), (), s32[]{:S(2)}) async-start(), calls=%async_computation.10 | async-start | bytes 2007040 | tf_op jit(solution)/shard_map/all_gather | solution.py:673
  112.5 92.5 %all-gather.15.cloned.1.call-start = ((), (), s32[]{:S(2)}) async-start(), calls=%async_computation.11 | async-start | bytes 2949120 | tf_op jit(solution)/shard_map/all_gather | solution.py:673
  154.9 160.2 %reduce-scatter.5.cloned.1.call-start = ((), (), s32[]{:S(2)}) async-start(), calls=%async_computation.4 | async-start | bytes 2949120 | tf_op jit(solution)/shard_map/reduce_scatter | solution.py:894
  249.4 107.6 %reduce-scatter.7.cloned.1.call-start = ((), (), s32[]{:S(2)}) async-start(), calls=%async_computation.5 | async-start | bytes 2007040 | tf_op jit(solution)/shard_map/reduce_scatter | solution.py:894
  249.5 27.8 %collective-permute-start.55 = (bf16[128,1024]{1,0:T(8,128)(2,1)S(1)}, bf16[128,1024]{1,0:T(8,128)(2,1)S(1)}, u32[]{:S(2)}, u32[]{:S(2)}) collective-permute-start(bf16[128,1024]{1,0:T(8,128)(2,1)S(1)} %get-tuple-element.361), channel_id=1, source_target_pairs={{0,4},{4,0},{8,12},{12,8},{1,5},{5,1},{9,13},{13,9},{2,6},{6,2},{1... | collective-permute-start | bytes 786440 | tf_op jit(solution)/shard_map/ppermute | solution.py:29
  250.4 26.9 %collective-permute-start.56 = (bf16[128,1024]{1,0:T(8,128)(2,1)S(1)}, bf16[128,1024]{1,0:T(8,128)(2,1)S(1)}, u32[]{:S(2)}, u32[]{:S(2)}) collective-permute-start(bf16[128,1024]{1,0:T(8,128)(2,1)S(1)} %get-tuple-element.362), channel_id=1, source_target_pairs={{0,8},{4,12},{8,0},{12,4},{1,9},{5,13},{9,1},{13,5},{2,10},{6,14},... | collective-permute-start | bytes 786440 | tf_op jit(solution)/shard_map/ppermute | solution.py:29
  251.9 25.5 %collective-permute-start.57 = (bf16[128,1024]{1,0:T(8,128)(2,1)S(1)}, bf16[128,1024]{1,0:T(8,128)(2,1)S(1)}, u32[]{:S(2)}, u32[]{:S(2)}) collective-permute-start(bf16[128,1024]{1,0:T(8,128)(2,1)S(1)} %get-tuple-element.363), channel_id=1, source_target_pairs={{0,12},{4,8},{8,4},{12,0},{1,13},{5,9},{9,5},{13,1},{2,14},{6,10},... | collective-permute-start | bytes 786440 | tf_op jit(solution)/shard_map/ppermute | solution.py:29
  315.1 88.9 %reduce-scatter.9.cloned.1.call-start = ((), (), s32[]{:S(2)}) async-start(), calls=%async_computation.6 | async-start | bytes 2949120 | tf_op jit(solution)/shard_map/reduce_scatter | solution.py:894
  343.2 33.5 %collective-permute-start.77 = (bf16[1152,256]{1,0:T(8,128)(2,1)S(1)}, bf16[1152,256]{1,0:T(8,128)(2,1)}, u32[]{:S(2)}, u32[]{:S(2)}) collective-permute-start(bf16[1152,256]{1,0:T(8,128)(2,1)S(1)} %bitcast.98), channel_id=1, source_target_pairs={{0,4},{4,0},{8,12},{12,8},{1,5},{5,1},{9,13},{13,9},{2,6},{6,2},{1... | collective-permute-start | bytes 1769480 | tf_op jit(solution)/shard_map/ppermute | solution.py:29
  344.9 31.8 %collective-permute-start.78 = (bf16[1152,256]{1,0:T(8,128)(2,1)S(1)}, bf16[1152,256]{1,0:T(8,128)(2,1)}, u32[]{:S(2)}, u32[]{:S(2)}) collective-permute-start(bf16[1152,256]{1,0:T(8,128)(2,1)S(1)} %bitcast.99), channel_id=1, source_target_pairs={{0,8},{4,12},{8,0},{12,4},{1,9},{5,13},{9,1},{13,5},{2,10},{6,14},... | collective-permute-start | bytes 1769480 | tf_op jit(solution)/shard_map/ppermute | solution.py:29
  357.1 92.4 %reduce-scatter.11.cloned.1.call-start = ((), (), s32[]{:S(2)}) async-start(), calls=%async_computation.7 | async-start | bytes 2007040 | tf_op jit(solution)/shard_map/reduce_scatter | solution.py:894
  358.1 18.6 %collective-permute-start.79 = (bf16[784,256]{1,0:T(8,128)(2,1)S(1)}, bf16[784,256]{1,0:T(8,128)(2,1)S(1)}, u32[]{:S(2)}, u32[]{:S(2)}) collective-permute-start(bf16[784,256]{1,0:T(8,128)(2,1)S(1)} %bitcast.102), channel_id=1, source_target_pairs={{0,4},{4,0},{8,12},{12,8},{1,5},{5,1},{9,13},{13,9},{2,6},{6,2},{1... | collective-permute-start | bytes 1204232 | tf_op jit(solution)/shard_map/ppermute | solution.py:29
  358.5 18.3 %collective-permute-start.80 = (bf16[784,256]{1,0:T(8,128)(2,1)S(1)}, bf16[784,256]{1,0:T(8,128)(2,1)S(1)}, u32[]{:S(2)}, u32[]{:S(2)}) collective-permute-start(bf16[784,256]{1,0:T(8,128)(2,1)S(1)} %bitcast.103), channel_id=1, source_target_pairs={{0,8},{4,12},{8,0},{12,4},{1,9},{5,13},{9,1},{13,5},{2,10},{6,14},... | collective-permute-start | bytes 1204232 | tf_op jit(solution)/shard_map/ppermute | solution.py:29
  408.3 21.5 %collective-permute-start.91 = (bf16[1152,256]{1,0:T(8,128)(2,1)}, bf16[1152,256]{1,0:T(8,128)(2,1)S(1)}, u32[]{:S(2)}, u32[]{:S(2)}) collective-permute-start(bf16[1152,256]{1,0:T(8,128)(2,1)} %bitcast.129), channel_id=1, source_target_pairs={{0,4},{4,0},{8,12},{12,8},{1,5},{5,1},{9,13},{13,9},{2,6},{6,2},{1... | collective-permute-start | bytes 1769480 | tf_op jit(solution)/shard_map/ppermute | solution.py:29
  409.5 20.3 %collective-permute-start.92 = (bf16[1152,256]{1,0:T(8,128)(2,1)}, bf16[1152,256]{1,0:T(8,128)(2,1)S(1)}, u32[]{:S(2)}, u32[]{:S(2)}) collective-permute-start(bf16[1152,256]{1,0:T(8,128)(2,1)} %bitcast.130), channel_id=1, source_target_pairs={{0,8},{4,12},{8,0},{12,4},{1,9},{5,13},{9,1},{13,5},{2,10},{6,14},... | collective-permute-start | bytes 1769480 | tf_op jit(solution)/shard_map/ppermute | solution.py:29
  410.3 31.7 %collective-permute-start.93 = (bf16[1152,256]{1,0:T(8,128)(2,1)}, bf16[1152,256]{1,0:T(8,128)(2,1)S(1)}, u32[]{:S(2)}, u32[]{:S(2)}) collective-permute-start(bf16[1152,256]{1,0:T(8,128)(2,1)} %bitcast.131), channel_id=1, source_target_pairs={{0,12},{4,8},{8,4},{12,0},{1,13},{5,9},{9,5},{13,1},{2,14},{6,10},... | collective-permute-start | bytes 1769480 | tf_op jit(solution)/shard_map/ppermute | solution.py:29
  420.4 39.5 %collective-permute-start.96 = (bf16[4,1152,256]{2,1,0:T(8,128)(2,1)}, bf16[4,1152,256]{2,1,0:T(8,128)(2,1)}, u32[]{:S(2)}, u32[]{:S(2)}) collective-permute-start(bf16[4,1152,256]{2,1,0:T(8,128)(2,1)} %pad_maximum_fusion.1.refs_2_), channel_id=1, source_target_pairs={{0,16},{1,17},{2,18},{3,19},{4,20},{5,21},{6,22},{7,23},{8,24},{9,... | collective-permute-start | bytes 7077896 | tf_op jit(solution)/shard_map/ppermute | solution.py:910
  443.8 22.5 %collective-permute-start.94 = (bf16[4,1152,256]{2,1,0:T(8,128)(2,1)}, bf16[4,1152,256]{2,1,0:T(8,128)(2,1)}, u32[]{:S(2)}, u32[]{:S(2)}) collective-permute-start(bf16[4,1152,256]{2,1,0:T(8,128)(2,1)} %pad_maximum_fusion.refs_0_), channel_id=1, source_target_pairs={{16,0},{17,1},{18,2},{19,3},{20,4},{21,5},{22,6},{23,7},{24,8},{25... | collective-permute-start | bytes 7077896 | tf_op jit(solution)/shard_map/ppermute | solution.py:910
  449.5 24.8 %collective-permute-start.97 = (bf16[784,256]{1,0:T(8,128)(2,1)}, bf16[784,256]{1,0:T(8,128)(2,1)S(1)}, u32[]{:S(2)}, u32[]{:S(2)}) collective-permute-start(bf16[784,256]{1,0:T(8,128)(2,1)} %bitcast.137), channel_id=1, source_target_pairs={{0,4},{4,0},{8,12},{12,8},{1,5},{5,1},{9,13},{13,9},{2,6},{6,2},{1... | collective-permute-start | bytes 1204232 | tf_op jit(solution)/shard_map/ppermute | solution.py:29
  450.9 23.4 %collective-permute-start.98 = (bf16[784,256]{1,0:T(8,128)(2,1)}, bf16[784,256]{1,0:T(8,128)(2,1)S(1)}, u32[]{:S(2)}, u32[]{:S(2)}) collective-permute-start(bf16[784,256]{1,0:T(8,128)(2,1)} %bitcast.138), channel_id=1, source_target_pairs={{0,8},{4,12},{8,0},{12,4},{1,9},{5,13},{9,1},{13,5},{2,10},{6,14},... | collective-permute-start | bytes 1204232 | tf_op jit(solution)/shard_map/ppermute | solution.py:29
  457.0 17.3 %collective-permute-start.99 = (bf16[784,256]{1,0:T(8,128)(2,1)}, bf16[784,256]{1,0:T(8,128)(2,1)S(1)}, u32[]{:S(2)}, u32[]{:S(2)}) collective-permute-start(bf16[784,256]{1,0:T(8,128)(2,1)} %bitcast.139), channel_id=1, source_target_pairs={{0,12},{4,8},{8,4},{12,0},{1,13},{5,9},{9,5},{13,1},{2,14},{6,10},... | collective-permute-start | bytes 1204232 | tf_op jit(solution)/shard_map/ppermute | solution.py:29
  (204 other events, 1634.2 us)
Sparse Core Ops, SparseCore 0:
  24.8 29.9 all-gather.8
  61.6 50.8 all-gather.10
  114.6 36.4 all-gather.12
  155.0 49.9 all-gather.14
  249.5 46.2 reduce-scatter.4
  315.2 33.6 reduce-scatter.6
  357.2 45.6 reduce-scatter.8
  408.4 34.1 reduce-scatter.10

commit v7 on v6

--- a/solution.py
+++ b/solution.py
@@ -755,7 +755,7 @@
         if gain is not None:
             operands += [gain, chosen]
             outputs += [(wide, low)]
-        return call(kernel, [*operands, *weights], outputs, 6, after=after)
+        return call(kernel, [*operands, *weights], outputs, 0.6, after=after)
 
     def mlp_forward(pieces, weights, form, down):
         kernel = functools.partial(mlp_forward_kernel, count, part, form)

time: 504 us -> 504 us (level)
  no operation moved by 1% of the time
where the time goes in v7:
time: 504 us; the launch traced here: 496 us
  waiting for transfers between devices  185 us (37%)
  Pallas kernels  128 us (25%)
  starting transfers between devices  112 us (22%)
  local copies, waits for them, and re-layouts  37.2 us (7%)
  other arithmetic  17.6 us (3%)
  between operations  16.1 us (3%)
    ppermute x72, waiting for transfers between devices, hop(): return lax.ppermute(value, 'ctx', [(i, i ^ step) for i in range(count)])  151 us
    pallas_call x33, Pallas kernels, call(): pl.pallas_call(body, out_shape=shapes, in_specs=[anywhere] * skipped + [s...  106 us
    ppermute x72, starting transfers between devices, hop(): return lax.ppermute(value, 'ctx', [(i, i ^ step) for i in range(count)])  87.1 us
    unnamed x242, local copies, waits for them, and re-layouts  29.6 us
    all_gather x4, waiting for transfers between devices, gathered(): return lax.all_gather(block, 'fsdp', axis=0, tiled=False)  18.4 us
    pallas_call x2, Pallas kernels, settle(): pl.pallas_call(body, grid_spec=pltpu.PrefetchScalarGridSpec(num_scalar_pr...  14 us
    ppermute x4, starting transfers between devices, returned(): return (own, lax.ppermute(own, 'section', [(1 - layer, layer)]))  11.8 us
    ppermute x24, waiting for transfers between devices, swap(): return lax.ppermute(value, 'section', [(0, 1), (1, 0)])  11.6 us
  transfers between devices with their start and end apart: 111, of which 49 were waited for; matrix products, arithmetic and copies ran while one was open for 4% of the time, Pallas kernels for 23%

profile of v7, /device:TPU:0, one launch (start us, length us, event | category | flops | bytes accessed | tf_op | source)
XLA Modules:
  0.0 495.5 jit_solution(12747912529001499215)
XLA Ops:
  53.8 6.2 %collective-permute-done.3.refs_2_ = bf16[128,1024]{1,0:T(8,128)(2,1)S(1)} collective-permute-done((bf16[128,1024]{1,0:T(8,128)(2,1)S(1)}, bf16[128,1024]{1,0:T(8,128)(2,1)S(1)}, u32[]{:S(2)}, u32[]{:S(2)}) %collective-permute-start.3) | collective-permute-done | bytes 262176 | tf_op jit(solution)/shard_map/ppermute | solution.py:29
  70.5 7.0 %shard_map.232 = (bf16[512,1024]{1,0:T(8,128)(2,1)S(1)}, f32[512,1024]{1,0:T(8,128)S(1)}, bf16[512,512]{1,0:T(8,128)(2,1)S(1)}, bf16[512,256]{1,0:T(8,128)(2,1)S...) custom-call(bf16[128,1024]{1,0:T(8,128)(2,1)S(1)} %get-tuple-element.259.refs_0_.refs_4_, ...), custom_call_target="tpu_custom_call" | custom-call | flops 6899999744 | bytes 8997888 | tf_op jit(solution)/shard_map/pallas_call | solution.py:129
  86.7 5.6 %collective-permute-done.20.refs_1_ = bf16[128,1024]{1,0:T(8,128)(2,1)S(1)} collective-permute-done((bf16[128,1024]{1,0:T(8,128)(2,1)S(1)}, bf16[128,1024]{1,0:T(8,128)(2,1)S(1)}, u32[]{:S(2)}, u32[]{:S(2)}) %collective-permute-start.20) | collective-permute-done | bytes 262176 | tf_op jit(solution)/shard_map/ppermute | solution.py:29
  92.3 5.9 %collective-permute-done.22.refs_3_ = bf16[128,1024]{1,0:T(8,128)(2,1)S(1)} collective-permute-done((bf16[128,1024]{1,0:T(8,128)(2,1)S(1)}, bf16[128,1024]{1,0:T(8,128)(2,1)S(1)}, u32[]{:S(2)}, u32[]{:S(2)}) %collective-permute-start.22) | collective-permute-done | bytes 262176 | tf_op jit(solution)/shard_map/ppermute | solution.py:29
  102.1 5.7 %collective-permute-done.23.refs_2_ = bf16[128,1024]{1,0:T(8,128)(2,1)S(1)} collective-permute-done((bf16[128,1024]{1,0:T(8,128)(2,1)S(1)}, bf16[128,1024]{1,0:T(8,128)(2,1)S(1)}, u32[]{:S(2)}, u32[]{:S(2)}) %collective-permute-start.23) | collective-permute-done | bytes 262176 | tf_op jit(solution)/shard_map/ppermute | solution.py:29
  119.0 5.3 %shard_map.235 = (bf16[512,1024]{1,0:T(8,128)(2,1)S(1)}, f32[512,768]{1,0:T(8,128)S(1)}, f32[512,768]{1,0:T(8,128)S(1)}, bf16[512,768]{1,0:T(8,128)(2,1)S(1)}, b...) custom-call(s32[2]{0:T(128)S(1)} %copy-done.5, ...), custom_call_target="tpu_custom_call" | custom-call | flops 9200000000 | bytes 13369344 | tf_op jit(solution)/shard_map/pallas_call | solution.py:129
  128.0 5.7 %collective-permute-done.27.refs_1_ = bf16[128,1024]{1,0:T(8,128)(2,1)S(1)} collective-permute-done((bf16[128,1024]{1,0:T(8,128)(2,1)S(1)}, bf16[128,1024]{1,0:T(8,128)(2,1)S(1)}, u32[]{:S(2)}, u32[]{:S(2)}) %collective-permute-start.27) | collective-permute-done | bytes 262176 | tf_op jit(solution)/shard_map/ppermute | solution.py:29
  133.6 6.0 %collective-permute-done.28.refs_2_ = bf16[128,1024]{1,0:T(8,128)(2,1)S(1)} collective-permute-done((bf16[128,1024]{1,0:T(8,128)(2,1)S(1)}, bf16[128,1024]{1,0:T(8,128)(2,1)S(1)}, u32[]{:S(2)}, u32[]{:S(2)}) %collective-permute-start.28) | collective-permute-done | bytes 262176 | tf_op jit(solution)/shard_map/ppermute | solution.py:29
  144.2 6.9 %all-gather.13.cloned.1.call-done = bf16[3136,256]{1,0:T(8,128)(2,1)} async-done(((bf16[784,256]{1,0:T(8,128)(2,1)}), bf16[3136,256]{1,0:T(8,128)(2,1)}) %all-gather.13.cloned.1.call-update) | async-done | bytes 1605648 | tf_op jit(solution)/shard_map/all_gather | solution.py:673
  160.7 8.3 %shard_map.237 = (bf16[512,1024]{1,0:T(8,128)(2,1)S(1)}, f32[512,1024]{1,0:T(8,128)S(1)}, bf16[512,512]{1,0:T(8,128)(2,1)S(1)}, bf16[512,256]{1,0:T(8,128)(2,1)S...) custom-call(bf16[128,1024]{1,0:T(8,128)(2,1)S(1)} %get-tuple-element.288.refs_0_, ...), custom_call_target="tpu_custom_call" | custom-call | flops 6899999744 | bytes 9255936 | tf_op jit(solution)/shard_map/pallas_call | solution.py:129
  178.3 5.6 %collective-permute-done.41.refs_1_ = bf16[128,1024]{1,0:T(8,128)(2,1)S(1)} collective-permute-done((bf16[128,1024]{1,0:T(8,128)(2,1)S(1)}, bf16[128,1024]{1,0:T(8,128)(2,1)S(1)}, u32[]{:S(2)}, u32[]{:S(2)}) %collective-permute-start.41) | collective-permute-done | bytes 262176 | tf_op jit(solution)/shard_map/ppermute | solution.py:29
  193.7 11.3 %all-gather.15.cloned.1.call-done = bf16[4608,256]{1,0:T(8,128)(2,1)} async-done(((bf16[1152,256]{1,0:T(8,128)(2,1)}), bf16[4608,256]{1,0:T(8,128)(2,1)}) %all-gather.15.cloned.1.call-update) | async-done | bytes 2359312 | tf_op jit(solution)/shard_map/all_gather | solution.py:673
  253.2 24.2 %shard_map.248 = (bf16[128,1024]{1,0:T(8,128)(2,1)S(1)}, bf16[128,1024]{1,0:T(8,128)(2,1)S(1)}, bf16[128,1024]{1,0:T(8,128)(2,1)S(1)}, bf16[128,1024]{1,0:T(8,12...) custom-call(f32[8,128]{1,0:T(8,128)S(1)} %shard_map.247.refs_0_, ...), custom_call_target="tpu_custom_call" | custom-call | flops 20700000256 | bytes 11878400 | tf_op jit(solution)/shard_map/pallas_call | solution.py:129
  303.3 5.6 %collective-permute-done.68.refs_4_ = bf16[128,1024]{1,0:T(8,128)(2,1)S(1)} collective-permute-done((bf16[128,1024]{1,0:T(8,128)(2,1)S(1)}, bf16[128,1024]{1,0:T(8,128)(2,1)S(1)}, u32[]{:S(2)}, u32[]{:S(2)}) %collective-permute-start.68) | collective-permute-done | bytes 262176 | tf_op jit(solution)/shard_map/ppermute | solution.py:29
  319.4 6.1 %shard_map.254 = (bf16[128,1024]{1,0:T(8,128)(2,1)S(1)}, bf16[128,1024]{1,0:T(8,128)(2,1)S(1)}, bf16[128,1024]{1,0:T(8,128)(2,1)S(1)}, bf16[128,1024]{1,0:T(8,12...) custom-call(f32[8,128]{1,0:T(8,128)S(1)} %shard_map.253.refs_0_, ...), custom_call_target="tpu_custom_call" | custom-call | flops 3449999872 | bytes 15728640 | tf_op jit(solution)/shard_map/pallas_call | solution.py:129
  349.7 6.7 %collective-permute-done.75.refs_3_ = bf16[128,1024]{1,0:T(8,128)(2,1)S(1)} collective-permute-done((bf16[128,1024]{1,0:T(8,128)(2,1)}, bf16[128,1024]{1,0:T(8,128)(2,1)S(1)}, u32[]{:S(2)}, u32[]{:S(2)}) %collective-permute-start.75) | collective-permute-done | bytes 262176 | tf_op jit(solution)/shard_map/ppermute | solution.py:29
  361.1 15.5 %shard_map.259 = (bf16[128,1024]{1,0:T(8,128)(2,1)S(1)}, bf16[128,1024]{1,0:T(8,128)(2,1)S(1)}, bf16[128,1024]{1,0:T(8,128)(2,1)S(1)}, bf16[128,1024]{1,0:T(8,12...) custom-call(f32[8,128]{1,0:T(8,128)S(1)} %shard_map.258.refs_0_, ...), custom_call_target="tpu_custom_call" | custom-call | flops 20700000256 | bytes 11616256 | tf_op jit(solution)/shard_map/pallas_call | solution.py:129
  383.3 5.7 %collective-permute-done.81.refs_1_ = bf16[128,1024]{1,0:T(8,128)(2,1)S(1)} collective-permute-done((bf16[128,1024]{1,0:T(8,128)(2,1)S(1)}, bf16[128,1024]{1,0:T(8,128)(2,1)S(1)}, u32[]{:S(2)}, u32[]{:S(2)}) %collective-permute-start.81) | collective-permute-done | bytes 262176 | tf_op jit(solution)/shard_map/ppermute | solution.py:29
  411.8 5.4 %collective-permute-done.95 = bf16[1152,256]{1,0:T(8,128)(2,1)} collective-permute-done((bf16[1152,256]{1,0:T(8,128)(2,1)S(1)}, bf16[1152,256]{1,0:T(8,128)(2,1)}, u32[]{:S(2)}, u32[]{:S(2)}) %collective-permute-start.95) | collective-permute-done | bytes 589856 | tf_op jit(solution)/shard_map/ppermute | solution.py:29
  423.2 6.6 %collective-permute-done.91 = bf16[1152,256]{1,0:T(8,128)(2,1)S(1)} collective-permute-done((bf16[1152,256]{1,0:T(8,128)(2,1)}, bf16[1152,256]{1,0:T(8,128)(2,1)S(1)}, u32[]{:S(2)}, u32[]{:S(2)}) %collective-permute-start.91) | collective-permute-done | bytes 589856 | tf_op jit(solution)/shard_map/ppermute | solution.py:29
  429.8 12.2 %collective-permute-done.93 = bf16[1152,256]{1,0:T(8,128)(2,1)S(1)} collective-permute-done((bf16[1152,256]{1,0:T(8,128)(2,1)}, bf16[1152,256]{1,0:T(8,128)(2,1)S(1)}, u32[]{:S(2)}, u32[]{:S(2)}) %collective-permute-start.93) | collective-permute-done | bytes 589856 | tf_op jit(solution)/shard_map/ppermute | solution.py:29
  459.9 6.3 %collective-permute-start.102 = (bf16[4,784,256]{2,1,0:T(8,128)(2,1)}, bf16[4,784,256]{2,1,0:T(8,128)(2,1)}, u32[]{:S(2)}, u32[]{:S(2)}) collective-permute-start(bf16[4,784,256]{2,1,0:T(8,128)(2,1)} %pad_maximum_fusion.3.refs_2_), channel_id=1, source_target_pairs={{0,16},{1,17},{2,18},{3,19},{4,20},{5,21},{6,22},{7,23},{8,24},{9,... | collective-permute-start | bytes 4816904 | tf_op jit(solution)/shard_map/ppermute | solution.py:910
  466.2 8.0 %shard_map.264 = (f32[256,3072]{1,0:T(8,128)}, f32[256,3072]{1,0:T(8,128)}, f32[8,96,1024]{2,1,0:T(8,128)}) custom-call(s32[2]{0:T(128)} %pad_add_fusion.1.where.refs_0_.refs_1_, bf16[4,1152,256]{2,1,0:T(8,128)(2,1)} %pad_maximum_fusion.refs_0_, bf16[4,1152,256]{2,1,0:T(8,128)(2,1)} %collective-permute-done.94.refs_1_, ...), custom_call_target="tpu_custom_call" | custom-call | bytes 14155776 | tf_op jit(solution)/shard_map/pallas_call | solution.py:1014
  480.3 6.0 %shard_map.265 = (f32[256,2048]{1,0:T(8,128)}, f32[256,1024]{1,0:T(8,128)}, f32[256,1024]{1,0:T(8,128)}, f32[2,256,1024]{2,1,0:T(8,128)}, f32[16,256]{1,0:T(8,128)}) custom-call(s32[2]{0:T(128)} %pad_add_fusion.1.where.refs_0_.refs_1_, bf16[4,784,256]{2,1,0:T(8,128)(2,1)} %copy-done.95, bf16[4,784,256]{2,1,0:T(8,128)(2,1)} %collective-permute-done.100.refs_1_, ...), custom_call_target="tpu_custom_call" | custom-call | bytes 9633792 | tf_op jit(solution)/shard_map/pallas_call | solution.py:1014
  (530 shorter events, 291.8 us)
Async XLA Ops:
  7.2 54.3 %all-gather.9.cloned.1.call-start = ((), (), s32[]{:S(2)}) async-start(), calls=%async_computation.8 | async-start | bytes 1351680 | tf_op jit(solution)/shard_map/all_gather | solution.py:673
  24.6 87.8 %all-gather.11.cloned.1.call-start = ((), (), s32[]{:S(2)}) async-start(), calls=%async_computation.9 | async-start | bytes 2949120 | tf_op jit(solution)/shard_map/all_gather | solution.py:673
  41.9 18.1 %collective-permute-start.3 = (bf16[128,1024]{1,0:T(8,128)(2,1)S(1)}, bf16[128,1024]{1,0:T(8,128)(2,1)S(1)}, u32[]{:S(2)}, u32[]{:S(2)}) collective-permute-start(bf16[128,1024]{1,0:T(8,128)(2,1)S(1)} %get-tuple-element.259.refs_0_.refs_4_), channel_id=1, source_target_pairs={{0,8},{4,12},{8,0},{12,4},{1,9},{5,13},{9,1},{13,5},{2,10},{6,14},... | collective-permute-start | bytes 786440 | tf_op jit(solution)/shard_map/ppermute | solution.py:29
  61.5 89.6 %all-gather.13.cloned.1.call-start = ((), (), s32[]{:S(2)}) async-start(), calls=%async_computation.10 | async-start | bytes 2007040 | tf_op jit(solution)/shard_map/all_gather | solution.py:673
  112.5 92.5 %all-gather.15.cloned.1.call-start = ((), (), s32[]{:S(2)}) async-start(), calls=%async_computation.11 | async-start | bytes 2949120 | tf_op jit(solution)/shard_map/all_gather | solution.py:673
  154.9 160.2 %reduce-scatter.5.cloned.1.call-start = ((), (), s32[]{:S(2)}) async-start(), calls=%async_computation.4 | async-start | bytes 2949120 | tf_op jit(solution)/shard_map/reduce_scatter | solution.py:894
  249.4 107.6 %reduce-scatter.7.cloned.1.call-start = ((), (), s32[]{:S(2)}) async-start(), calls=%async_computation.5 | async-start | bytes 2007040 | tf_op jit(solution)/shard_map/reduce_scatter | solution.py:894
  249.5 27.8 %collective-permute-start.55 = (bf16[128,1024]{1,0:T(8,128)(2,1)S(1)}, bf16[128,1024]{1,0:T(8,128)(2,1)S(1)}, u32[]{:S(2)}, u32[]{:S(2)}) collective-permute-start(bf16[128,1024]{1,0:T(8,128)(2,1)S(1)} %get-tuple-element.361), channel_id=1, source_target_pairs={{0,4},{4,0},{8,12},{12,8},{1,5},{5,1},{9,13},{13,9},{2,6},{6,2},{1... | collective-permute-start | bytes 786440 | tf_op jit(solution)/shard_map/ppermute | solution.py:29
  250.4 26.9 %collective-permute-start.56 = (bf16[128,1024]{1,0:T(8,128)(2,1)S(1)}, bf16[128,1024]{1,0:T(8,128)(2,1)S(1)}, u32[]{:S(2)}, u32[]{:S(2)}) collective-permute-start(bf16[128,1024]{1,0:T(8,128)(2,1)S(1)} %get-tuple-element.362), channel_id=1, source_target_pairs={{0,8},{4,12},{8,0},{12,4},{1,9},{5,13},{9,1},{13,5},{2,10},{6,14},... | collective-permute-start | bytes 786440 | tf_op jit(solution)/shard_map/ppermute | solution.py:29
  251.9 25.5 %collective-permute-start.57 = (bf16[128,1024]{1,0:T(8,128)(2,1)S(1)}, bf16[128,1024]{1,0:T(8,128)(2,1)S(1)}, u32[]{:S(2)}, u32[]{:S(2)}) collective-permute-start(bf16[128,1024]{1,0:T(8,128)(2,1)S(1)} %get-tuple-element.363), channel_id=1, source_target_pairs={{0,12},{4,8},{8,4},{12,0},{1,13},{5,9},{9,5},{13,1},{2,14},{6,10},... | collective-permute-start | bytes 786440 | tf_op jit(solution)/shard_map/ppermute | solution.py:29
  315.1 88.9 %reduce-scatter.9.cloned.1.call-start = ((), (), s32[]{:S(2)}) async-start(), calls=%async_computation.6 | async-start | bytes 2949120 | tf_op jit(solution)/shard_map/reduce_scatter | solution.py:894
  343.2 33.5 %collective-permute-start.77 = (bf16[1152,256]{1,0:T(8,128)(2,1)S(1)}, bf16[1152,256]{1,0:T(8,128)(2,1)}, u32[]{:S(2)}, u32[]{:S(2)}) collective-permute-start(bf16[1152,256]{1,0:T(8,128)(2,1)S(1)} %bitcast.101), channel_id=1, source_target_pairs={{0,4},{4,0},{8,12},{12,8},{1,5},{5,1},{9,13},{13,9},{2,6},{6,2},{1... | collective-permute-start | bytes 1769480 | tf_op jit(solution)/shard_map/ppermute | solution.py:29
  344.9 31.8 %collective-permute-start.78 = (bf16[1152,256]{1,0:T(8,128)(2,1)S(1)}, bf16[1152,256]{1,0:T(8,128)(2,1)}, u32[]{:S(2)}, u32[]{:S(2)}) collective-permute-start(bf16[1152,256]{1,0:T(8,128)(2,1)S(1)} %bitcast.102), channel_id=1, source_target_pairs={{0,8},{4,12},{8,0},{12,4},{1,9},{5,13},{9,1},{13,5},{2,10},{6,14},... | collective-permute-start | bytes 1769480 | tf_op jit(solution)/shard_map/ppermute | solution.py:29
  357.1 92.4 %reduce-scatter.11.cloned.1.call-start = ((), (), s32[]{:S(2)}) async-start(), calls=%async_computation.7 | async-start | bytes 2007040 | tf_op jit(solution)/shard_map/reduce_scatter | solution.py:894
  358.1 18.6 %collective-permute-start.79 = (bf16[784,256]{1,0:T(8,128)(2,1)S(1)}, bf16[784,256]{1,0:T(8,128)(2,1)S(1)}, u32[]{:S(2)}, u32[]{:S(2)}) collective-permute-start(bf16[784,256]{1,0:T(8,128)(2,1)S(1)} %bitcast.105), channel_id=1, source_target_pairs={{0,4},{4,0},{8,12},{12,8},{1,5},{5,1},{9,13},{13,9},{2,6},{6,2},{1... | collective-permute-start | bytes 1204232 | tf_op jit(solution)/shard_map/ppermute | solution.py:29
  358.5 18.3 %collective-permute-start.80 = (bf16[784,256]{1,0:T(8,128)(2,1)S(1)}, bf16[784,256]{1,0:T(8,128)(2,1)S(1)}, u32[]{:S(2)}, u32[]{:S(2)}) collective-permute-start(bf16[784,256]{1,0:T(8,128)(2,1)S(1)} %bitcast.106), channel_id=1, source_target_pairs={{0,8},{4,12},{8,0},{12,4},{1,9},{5,13},{9,1},{13,5},{2,10},{6,14},... | collective-permute-start | bytes 1204232 | tf_op jit(solution)/shard_map/ppermute | solution.py:29
  408.3 21.5 %collective-permute-start.91 = (bf16[1152,256]{1,0:T(8,128)(2,1)}, bf16[1152,256]{1,0:T(8,128)(2,1)S(1)}, u32[]{:S(2)}, u32[]{:S(2)}) collective-permute-start(bf16[1152,256]{1,0:T(8,128)(2,1)} %bitcast.129), channel_id=1, source_target_pairs={{0,4},{4,0},{8,12},{12,8},{1,5},{5,1},{9,13},{13,9},{2,6},{6,2},{1... | collective-permute-start | bytes 1769480 | tf_op jit(solution)/shard_map/ppermute | solution.py:29
  409.5 20.3 %collective-permute-start.92 = (bf16[1152,256]{1,0:T(8,128)(2,1)}, bf16[1152,256]{1,0:T(8,128)(2,1)S(1)}, u32[]{:S(2)}, u32[]{:S(2)}) collective-permute-start(bf16[1152,256]{1,0:T(8,128)(2,1)} %bitcast.130), channel_id=1, source_target_pairs={{0,8},{4,12},{8,0},{12,4},{1,9},{5,13},{9,1},{13,5},{2,10},{6,14},... | collective-permute-start | bytes 1769480 | tf_op jit(solution)/shard_map/ppermute | solution.py:29
  410.3 31.7 %collective-permute-start.93 = (bf16[1152,256]{1,0:T(8,128)(2,1)}, bf16[1152,256]{1,0:T(8,128)(2,1)S(1)}, u32[]{:S(2)}, u32[]{:S(2)}) collective-permute-start(bf16[1152,256]{1,0:T(8,128)(2,1)} %bitcast.131), channel_id=1, source_target_pairs={{0,12},{4,8},{8,4},{12,0},{1,13},{5,9},{9,5},{13,1},{2,14},{6,10},... | collective-permute-start | bytes 1769480 | tf_op jit(solution)/shard_map/ppermute | solution.py:29
  420.4 39.5 %collective-permute-start.96 = (bf16[4,1152,256]{2,1,0:T(8,128)(2,1)}, bf16[4,1152,256]{2,1,0:T(8,128)(2,1)}, u32[]{:S(2)}, u32[]{:S(2)}) collective-permute-start(bf16[4,1152,256]{2,1,0:T(8,128)(2,1)} %pad_maximum_fusion.1.refs_2_), channel_id=1, source_target_pairs={{0,16},{1,17},{2,18},{3,19},{4,20},{5,21},{6,22},{7,23},{8,24},{9,... | collective-permute-start | bytes 7077896 | tf_op jit(solution)/shard_map/ppermute | solution.py:910
  443.8 22.5 %collective-permute-start.94 = (bf16[4,1152,256]{2,1,0:T(8,128)(2,1)}, bf16[4,1152,256]{2,1,0:T(8,128)(2,1)}, u32[]{:S(2)}, u32[]{:S(2)}) collective-permute-start(bf16[4,1152,256]{2,1,0:T(8,128)(2,1)} %pad_maximum_fusion.refs_0_), channel_id=1, source_target_pairs={{16,0},{17,1},{18,2},{19,3},{20,4},{21,5},{22,6},{23,7},{24,8},{25... | collective-permute-start | bytes 7077896 | tf_op jit(solution)/shard_map/ppermute | solution.py:910
  449.5 24.8 %collective-permute-start.97 = (bf16[784,256]{1,0:T(8,128)(2,1)}, bf16[784,256]{1,0:T(8,128)(2,1)S(1)}, u32[]{:S(2)}, u32[]{:S(2)}) collective-permute-start(bf16[784,256]{1,0:T(8,128)(2,1)} %bitcast.137), channel_id=1, source_target_pairs={{0,4},{4,0},{8,12},{12,8},{1,5},{5,1},{9,13},{13,9},{2,6},{6,2},{1... | collective-permute-start | bytes 1204232 | tf_op jit(solution)/shard_map/ppermute | solution.py:29
  450.9 23.4 %collective-permute-start.98 = (bf16[784,256]{1,0:T(8,128)(2,1)}, bf16[784,256]{1,0:T(8,128)(2,1)S(1)}, u32[]{:S(2)}, u32[]{:S(2)}) collective-permute-start(bf16[784,256]{1,0:T(8,128)(2,1)} %bitcast.138), channel_id=1, source_target_pairs={{0,8},{4,12},{8,0},{12,4},{1,9},{5,13},{9,1},{13,5},{2,10},{6,14},... | collective-permute-start | bytes 1204232 | tf_op jit(solution)/shard_map/ppermute | solution.py:29
  457.0 17.3 %collective-permute-start.99 = (bf16[784,256]{1,0:T(8,128)(2,1)}, bf16[784,256]{1,0:T(8,128)(2,1)S(1)}, u32[]{:S(2)}, u32[]{:S(2)}) collective-permute-start(bf16[784,256]{1,0:T(8,128)(2,1)} %bitcast.139), channel_id=1, source_target_pairs={{0,12},{4,8},{8,4},{12,0},{1,13},{5,9},{9,5},{13,1},{2,14},{6,10},... | collective-permute-start | bytes 1204232 | tf_op jit(solution)/shard_map/ppermute | solution.py:29
  (204 other events, 1634.2 us)
Sparse Core Ops, SparseCore 0:
  24.8 29.9 all-gather.8
  61.6 50.8 all-gather.10
  114.6 36.4 all-gather.12
  155.0 49.9 all-gather.14
  249.5 46.2 reduce-scatter.4
  315.2 33.6 reduce-scatter.6
  357.2 45.7 reduce-scatter.8
  408.4 34.1 reduce-scatter.10
